TPU v7x, 32 devices: a whole 2x2x4 slice. The times are simulated.
32 devices in a mesh: dp: 8 (over z, y), pipe: 4 (over x, core).
Axes of the slice: x: 2, y: 2, z: 4, core: 2. Of those that a mesh axis runs over, the one named last changes fastest.
Arguments:
- numeric: float32 [8192, 128], P('dp'), may hold values from -6 to 6
- categories: int32 [8192, 24], P('dp'), may hold values from 0 to 255, as said below
- cardinalities: int32 [24], replicated, may hold values from 64 to 256, as said below
- embed_table: bfloat16 [24, 256, 16], replicated, may hold values from -6 to 6
- bn_gain: float32 [2, 512], replicated, may hold values from 0.25 to 1.75
- bn_bias: float32 [2, 512], replicated, may hold values from -3 to 3
- mask_logits: float32 [12, 512], P('pipe'), may hold values from -5 to 5
- feature_allow: int32 [12, 512], P('pipe'), may hold values from 0 to 1, as said below
- gate_weight: bfloat16 [12, 1024, 1024], P('pipe'), may hold values from -0.1875 to 0.1875
- gate_bias: float32 [12, 1024], P('pipe'), may hold values from -3 to 3
- cand_weight: bfloat16 [12, 1024, 512], P('pipe'), may hold values from -0.1875 to 0.1875
- cand_bias: float32 [12, 512], P('pipe'), may hold values from -3 to 3
- out_grad: float32 [8192, 512], P('dp'), may hold values from -6 to 6
Outputs:
- block_out: float32 [8192, 512], P('dp', 'pipe')
- numeric_grad: float32 [8192, 128], P('dp', 'pipe')
- table_grad: float32 [24, 256, 16], replicated
- gain_grad: float32 [2, 512], replicated
- bias_grad: float32 [2, 512], replicated
- logit_grad: float32 [12, 512], P('pipe')
- gate_weight_grad: float32 [12, 1024, 1024], P('pipe')
- gate_bias_grad: float32 [12, 1024], P('pipe')
- cand_weight_grad: float32 [12, 1024, 512], P('pipe')
- cand_bias_grad: float32 [12, 512], P('pipe')
Inputs may be any that keep to these rules, and one draw needn't show every extreme that they name: categories[r, c] is below cardinalities[c]. `cardinalities`: some column has exactly 256 categories. `feature_allow`: every segment allows at least one feature.
All inputs are finite; a program needn't handle non-finite values.
Results may differ from a plain program's by a relative error of at most 0.0128.
The roundings to bfloat16 on the way count: a program that leaves them out, or rounds other values in their place, can miss the bound.
Values may be sent and summed in bfloat16 or wider, within the bound.
No kernel may reach another device: no remote copies, remote signals or barrier semaphores. Data moves between devices by JAX's collectives and lax.ppermute only.
A program may use at most 192 MiB of HBM per device.

v0:
```python
import functools

import jax
import jax.numpy as jnp
from jax import lax
from jax.experimental import pallas as pl
from jax.experimental.pallas import tpu as pltpu
from jax.sharding import PartitionSpec as P

MB = 8
ROWS_MB = 128
BLOCK = 512
EPS = 1e-05
BF = jnp.bfloat16
F32 = jnp.float32


def feature_share(logits, allow):
    allowed = allow > 0
    largest = jnp.max(jnp.where(allowed, logits, -1e30), axis=-1, keepdims=True)
    raised = jnp.where(allowed, jnp.exp(jnp.where(allowed, logits - largest, 0.0)), 0.0)
    return raised / jnp.sum(raised, axis=-1, keepdims=True)


def core_swap(value):
    return lax.ppermute(value, "pipe", [(i, i ^ 1) for i in range(lax.axis_size("pipe"))])


def to_layer(value, up):
    half = lax.axis_size("pipe") // 2
    pairs = [(i, i + half) if up else (i + half, i) for i in range(half)]
    return lax.ppermute(value, "pipe", pairs)


def dp_swap(value, step):
    return lax.ppermute(value, "dp", [(i, i ^ step) for i in range(lax.axis_size("dp"))])


def merged(a, b, held):
    gap = a[0] - b[0]
    return 0.5 * (a[0] + b[0]), a[1] + b[1] + gap * gap * (0.5 * held)


def dp_levels():
    return [1 << i for i in range(lax.axis_size("dp").bit_length() - 1)]


def dp_moments(both, count):
    held = count
    for step in dp_levels()[1:]:
        both = jnp.stack(merged(both, dp_swap(both, step), held))
        held *= 2
    return both


def last_pair(both):
    return both, dp_swap(both, dp_levels()[0])


def last_pair_to_layer(both, up):
    lanes = lax.axis_size("pipe")
    half = lanes // 2
    pairs = []
    for place in range(lax.axis_size("dp")):
        for lane in range(half):
            low, high = lane, lane + half
            start, end = (low, high) if up else (high, low)
            pairs.append((place * lanes + start, (place ^ dp_levels()[0]) * lanes + end))
    return to_layer(both, up), lax.ppermute(both, ("dp", "pipe"), pairs)


def partial_total(value):
    for step in dp_levels()[1:]:
        value = value + dp_swap(value, step)
    return value


def dp_total(value):
    step = 1
    while step < lax.axis_size("dp"):
        value = value + dp_swap(value, step)
        step *= 2
    return value


def plus(a, b):
    return lax.reduce_precision(a.astype(F32) + b.astype(F32), 8, 7).astype(BF)


def halves(value, second):
    mid = value.shape[0] // 2
    a, b = value[:mid], value[mid:]
    return jnp.where(second, b, a), jnp.where(second, a, b)


def joined(kept, got, second):
    return jnp.where(second, jnp.concatenate([got, kept]), jnp.concatenate([kept, got]))


def rounded(value):
    return lax.reduce_precision(value, 8, 7)


def dot(a, b, dims):
    return lax.dot_general(a, b, ((dims[0], dims[1]), ((), ())), preferred_element_type=F32)


def sigmoid(v):
    return 0.5 * jnp.tanh(0.5 * v) + 0.5


def low(v):
    return v.astype(BF).astype(F32)


def nn(a, b):
    return lax.dot_general(a, b, (((1,), (0,)), ((), ())), preferred_element_type=F32)


def nt(a, b):
    return lax.dot_general(a, b, (((1,), (1,)), ((), ())), preferred_element_type=F32)


def column_sum(v):
    return jnp.sum(v, axis=0, keepdims=True)


def batch_rows(i):
    return slice(i * ROWS_MB, (i + 1) * ROWS_MB)


def when_active(layer):
    rank = lax.axis_index("pipe")
    return rank // (lax.axis_size("pipe") // 2) == layer


class Weights:
    def __init__(self, refs, scratch):
        self.own_gate, self.other_gate, self.own_cand, self.other_cand = refs
        self.gate, self.cand, self.sems = scratch
        self.slots = self.gate.shape[0]

    def start(self, k):
        core = lax.axis_index("pipe") % 2
        per_core = self.own_gate.shape[0]
        i, slot = k % per_core, k % self.slots

        def begin(gate, cand):
            pltpu.make_async_copy(gate.at[i], self.gate.at[slot], self.sems.at[0, slot]).start()
            pltpu.make_async_copy(cand.at[i], self.cand.at[slot], self.sems.at[1, slot]).start()

        pl.when(core == k // per_core)(functools.partial(begin, self.own_gate, self.own_cand))
        pl.when(core != k // per_core)(functools.partial(begin, self.other_gate, self.other_cand))

    def wait(self, k):
        slot = k % self.slots
        pltpu.make_async_copy(self.own_gate.at[0], self.gate.at[slot], self.sems.at[0, slot]).wait()
        pltpu.make_async_copy(self.own_cand.at[0], self.cand.at[slot], self.sems.at[1, slot]).wait()


def finish_moments(a, b, moments, held):
    mean, spread = merged(a[...], b[...], held)
    moments[0] = mean
    moments[1] = lax.rsqrt(spread / (2 * held) + EPS)


def normalise(source, moments, affine, x):
    for i in range(source.shape[0] // ROWS_MB):
        at = batch_rows(i)
        xhat = (source[at, :].astype(F32) - moments[0, i : i + 1, :]) * moments[1, i : i + 1, :]
        x[at, :] = xhat * affine[0:1, :] + affine[1:2, :]


def run_forward(x, scales, gate_bias, cand_bias, weights, h, keep=None, after=None):
    rows, width = x.shape
    count = scales.shape[0]
    section = count // 2
    blocks = [slice(i, i + BLOCK) for i in range(0, rows, BLOCK)]

    def spot(k):
        return k if keep else k % 2

    weights.wait(0)
    for at in blocks:
        m = (x[at, :] * scales[0:1, :]).astype(BF)
        zz = sigmoid(nn(m, weights.gate[0, width:, :width]) + gate_bias[0:1, :width])
        cc = jnp.tanh(nn(m, weights.cand[0, width:, :]) + cand_bias[0:1, :])
        h[1, at, :] = zz * cc
        if keep:
            z, r, c, operands = keep
            z[0, at, :], c[0, at, :] = zz, cc
            if operands is not None:
                operands[0, at, width : 2 * width] = m
    if keep:
        after(0)

    def segment(k, _):
        weights.wait(k)
        if keep:
            after.before(k)

        @pl.when(k == section)
        def _():
            x[...] = low(x[...])
            h[spot(k)] = low(h[spot(k)])

        for at in blocks:
            hh = h[spot(k), at, :]
            hb = hh.astype(BF)
            m = (x[at, :] * scales[pl.ds(k, 1), :]).astype(BF)
            both = jnp.concatenate([hb, m], 1)
            bias = gate_bias[pl.ds(k, 1), :]
            rr = sigmoid(nn(both, weights.gate[k, :, width:]) + bias[:, width:])
            zz = sigmoid(nn(both, weights.gate[k, :, :width]) + bias[:, :width])
            rh = (rr * hh).astype(BF)
            cc = jnp.tanh(nn(jnp.concatenate([rh, m], 1), weights.cand[k]) + cand_bias[pl.ds(k, 1), :])
            if keep:
                z[k, at, :], r[k, at, :], c[k, at, :] = zz, rr, cc
                if operands is not None:
                    slot = k % 2
                    operands[slot, at, :width] = hb
                    operands[slot, at, width : 2 * width] = m
                    operands[slot, at, 2 * width :] = rh
            h[spot(k + 1), at, :] = (1.0 - zz) * hh + zz * cc
        if keep:
            after(k)
        return 0

    lax.fori_loop(1, count, segment, 0)


class Out:
    def __init__(self, slotted, sems, kept=(), kept_sems=None):
        self.slotted, self.sems, self.kept, self.kept_sems = slotted, sems, kept, kept_sems

    def slot_copy(self, k):
        source, target = self.slotted
        return pltpu.make_async_copy(source.at[k % 2], target.at[k], self.sems.at[k % 2])

    def kept_copies(self, k):
        return [
            pltpu.make_async_copy(source.at[k], target.at[k], self.kept_sems.at[i, k])
            for i, (source, target) in enumerate(self.kept)
        ]

    def before(self, k):
        if not self.slotted:
            return

        @pl.when(k >= 2)
        def _():
            self.slot_copy(k - 2).wait()

    def __call__(self, k):
        if self.slotted:
            self.slot_copy(k).start()
        for copy in self.kept_copies(k):
            copy.start()

    def finish(self, count):
        if self.slotted:
            self.slot_copy(count - 2).wait()
            self.slot_copy(count - 1).wait()
        if self.kept:
            def wait(k, _):
                for copy in self.kept_copies(k):
                    copy.wait()
                return 0
            lax.fori_loop(0, count, wait, 0)


def run_backward(segments, g, gx, x, scales, weights, states, slots, grads, sums, arrive, done):
    h, z, r, c = states
    rows, width = g.shape
    blocks = [slice(i, i + BLOCK) for i in range(0, rows, BLOCK)]
    high = max(segments)

    def segment(i, _):
        k = high - i
        s = k % slots
        arrive(k)
        totals = None
        for at in blocks:
            gg, hh, zz, rr, cc = g[at, :], h[s, at, :], z[s, at, :], r[s, at, :], c[s, at, :]
            gc = (gg * zz * (1.0 - cc * cc)).astype(BF)
            reset_h = nt(gc, weights.cand[k % weights.slots, :width, :])
            gate_z = (gg * (cc - hh) * zz * (1.0 - zz)).astype(BF)
            gm = nt(gc, weights.cand[k % weights.slots, width:, :])
            gate_r = (reset_h * hh * rr * (1.0 - rr)).astype(BF)
            gates = jnp.concatenate([gate_z, gate_r], 1)
            g[at, :] = gg * (1.0 - zz) + reset_h * rr + nt(gates, weights.gate[k % weights.slots, :width, :])
            gm = gm + nt(gates, weights.gate[k % weights.slots, width:, :])
            gx[at, :] = gx[at, :] + gm * scales[pl.ds(k, 1), :]
            grads[k % 2, at, : 2 * width] = gates
            grads[k % 2, at, 2 * width :] = gc
            part = jnp.concatenate([column_sum(gates.astype(F32)), column_sum(gc.astype(F32)),
                                    column_sum(gm * x[at, :])], 1)
            totals = part if totals is None else totals + part
            done.stage(k, at, lambda: ((x[at, :] * scales[pl.ds(k, 1), :]).astype(BF), hh.astype(BF),
                                       (rr * hh).astype(BF)))
        sums[pl.ds(k, 1), :] = totals
        done(k)
        return 0

    full = [k for k in segments if k > 0]
    lax.fori_loop(0, len(full), segment, 0)
    if min(segments) == 0:
        arrive(0)
        totals = None
        for at in blocks:
            gg, zz, cc = g[at, :], z[0, at, :], c[0, at, :]
            gc = (gg * zz * (1.0 - cc * cc)).astype(BF)
            gate_z = (gg * cc * zz * (1.0 - zz)).astype(BF)
            gm = nt(gc, weights.cand[0, width:, :]) + nt(gate_z, weights.gate[0, width:, :width])
            gx[at, :] = gx[at, :] + gm * scales[0:1, :]
            grads[0, at, :width] = gate_z
            grads[0, at, width : 2 * width] = gc
            part = jnp.concatenate([column_sum(gate_z.astype(F32)), jnp.zeros((1, width), F32),
                                    column_sum(gc.astype(F32)), column_sum(gm * x[at, :])], 1)
            totals = part if totals is None else totals + part
            done.stage(0, at, lambda: ((x[at, :] * scales[0:1, :]).astype(BF),))
        sums[0:1, :] = totals
        done.first()


def tn(a, b):
    return lax.dot_general(a, b, (((0,), (0,)), ((), ())), preferred_element_type=F32)


class Terms:
    def __init__(self, count, a, b, grads, made, sems, arrays, after=None):
        self.first_core = lax.axis_index("pipe") % 2 == 0
        self.count, self.a, self.b, self.grads, self.made, self.sems = count, a, b, grads, made, sems
        self.arrays, self.after = arrays, after
        self.width = a.shape[-1]

    def slot(self, k):
        return (self.count - 1 - k) % 2

    def copies(self, k):
        w, part, slot = self.width, self.arrays[0][0].shape[1], self.slot(k)
        start, size = (self.count - 1 - k) * 3 * w, w if k == 0 else 3 * w
        cuts = [(0, start, size)]
        if start < part < start + size:
            cuts = [(0, start, part - start), (part - start, part, start + size - part)]
        return [pltpu.make_async_copy(self.made.at[slot, i, :, pl.ds(at, n)],
                                      self.arrays[i][to // part].at[:, pl.ds(to % part, n)], self.sems.at[slot, i, j])
                for i in range(2) for j, (at, to, n) in enumerate(cuts)]

    def each(self, k, function):
        if isinstance(k, int):
            function(k)
            return
        for known in range(1, self.count):
            pl.when(k == known)(functools.partial(function, known))

    def start(self, k):
        for copy in self.copies(k):
            copy.start()

    def wait(self, k):
        if k < self.count:
            for copy in self.copies(k):
                copy.wait()

    def stage(self, k, at, operands):
        m, *others = operands()
        if not others:
            self.a[0, at, :] = m
            return
        for i, upper in enumerate((~self.first_core, self.first_core)):
            self.a[i, at, :] = jnp.where(upper, others[0], m)
            self.b[i, at, :] = jnp.where(upper, others[1], m)

    def __call__(self, k, source=0, a=None, b=None, grads=None):
        w = self.width
        a, b = (self.a, self.b) if a is None else (a, b)
        grads = self.grads.at[k % 2] if grads is None else grads
        self.each(k, lambda k: self.wait(k + 2))
        for i in range(2):
            self.made[self.slot(k), i, :, : 2 * w] = tn(a[i], grads[:, : 2 * w]).astype(BF)
            self.made[self.slot(k), i, :, 2 * w :] = tn(b[i], grads[:, 2 * w :]).astype(BF)
        self.each(k, self.start)
        if self.after:
            self.after(k)

    def first(self, a=None, grads=None):
        w = self.width
        a = self.a if a is None else a
        grads = self.grads.at[0] if grads is None else grads
        self.wait(2)
        for i, upper in enumerate((~self.first_core, self.first_core)):
            at = pl.multiple_of(jnp.where(upper, 0, w), w)
            self.made[self.slot(0), i, :, :w] = tn(a[0], grads[:, pl.ds(at, w)]).astype(BF)
        self.start(0)
        self.wait(1)
        self.wait(0)


def terms_from_hbm(terms, operands, grads, buffers, sems):
    a, b, g = buffers
    count = terms.count
    width = terms.width

    def copies(k):
        slot = k % 2
        pieces = []
        if k == 0:
            pieces = [(operands.at[0, :, pl.ds(width, width)], a.at[2 * slot])]
        else:
            for j, upper in enumerate((~terms.first_core, terms.first_core)):
                at_a = pl.multiple_of(jnp.where(upper, 0, width), width)
                at_b = pl.multiple_of(jnp.where(upper, 2 * width, width), width)
                pieces += [(operands.at[k, :, pl.ds(at_a, width)], a.at[2 * slot + j]),
                           (operands.at[k, :, pl.ds(at_b, width)], b.at[2 * slot + j])]
        pieces.append((grads.at[k], g.at[slot]))
        return [pltpu.make_async_copy(x, y, sems.at[slot, j]) for j, (x, y) in enumerate(pieces)]

    for copy in copies(count - 1):
        copy.start()
    for k in range(count - 1, -1, -1):
        slot = k % 2
        if k:
            for copy in copies(k - 1):
                copy.start()
        for copy in copies(k):
            copy.wait()
        if k:
            terms(k, a=a.at[pl.ds(2 * slot, 2)], b=b.at[pl.ds(2 * slot, 2)], grads=g.at[slot])
        else:
            terms.first(a=a.at[pl.ds(2 * slot, 2)], grads=g.at[slot])


def norm_sums(gx, xhat_of, sums):
    for i in range(gx.shape[0] // ROWS_MB):
        part = gx[batch_rows(i), :]
        sums[0, i : i + 1, :] = column_sum(part)
        sums[1, i : i + 1, :] = column_sum(part * xhat_of(i))


def xhat_rows(source, moments, i):
    return (source[batch_rows(i), :].astype(F32) - moments[0, i : i + 1, :]) * moments[1, i : i + 1, :]


ANY = pl.BlockSpec(memory_space=pl.ANY)
VM = pl.BlockSpec(memory_space=pltpu.VMEM)
LIMIT = 62 * 1024 * 1024


def layer_cost(segments, rows, width, passes):
    return pl.CostEstimate(flops=segments * passes * rows * 12 * width * width, transcendentals=0,
                           bytes_accessed=segments * (12 * width * width + 16 * rows * width))


def layer1_forward(source, moments, affine, scales, gate_bias, cand_bias, weights, keep):
    rows, width = source.shape
    count = scales.shape[0]

    dp_half = ROWS_MB * lax.axis_size("dp") // 2

    def kernel(*refs):
        if keep:
            source, moments = refs[:2]
            refs = refs[2:]
        else:
            source, first_half, second_half = refs[:3]
            refs = refs[3:]
        affine, scales, gate_bias, cand_bias, w0, w1, w2, w3 = refs[:8]
        refs = refs[8:]
        if keep:
            kept_h, kept_z, kept_r, kept_c = refs[:4]
            x, gate, cand, wsems, h, z, r, c, ksems = refs[4:]
        else:
            last, local, moments = refs[:3]
            x, gate, cand, wsems, h = refs[3:]

        @pl.when(when_active(0))
        def _():
            held = Weights((w0, w1, w2, w3), (gate, cand, wsems))
            for k in range(count):
                held.start(k)
            if not keep:
                finish_moments(first_half, second_half, moments, dp_half)
            normalise(source, moments, affine.at[0], x)
            if keep:
                out = Out(None, None, ((h, kept_h), (z, kept_z), (r, kept_r), (c, kept_c)), ksems)
                run_forward(x, scales, gate_bias, cand_bias, held, h, (z, r, c, None), out)
                out.finish(count)
                return
            run_forward(x, scales, gate_bias, cand_bias, held, h)
            final = h.at[count % 2]
            last[...] = final[...].astype(BF)
            for i in range(rows // ROWS_MB):
                part = low(final[batch_rows(i), :])
                mean = column_sum(part) * (1.0 / ROWS_MB)
                local[0, i : i + 1, :] = mean
                local[1, i : i + 1, :] = column_sum((part - mean) * (part - mean))

    state = jax.ShapeDtypeStruct((count, rows, width), F32)
    by_batch = jax.ShapeDtypeStruct((2, rows // ROWS_MB, width), F32)
    scratch = [pltpu.VMEM((rows, width), F32),
               pltpu.VMEM((count, 2 * width, 2 * width), BF),
               pltpu.VMEM((count, 2 * width, width), BF),
               pltpu.SemaphoreType.DMA((2, count))]
    if keep:
        out_shape = (state,) * 4
        out_specs = (ANY,) * 4
        scratch += [pltpu.VMEM((count + 1, rows, width), F32)] + [pltpu.VMEM((count, rows, width), F32)] * 3
        scratch += [pltpu.SemaphoreType.DMA((4, count))]
    else:
        out_shape = (jax.ShapeDtypeStruct((rows, width), BF), by_batch, by_batch)
        out_specs = (VM, VM, VM)
        scratch += [pltpu.VMEM((2, rows, width), F32)]
    args = (source,) + (moments if isinstance(moments, tuple) else (moments,))
    args += (affine, scales, gate_bias, cand_bias)
    return pl.pallas_call(
        kernel,
        out_shape=out_shape,
        in_specs=[VM] * len(args) + [ANY] * 4,
        out_specs=out_specs,
        scratch_shapes=scratch,
        compiler_params=pltpu.CompilerParams(vmem_limit_bytes=LIMIT),
        cost_estimate=layer_cost(count, rows, width, 1),
        name="layer1_states" if keep else "layer1_forward",
    )(*args, *weights)


def layer2_both(source, halves_of_moments, affine, scales, gate_bias, cand_bias, weights, cotangent):
    rows, width = source.shape
    count = scales.shape[0]

    dp_half = ROWS_MB * lax.axis_size("dp") // 2

    def kernel(source, first_half, second_half, affine, scales, gate_bias, cand_bias, w0, w1, w2, w3, cotangent,
               last, gx_out, nsums, sums, operands_out, grads_out,
               x, gate, cand, wsems, h, z, r, c, operands, osems, g, gx, gsem, moments):
        @pl.when(when_active(1))
        def _():
            held = Weights((w0, w1, w2, w3), (gate, cand, wsems))
            for k in range(count):
                held.start(k)
            core = lax.axis_index("pipe") % 2
            first = pl.multiple_of(core * rows, rows)
            load_g = pltpu.make_async_copy(cotangent.at[pl.ds(first, rows), :], g, gsem.at[0])
            load_g.start()
            finish_moments(first_half, second_half, moments, dp_half)
            normalise(source, moments, affine.at[1], x)
            out = Out((operands, operands_out), osems)
            run_forward(x, scales, gate_bias, cand_bias, held, h, (z, r, c, operands), out)
            last[...] = h[count]
            out.finish(count)
            load_g.wait()
            gx[...] = jnp.zeros_like(gx)

            section = count // 2

            class Left:
                def stage(self, k, at, operands):
                    pass

                def copy(self, k):
                    return pltpu.make_async_copy(operands.at[k % 2], grads_out.at[k], osems.at[k % 2])

                def __call__(self, k):
                    self.copy(k).start()

                def first(self):
                    self.copy(0).start()
                    self.copy(1).wait()
                    self.copy(0).wait()

            left = Left()

            def free(k):
                @pl.when(k <= count - 3)
                def _():
                    left.copy(k + 2).wait()

            run_backward(range(section, count), g, gx, x, scales, held, (h, z, r, c), count, operands, sums, free, left)
            g[...] = low(g[...])
            gx[...] = low(gx[...])
            normalise(source, moments, affine.at[1], x)
            run_backward(range(section), g, gx, x, scales, held, (h, z, r, c), count, operands, sums, free, left)
            gx_out[...] = gx[...].astype(BF)
            norm_sums(gx, lambda i: xhat_rows(source, moments, i), nsums)

    state = pltpu.VMEM((count, rows, width), F32)
    left_out = jax.ShapeDtypeStruct((count, rows, 3 * width), BF)
    return pl.pallas_call(
        kernel,
        out_shape=(jax.ShapeDtypeStruct((rows, width), F32),
                   jax.ShapeDtypeStruct((rows, width), BF),
                   jax.ShapeDtypeStruct((2, rows // ROWS_MB, width), F32),
                   jax.ShapeDtypeStruct((count, 4 * width), F32),
                   left_out, left_out),
        in_specs=[VM] * 7 + [ANY] * 5,
        out_specs=(VM, VM, VM, VM, ANY, ANY),
        scratch_shapes=[pltpu.VMEM((rows, width), F32),
                        pltpu.VMEM((count, 2 * width, 2 * width), BF),
                        pltpu.VMEM((count, 2 * width, width), BF),
                        pltpu.SemaphoreType.DMA((2, count)),
                        pltpu.VMEM((count + 1, rows, width), F32), state, state, state,
                        pltpu.VMEM((2, rows, 3 * width), BF),
                        pltpu.SemaphoreType.DMA((2,)),
                        pltpu.VMEM((rows, width), F32),
                        pltpu.VMEM((rows, width), F32),
                        pltpu.SemaphoreType.DMA((1,)),
                        pltpu.VMEM((2, rows // ROWS_MB, width), F32)],
        compiler_params=pltpu.CompilerParams(vmem_limit_bytes=LIMIT),
        cost_estimate=layer_cost(count, rows, width, 2),
        name="layer2_both",
    )(source, *halves_of_moments, affine, scales, gate_bias, cand_bias, *weights, cotangent)


def layer1_backward(carried, source, moments, affine, scales, weights, kept, operands, grads):
    rows, width = source.shape
    count = scales.shape[0]
    section = count // 2
    slots = 3
    counted = ROWS_MB * lax.axis_size("dp")
    part = (3 * count - 2) * width // 2

    def kernel(gxr, hb, moments2, total_a, total_b, source, moments, affine, scales, w0, w1, w2, w3,
               kept_h, kept_z, kept_r, kept_c, operands_in, grads_in,
               gx, nsums, sums, sent_a, sent_b, mine_a, mine_b,
               x, gate, cand, wsems, h, z, r, c, ksems, g, loaded, a, b, lsems, made, msems):
        held = Weights((w0, w1, w2, w3), (gate, cand, wsems))
        states = ((kept_h, h), (kept_z, z), (kept_r, r), (kept_c, c))

        def copies(k):
            return [pltpu.make_async_copy(x.at[k], y.at[k % slots], ksems.at[i, k % slots])
                    for i, (x, y) in enumerate(states)]

        def arrive(k):
            held.wait(k)
            for copy in copies(k):
                copy.wait()

        def load(k):
            for copy in copies(k):
                copy.start()
            held.start(k)

        def after(k):
            @pl.when(k >= slots)
            def _():
                load(k - slots)

        terms = Terms(count, a, b, loaded, made, msems, ((sent_a, sent_b), (mine_a, mine_b)), after)

        @pl.when(when_active(1))
        def _():
            terms.after = None
            terms_from_hbm(terms, operands_in, grads_in, (a, b, loaded), lsems)

        @pl.when(when_active(0))
        def _():
            terms.after = after
            for k in range(count - 1, count - 1 - slots, -1):
                load(k)
            normalise(source, moments, affine.at[0], x)
            x[...] = low(x[...])
            for i in range(rows // ROWS_MB):
                at = batch_rows(i)
                mean_g, mean_gx = [(total_a[j, i : i + 1, :] + total_b[j, i : i + 1, :]) / counted for j in (0, 1)]
                back = gxr[at, :].astype(F32) - mean_g - xhat_rows(hb, moments2, i) * mean_gx
                g[at, :] = low(affine[1, 0:1, :] * moments2[1, i : i + 1, :] * back)
            gx[...] = jnp.zeros_like(gx)
            run_backward(range(section, count), g, gx, x, scales, held, (h, z, r, c), slots, loaded, sums, arrive, terms)
            g[...] = low(g[...])
            gx[...] = low(gx[...])
            normalise(source, moments, affine.at[0], x)
            run_backward(range(section), g, gx, x, scales, held, (h, z, r, c), slots, loaded, sums, arrive, terms)
            norm_sums(gx, lambda i: xhat_rows(source, moments, i), nsums)

    state = pltpu.VMEM((slots, rows, width), F32)
    terms = jax.ShapeDtypeStruct((width, part), BF)
    args = [*carried, source, moments, affine, scales, *weights, *kept, operands, grads]
    return pl.pallas_call(
        kernel,
        out_shape=(jax.ShapeDtypeStruct((rows, width), F32),
                   jax.ShapeDtypeStruct((2, rows // ROWS_MB, width), F32),
                   jax.ShapeDtypeStruct((count, 4 * width), F32), terms, terms, terms, terms),
        in_specs=[VM] * 9 + [ANY] * 10,
        out_specs=(VM,) * 3 + (ANY,) * 4,
        scratch_shapes=[pltpu.VMEM((rows, width), F32),
                        pltpu.VMEM((slots, 2 * width, 2 * width), BF),
                        pltpu.VMEM((slots, 2 * width, width), BF),
                        pltpu.SemaphoreType.DMA((2, slots)),
                        state, state, state, state,
                        pltpu.SemaphoreType.DMA((4, slots)),
                        pltpu.VMEM((rows, width), F32),
                        pltpu.VMEM((2, rows, 3 * width), BF),
                        pltpu.VMEM((4, rows, width), BF), pltpu.VMEM((4, rows, width), BF),
                        pltpu.SemaphoreType.DMA((2, 5)),
                        pltpu.VMEM((2, 2, width, 3 * width), BF),
                        pltpu.SemaphoreType.DMA((2, 2, 2))],
        compiler_params=pltpu.CompilerParams(vmem_limit_bytes=LIMIT),
        cost_estimate=layer_cost(count, rows, width, 2),
        name="layer1_backward",
    )(*args)


def hot_rows(cats, c, levels):
    level = lax.broadcasted_iota(jnp.int32, (levels, cats.shape[1]), 0)
    return jnp.where(cats[c : c + 1, :] == level, 1.0, 0.0).astype(BF)


def load_columns(categories, cats, sem, rows):
    first = pl.multiple_of((lax.axis_index("pipe") % 2) * rows, rows)
    return pltpu.make_async_copy(categories.at[:, pl.ds(first, rows)], cats, sem)


def embed(numeric, categories, table, rows, own, other, affine):
    numeric_width, columns = numeric.shape[1], categories.shape[0]
    embedded, levels = table.shape
    each = embedded // columns
    packed = 128 // each
    width = numeric_width + embedded

    half = own[0].shape[0]

    def kernel(numeric, categories, table, *refs):
        own, other, (bn_gain, bn_bias) = refs[:4], refs[4:8], refs[8:10]
        source, local, scales, gate_bias, cand_bias, affine, cats, nums, sems = refs[10:]
        core = lax.axis_index("pipe") % 2

        def put(logits, allow, gates, cands, at):
            scales[at : at + half, :] = width * feature_share(logits[...], allow[...])
            gate_bias[at : at + half, :] = gates[...]
            cand_bias[at : at + half, :] = cands[...]

        for at, owner in ((0, 0), (half, 1)):
            pl.when(core == owner)(functools.partial(put, *own, at))
            pl.when(core != owner)(functools.partial(put, *other, at))
        for layer in range(2):
            affine[layer, 0:1, :] = bn_gain[layer : layer + 1, :]
            affine[layer, 1:2, :] = bn_bias[layer : layer + 1, :]
        first = pl.multiple_of((lax.axis_index("pipe") % 2) * rows, rows)
        load = load_columns(categories, cats, sems.at[0], rows)
        load_numeric = pltpu.make_async_copy(numeric.at[pl.ds(first, rows), :], nums, sems.at[1])
        load.start()
        load_numeric.start()
        load.wait()
        row = lax.broadcasted_iota(jnp.int32, (128, levels), 0) // each
        for group in range(columns // packed):
            part = table[group * 128 : (group + 1) * 128, :]
            weights = jnp.concatenate([jnp.where(row == i, part, jnp.zeros_like(part)) for i in range(packed)], 1)
            hot = jnp.concatenate([hot_rows(cats, group * packed + i, levels) for i in range(packed)], 0)
            start = numeric_width + group * 128
            source[:, start : start + 128] = nn(weights, hot).T
        load_numeric.wait()
        source[:, :numeric_width] = nums[...]
        for i in range(rows // ROWS_MB):
            part = source[batch_rows(i), :]
            mean = column_sum(part) * (1.0 / ROWS_MB)
            local[0, i : i + 1, :] = mean
            local[1, i : i + 1, :] = column_sum((part - mean) * (part - mean))

    return pl.pallas_call(
        kernel,
        out_shape=(jax.ShapeDtypeStruct((rows, width), F32),
                   jax.ShapeDtypeStruct((2, rows // ROWS_MB, width), F32),
                   jax.ShapeDtypeStruct((2 * half, width), F32),
                   jax.ShapeDtypeStruct((2 * half, 2 * width), F32),
                   jax.ShapeDtypeStruct((2 * half, width), F32),
                   jax.ShapeDtypeStruct((2, 2, width), F32)),
        in_specs=[ANY, ANY] + [VM] * 11,
        out_specs=(VM,) * 6,
        scratch_shapes=[pltpu.VMEM((columns, rows), jnp.int32), pltpu.VMEM((rows, numeric_width), F32),
                        pltpu.SemaphoreType.DMA((2,))],
        compiler_params=pltpu.CompilerParams(vmem_limit_bytes=LIMIT),
        cost_estimate=pl.CostEstimate(flops=8 * rows * width * levels, transcendentals=0, bytes_accessed=8 * rows * width),
        name="embed",
    )(numeric, categories, table, *own, *other, *affine)


def feature_grads(gx, source, moments, totals, gain, categories, table_shape):
    rows, width = gx.shape
    embedded, levels = table_shape
    columns = categories.shape[0]
    each = embedded // columns
    numeric_width = width - embedded
    half = columns // 2

    def kernel(gx, source, moments, totals, gain, categories, numeric, sent, mine, cats, back, table, sem):
        load = load_columns(categories, cats, sem.at[0], rows)
        load.start()
        for i in range(rows // ROWS_MB):
            at = batch_rows(i)
            part = gx[at, :] - totals[0, i : i + 1, :] - xhat_rows(source, moments, i) * totals[1, i : i + 1, :]
            back[at, :] = gain[...] * moments[1, i : i + 1, :] * part
        numeric[...] = back[:, :numeric_width]
        load.wait()
        table[...] = jnp.zeros_like(table)
        for group in range(embedded // 128):
            start = numeric_width + group * 128
            grads = back[:, start : start + 128].astype(BF)
            lane = lax.broadcasted_iota(jnp.int32, (levels, 128), 1) // each
            blocks = jnp.zeros((levels, 128), F32)
            for i in range(128 // each):
                c = group * (128 // each) + i
                blocks = jnp.where(lane == i, nn(hot_rows(cats, c, levels), grads), blocks)
            turned = blocks.T
            for i in range(128 // each):
                c = group * (128 // each) + i
                for e in range(each):
                    at = i * each + e
                    table[c // half, c % half : c % half + 1, e * levels : (e + 1) * levels] = turned[at : at + 1, :]
        core = lax.axis_index("pipe") % 2
        sent[...] = table[1 - core].astype(BF)
        mine[...] = table[core].astype(BF)

    part = jax.ShapeDtypeStruct((16, each * levels), BF)
    return pl.pallas_call(
        kernel,
        out_shape=(jax.ShapeDtypeStruct((rows, numeric_width), F32), part, part),
        in_specs=[VM] * 5 + [ANY],
        out_specs=(VM, VM, VM),
        scratch_shapes=[pltpu.VMEM((columns, rows), jnp.int32), pltpu.VMEM((rows, width), F32),
                        pltpu.VMEM((2, 16, each * levels), F32), pltpu.SemaphoreType.DMA((1,))],
        compiler_params=pltpu.CompilerParams(vmem_limit_bytes=LIMIT),
        cost_estimate=pl.CostEstimate(flops=8 * rows * width * levels, transcendentals=0, bytes_accessed=16 * rows * width),
        name="feature_grads",
    )(gx, source, moments, totals, gain, categories)


def spare_totals(pieces, rows, used, logits, allow):
    count = len(pieces)
    spare, columns = pieces[0].shape[0] - rows, pieces[0].shape[1]
    half, width = logits.shape

    def kernel(logits, allow, *refs):
        pieces, (table, gate_b, cand_b, logit, gain, bias, parts, sems) = refs[:count], refs[count:]
        copies = [pltpu.make_async_copy(piece.at[pl.ds(rows, spare), :], parts.at[i], sems.at[i])
                  for i, piece in enumerate(pieces)]
        for copy in copies:
            copy.start()
        shares = feature_share(logits[...], allow[...])
        for copy in copies:
            copy.wait()
        spot = ring_place(count)
        added = jnp.zeros((spare, columns), F32)
        for place in range(count):
            added = added + parts[lax.rem(spot - place + count, count)].astype(F32)
        table[...] = added[:used, :]
        small = added[used:, : columns // 2] + added[used:, columns // 2 :]
        gate_b[...] = small[:half, : 2 * width]
        cand_b[...] = small[:half, 2 * width : 3 * width]
        scaled = width * small[:half, 3 * width :]
        logit[...] = shares * (scaled - jnp.sum(shares * scaled, axis=-1, keepdims=True))
        for layer in range(2):
            at = layer * width
            bias[layer : layer + 1, :] = small[half : half + 1, at : at + width]
            gain[layer : layer + 1, :] = small[half : half + 1, 2 * width + at : 3 * width + at]

    def out(*shape):
        return jax.ShapeDtypeStruct(shape, F32)

    return pl.pallas_call(
        kernel,
        out_shape=(out(used, columns), out(half, 2 * width), out(half, width), out(half, width), out(2, width),
                   out(2, width)),
        in_specs=[VM, VM] + [ANY] * count,
        out_specs=(VM,) * 6,
        scratch_shapes=[pltpu.VMEM((count, spare, columns), BF), pltpu.SemaphoreType.DMA((count,))],
        compiler_params=pltpu.CompilerParams(vmem_limit_bytes=LIMIT),
        name="spare_totals",
    )(logits, allow, *pieces)


def ring_place(places):
    place = lax.axis_index("dp")
    spot = jnp.where(place % 2 == 0, place // 2, places - 1 - place // 2)
    return jnp.where(lax.axis_index("pipe") % 2 == 0, spot, places - 1 - spot)


def blank_outputs(per_core, width):
    def kernel(gate, cand, zeros, sems):
        @pl.when(lax.axis_index("pipe") % 2 == 0)
        def _():
            zeros[...] = jnp.zeros_like(zeros)
            copies = [
                pltpu.make_async_copy(zeros, gate.at[0, pl.ds(0, width), :], sems.at[0]),
                pltpu.make_async_copy(zeros.at[:, pl.ds(0, width)],
                                      gate.at[0, pl.ds(width, width), pl.ds(width, width)], sems.at[1]),
                pltpu.make_async_copy(zeros.at[:, pl.ds(0, width)], cand.at[0, pl.ds(0, width), :], sems.at[2])]
            for copy in copies:
                copy.start()
            for copy in copies:
                copy.wait()

    return pl.pallas_call(
        kernel,
        out_shape=(jax.ShapeDtypeStruct((per_core, 2 * width, 2 * width), F32),
                   jax.ShapeDtypeStruct((per_core, 2 * width, width), F32)),
        out_specs=(ANY, ANY),
        scratch_shapes=[pltpu.VMEM((width, 2 * width), F32), pltpu.SemaphoreType.DMA((3,))],
        name="blank_outputs",
    )()


def place_block(step, blocks, mine, other, extra, gate, cand):
    rows, columns = other.shape
    per_core, width = gate.shape[0], cand.shape[2]
    given = () if extra is None else (extra,)

    def kernel(*refs):
        mine, other = refs[:2]
        extra = refs[2] if given else None
        gate, cand, onward, full, tail, sems = refs[4 + len(given) :]
        spot = ring_place(blocks)
        copies = []

        def copy(source, target, j, row, size):
            copies.append(pltpu.make_async_copy(
                source, target.at[j, pl.ds(row, rows), pl.ds(0, size)], sems.at[len(copies)]))
            copies[-1].start()

        def at(block):
            return pl.multiple_of(block * rows, rows)

        def put(own_half, first_layer):
            del copies[:]
            own_block = lax.rem(spot + 1 - step + blocks, blocks)
            other_block = lax.rem(2 * blocks - spot + step, blocks)
            if not first_layer and given:
                put_extra(spot, step - 1, blocks, extra, tail, cand, copies, sems)
            for piece, half, block in ((mine, own_half, own_block), (other, 1 - own_half, other_block)):
                full[half] = piece[:rows, :].astype(F32)
                for j in range(per_core):
                    start = (per_core - 1 - j) * 3 * width + (width if first_layer else 0)
                    source = full.at[half]
                    if first_layer and j == 0:
                        copy(source.at[:, pl.ds(start, width)], cand if half else gate, 0, width + at(block), width)
                        continue
                    copy(source.at[:, pl.ds(start, 2 * width)], gate, j, half * width + at(block), 2 * width)
                    if j or first_layer:
                        copy(source.at[:, pl.ds(start + 2 * width, width)], cand, j, half * width + at(block), width)
            if first_layer:
                onward[:rows, :] = mine[:rows, :width]
                onward[rows:, :] = other[:, :width]
            for item in copies:
                item.wait()

        core = lax.axis_index("pipe") % 2
        pl.when(core == 0)(functools.partial(put, 0, True))
        pl.when(core == 1)(functools.partial(put, 1, False))

    args = (mine, other, *given, gate, cand)
    return pl.pallas_call(
        kernel,
        out_shape=(jax.ShapeDtypeStruct(gate.shape, F32), jax.ShapeDtypeStruct(cand.shape, F32),
                   jax.ShapeDtypeStruct((2 * rows, width), BF)),
        in_specs=[VM] * (len(args) - 2) + [ANY] * 2,
        out_specs=(ANY, ANY, VM),
        input_output_aliases={len(args) - 2: 0, len(args) - 1: 1},
        scratch_shapes=[pltpu.VMEM((2, rows, columns), F32), pltpu.VMEM((2, rows, width), F32),
                        pltpu.SemaphoreType.DMA((4 * per_core,))],
        compiler_params=pltpu.CompilerParams(vmem_limit_bytes=LIMIT),
        name=f"place_block_{step}",
    )(*args)


def put_extra(spot, step, blocks, extra, tail, cand, copies, sems):
    rows, width = tail.shape[1:]
    for half, block in ((0, lax.rem(2 * blocks - spot - step, blocks)), (1, lax.rem(spot + 1 + step, blocks))):
        tail[half] = extra[half * rows : (half + 1) * rows, :].astype(F32)
        row = half * width + pl.multiple_of(block * rows, rows)
        copies.append(pltpu.make_async_copy(tail.at[half], cand.at[0, pl.ds(row, rows), :], sems.at[len(copies)]))
        copies[-1].start()


def place_extra(step, blocks, extra, cand):
    width = cand.shape[2]
    rows = extra.shape[0] // 2

    def kernel(extra, unused, cand, tail, sems):
        @pl.when(lax.axis_index("pipe") % 2 == 1)
        def _():
            copies = []
            put_extra(ring_place(blocks), step, blocks, extra, tail, cand, copies, sems)
            for item in copies:
                item.wait()

    return pl.pallas_call(
        kernel,
        out_shape=jax.ShapeDtypeStruct(cand.shape, F32),
        in_specs=[VM, ANY],
        out_specs=ANY,
        input_output_aliases={1: 0},
        scratch_shapes=[pltpu.VMEM((2, rows, width), F32), pltpu.SemaphoreType.DMA((2,))],
        compiler_params=pltpu.CompilerParams(vmem_limit_bytes=LIMIT),
        name="place_extra",
    )(extra, cand)


def tied(*values):
    return lax.optimization_barrier(values)


class Ring:
    def __init__(self, parts=None, held=None, unit=None, turn=None):
        self.turn = turn
        self.unit = unit
        self.places = lax.axis_size("dp")
        order = list(range(0, self.places, 2)) + list(range(1, self.places, 2))[::-1]
        lanes = lax.axis_size("pipe")
        self.pairs = []
        for lane in range(lanes):
            way = order if lane % 2 == 0 else order[::-1]
            self.pairs += [(way[i] * lanes + lane, way[(i + 1) % self.places] * lanes + lane)
                           for i in range(self.places)]
        self.spot = ring_place(self.places)
        self.parts = ()
        self.done = 0
        self.held = held
        if held is None:
            mine, received, first = parts
            self.rows = mine.shape[0] // self.places
            self.parts = (mine, received)
            self.held = (self.rows_of(mine, self.spot).astype(F32) + first.astype(F32)).astype(BF)

    def rows_of(self, part, number):
        at = lax.rem(number + self.places, self.places) * self.rows
        return lax.dynamic_slice_in_dim(part, at, self.rows, 0)

    def block(self, number):
        a, b = [self.rows_of(part, number) for part in self.parts]
        return a.astype(F32) + b.astype(F32)

    def step(self, sends=(), work=None, ends=None, wait=True):
        self.done += 1
        sent = len(sends)
        works = work if isinstance(work, list) else [work] if work else []
        held, *values = tied(self.held, *[value for _, value in sends], *[value for _, given in works for value in given])
        got = lax.ppermute(held, ("dp", "pipe"), self.pairs)
        given = [send(value) for (send, _), value in zip(sends, values)]
        outs, values = [], values[sent:]
        for function, arguments in works + ([ends] if ends else []):
            if function is not (ends or [None])[0]:
                arguments, values = values[: len(arguments)], values[len(arguments) :]
            result = function(*arguments)
            outs += list(result) if isinstance(result, (tuple, list)) else [result]
        if self.turn is not None:
            got, *_ = tied(got, *self.turn)
            self.turn[:] = [got]
        got, *outs = tied(got, *outs, *(given if wait else ()))
        if wait:
            given, outs = outs[len(outs) - sent :], outs[: len(outs) - sent]
        if self.unit is not None and self.done < self.places - 1:
            got = got * self.unit
        if self.parts:
            got = (self.block(self.spot - self.done) + got.astype(F32)).astype(BF)
        self.held = got
        return list(given) + outs


def on_device(numeric, categories, cardinalities, embed_table, bn_gain, bn_bias, mask_logits,
              feature_allow, gate_weight, gate_bias, cand_weight, cand_bias, out_grad):
    rank = lax.axis_index("pipe")
    core = rank % 2
    first_core = core == 0
    top = rank >= lax.axis_size("pipe") // 2
    width = out_grad.shape[1]
    numeric_width = numeric.shape[1]
    columns, levels, embed_width = embed_table.shape
    batches = MB // 2
    rows = batches * ROWS_MB
    counted = ROWS_MB * lax.axis_size("dp")

    def my_rows(array):
        return lax.dynamic_slice_in_dim(array, core * rows, rows, 0)

    def by_batch(array):
        return array.reshape(batches, ROWS_MB, array.shape[-1])

    half = gate_weight.shape[0]
    count = 2 * half
    flat_table = jnp.swapaxes(embed_table, 1, 2).reshape(columns * embed_width, levels)
    category_columns = categories.T
    own_small = (mask_logits, feature_allow, gate_bias, cand_bias)
    other_small = tuple(core_swap(value) for value in own_small)
    *other_small, own_gate, own_cand = tied(*other_small, gate_weight, cand_weight)
    weights = (gate_weight, core_swap(own_gate), cand_weight, core_swap(own_cand))
    source1, local1, scales, gate_b, cand_b, affine = embed(
        numeric, category_columns, flat_table, rows, own_small, other_small, (bn_gain, bn_bias))
    h1, local2, moments1 = layer1_forward(
        source1, last_pair(dp_moments(local1, ROWS_MB)), affine, scales, gate_b, cand_b, weights, False)
    source2 = to_layer(h1, True)
    local2 = dp_moments(local2, ROWS_MB)
    halves2 = last_pair_to_layer(local2, True)
    local2, source1 = lax.optimization_barrier((local2, source1))
    kept_states = layer1_forward(source1, moments1, affine, scales, gate_b, cand_b, weights, True)
    mean2, spread2 = merged(*last_pair(local2), counted // 2)
    moments2 = jnp.stack([mean2, lax.rsqrt(spread2 / counted + EPS)])
    h2, gx2, nsums2, sums2, operands, grads = layer2_both(
        source2, halves2, affine, scales, gate_b, cand_b, weights, out_grad)
    received = to_layer(gx2, False)
    totals2 = last_pair_to_layer(partial_total(nsums2), False)

    def layer_columns(value):
        share = value.shape[1] // 4
        pieces = value.reshape(rows, 2, 2, share)
        kept = jnp.where(first_core, pieces[:, :, 0], pieces[:, :, 1])
        got = core_swap(jnp.where(first_core, pieces[:, :, 1], pieces[:, :, 0]))
        both = jnp.where(first_core, jnp.stack([kept, got]), jnp.stack([got, kept]))
        return both.reshape(2 * rows, 2, share)

    def pick(a, b):
        return jnp.where(top, a, b)

    gx1, nsums1, sums1, sent_a, sent_b, mine_a, mine_b = layer1_backward(
        (received, h1, moments2, *totals2), source1, moments1, affine, scales, weights, kept_states, operands, grads)
    places = lax.axis_size("dp")

    def first_block(sent):
        rows = sent.shape[0] // places
        return core_swap(lax.dynamic_slice_in_dim(sent, (places - 1 - ring_place(places)) * rows, rows, 0))

    first_a, first_b = first_block(sent_a), first_block(sent_b)
    first_a, first_b, sent_a, sent_b = tied(first_a, first_b, sent_a, sent_b)
    upper = Ring((mine_a, core_swap(sent_a), first_a))
    lower = Ring((mine_b, core_swap(sent_b), first_b))
    pipes = lax.axis_size("pipe")

    levels_of_dp = [1 << i for i in range(places.bit_length() - 1)]

    def over_layers(value):
        return lax.ppermute(value, "pipe", [(i, (i + pipes // 2) % pipes) for i in range(pipes)])

    def small_sums(sums1, sums2, nsums1, nsums2):
        small = pick(sums2, sums1).reshape(count, 4 * width)
        kept, sent_sums = halves(small, ~first_core)
        sums = [nsums.sum(axis=1) for nsums in (nsums1, nsums2)]
        sums = jnp.stack([jnp.where(top, 0.0, sums[0]), jnp.where(top, sums[1], 0.0)], axis=1).reshape(-1, 4 * width)
        small = jnp.concatenate([kept, sums]) + core_swap(jnp.concatenate([sent_sums, sums]))
        return small

    def features(gx1, totals1):
        return feature_grads(gx1, source1, moments1, totals1, bn_gain[:1], category_columns, flat_table.shape)

    totals1 = nsums1
    used = columns // 2
    chain = [("sum", level) for level in levels_of_dp] + [("features",), ("cores",), ("layers",)]
    while lower.done < places - 1:
        act = chain.pop(0) if chain else ("",)
        if act[0] == "sum":
            got, *_ = upper.step(((functools.partial(dp_swap, step=act[1]), totals1),),
                                 ends=None if lower.done else (lambda held: held, (lower.held,)))
            totals1 = totals1 + got
        elif act[0] == "features":
            numeric_back, table_sent, table = upper.step(work=(features, (gx1, totals1 / counted)))
        elif act[0] == "cores":
            got, = upper.step(((core_swap, table_sent),))
            table = plus(table, got)
        elif act[0] == "layers":
            got, got_sums = upper.step(((functools.partial(to_layer, up=True), table), (over_layers, small[half:])))
            high = lax.reduce_precision(jnp.concatenate([small[:half], small[half:] + got_sums]), 8, 7)
            low_part = jnp.concatenate([small[:half], small[half:] + got_sums]) - high
            table = jnp.concatenate([pick(got, table)[:used], jnp.concatenate([high, low_part], 1).astype(BF)])
        else:
            upper.step()
        if lower.done == 1:
            small, = lower.step(work=(small_sums, (sums1, sums2, nsums1, nsums2)))
        elif lower.done == 5:
            block, = lower.step(work=(layer_columns, (h2,)))
        elif lower.done == 2:
            gate_w, cand_w = lower.step(work=(lambda: blank_outputs(half, width), ()))
        else:
            lower.step()

    block_rows = upper.held.shape[0]
    unit = (1.0 + 0.0 * cardinalities[0].astype(F32)).astype(BF)
    turn = []
    own = Ring(held=jnp.concatenate([jnp.where(first_core, lower.held, upper.held), table]), unit=unit, turn=turn)
    other = Ring(held=core_swap(jnp.where(first_core, upper.held, lower.held)), unit=unit, turn=turn)
    mine, extra = [], None
    for s in range(places):
        mine.append(own.held)
        place = functools.partial(place_block, s, places)
        if extra is None:
            place = lambda a, b, *rest: place_block(0, places, a, b, None, *rest)
        values = (own.held, other.held, *(() if extra is None else (extra,)), gate_w, cand_w)
        if s == places - 1:
            gate_w, cand_w, extra = place(*values)
            break
        if s == places - 2:
            gate_w, cand_w, extra = own.step(ends=(place, values))
            extra = core_swap(extra)
            other.step()
            continue
        own.step()
        sends, ends, works = (), None, [(place, values)]
        if s == 1:
            sends = ((functools.partial(to_layer, up=False), block[:, 0]),)
        elif s == 2:
            ends = (layer_columns, (numeric_back,))
        elif s == 3:
            sends = ((functools.partial(to_layer, up=True), numeric_part[:, 1]),)
        elif s == 5:
            works.append((lambda a, b, c, d: (pick(a, b), pick(c, d)),
                          (block[:, 1], got_block, got_numeric, numeric_part[:, 0])))
        outs = other.step(sends, works, ends, wait=False)
        if s == 1:
            got_block = outs.pop(0)
        elif s == 3:
            got_numeric = outs.pop(0)
        gate_w, cand_w, extra, *outs = outs
        extra = core_swap(extra)
        if s == 2:
            numeric_part, = outs
        elif s == 5:
            block_out, numeric_grad = outs
    cand_w = place_extra(places - 1, places, core_swap(extra), cand_w)
    table, gate_b, cand_b, logit, gain, bias = spare_totals(mine, block_rows, used, mask_logits, feature_allow)
    table = joined(table, core_swap(table), ~first_core)
    table = jnp.swapaxes(table.reshape(columns, embed_width, levels), 1, 2)
    return (block_out, numeric_grad, table, gain, bias, logit,
            gate_w, gate_b, cand_w, cand_b)


def solution(mesh):
    in_specs = (P("dp", None), P("dp", None), P(), P(), P(), P(), P("pipe", None), P("pipe", None),
                P("pipe", None, None), P("pipe", None), P("pipe", None, None), P("pipe", None),
                P("dp", None))
    out_specs = (P("dp", "pipe"), P("dp", "pipe"), P(), P(), P(), P("pipe", None),
                 P("pipe", None, None), P("pipe", None), P("pipe", None, None), P("pipe", None))
    return jax.shard_map(on_device, mesh=mesh, in_specs=in_specs, out_specs=out_specs, check_vma=False)
```

profile of v0, /device:TPU:1, one launch (start us, length us, event | category | flops | bytes accessed | tf_op | source)
XLA Modules:
  0.0 344.5 jit_solution(4897241041460104986)
XLA Ops:
  3.4 4.6 %embed.1 = (f32[512,512]{1,0:T(8,128)}, f32[2,4,512]{2,1,0:T(4,128)}, f32[6,512]{1,0:T(8,128)}, f32[6,1024]{1,0:T(8,128)}, f32[6,512]{1,0:T(8,128)}, /*index=5*/f32[2,2,512]{2,1,0:T(2,128)}) custom-call(f32[1024,128]{1,0:T(8,128)} %numeric.1, s32[24,1024]{1,0:T(8,128)} %bitcast.66, bf16[384,256]{1,0:T(8,128)(2,1)} %bitcast.68, f32[3,512]{1,0:T(4,128)} %logits.1, ...), custom_call_target="tpu_custom_call" | custom-call | flops 536870912 | bytes 2097152 | tf_op jit(solution)/shard_map/embed/pallas_call | solution.py:760
  8.0 2.7 collective-permute-start.4
  12.7 2.5 collective-permute-start.5
  19.7 14.6 %layer1_forward.1 = (bf16[512,512]{1,0:T(8,128)(2,1)}, f32[2,4,512]{2,1,0:T(4,128)}, f32[2,4,512]{2,1,0:T(4,128)}) custom-call(f32[512,512]{1,0:T(8,128)} %get-tuple-element.228.refs_0_.source, f32[2,4,512]{2,1,0:T(4,128)} %copy-done.31, f32[2,4,512]{2,1,0:T(4,128)} %copy-done.42, f32[2,2,512]{2,1,0:T(2,128)} %get-tuple-element.217.refs_3_.affine.refs_2_, ...), custom_call_target="tpu_custom_call" | custom-call | flops 9663676416 | bytes 44040192 | tf_op jit(solution)/shard_map/layer1_forward/pallas_call | solution.py:516
  34.4 1.4 collective-permute-start.10
  38.0 2.4 collective-permute-start.11
  47.0 3.0 layer2_both.1
  52.6 17.5 %layer1_states.1 = (f32[6,512,512]{2,1,0:T(8,128)}, f32[6,512,512]{2,1,0:T(8,128)}, f32[6,512,512]{2,1,0:T(8,128)}, f32[6,512,512]{2,1,0:T(8,128)}) custom-call(f32[512,512]{1,0:T(8,128)} %get-tuple-element.228.refs_0_.source, f32[2,4,512]{2,1,0:T(4,128)} %get-tuple-element.229.refs_1_.moments, f32[2,2,512]{2,1,0:T(2,128)} %get-tuple-element.217.refs_3_.affine.refs_2_, ...), custom_call_target="tpu_custom_call" | custom-call | flops 9663676416 | bytes 44040192 | tf_op jit(solution)/shard_map/layer1_states/pallas_call | solution.py:516
  70.1 2.4 collective-permute-start.17
  77.0 11.1 %collective-permute-done.18.total_a = f32[2,4,512]{2,1,0:T(4,128)S(1)} collective-permute-done((f32[2,4,512]{2,1,0:T(4,128)S(1)}, f32[2,4,512]{2,1,0:T(4,128)S(1)}, u32[]{:S(2)}, u32[]{:S(2)}) %collective-permute-start.18) | collective-permute-done | bytes 16416 | tf_op jit(solution)/shard_map/ppermute | solution.py:32
  90.2 38.6 %layer1_backward.1 = (f32[512,512]{1,0:T(8,128)}, f32[2,4,512]{2,1,0:T(4,128)}, f32[6,2048]{1,0:T(8,128)}, bf16[512,4096]{1,0:T(8,128)(2,1)}, bf16[512,4096]{1,0...) custom-call(bf16[512,512]{1,0:T(8,128)(2,1)} %copy-done.34, ...), custom_call_target="tpu_custom_call" | custom-call | flops 19327352832 | bytes 44040192 | tf_op jit(solution)/shard_map/layer1_backward/pallas_call | solution.py:679
  130.0 8.8 %collective-permute-start.21 = (bf16[64,4096]{1,0:T(8,128)(2,1)S(1)}, bf16[64,4096]{1,0:T(8,128)(2,1)S(1)}, u32[]{:S(2)}, u32[]{:S(2)}) collective-permute-start(bf16[64,4096]{1,0:T(8,128)(2,1)S(1)} %constant_dynamic-slice_fusion), channel_id=1, source_target_pairs={{0,1},{1,0},{2,3},{3,2},{4,5},{5,4},{6,7},{7,6},{8,9},{9,8},{10,11... | collective-permute-start | bytes 1572872 | tf_op jit(solution)/shard_map/ppermute | solution.py:26
  140.3 1.6 collective-permute-done.20
  146.8 2.0 collective-permute-start.24
  148.7 8.2 %collective-permute-done.24 = f32[2,4,512]{2,1,0:T(4,128)S(1)} collective-permute-done((f32[2,4,512]{2,1,0:T(4,128)S(1)}, f32[2,4,512]{2,1,0:T(4,128)S(1)}, u32[]{:S(2)}, u32[]{:S(2)}) %collective-permute-start.24) | collective-permute-done | bytes 16416 | tf_op jit(solution)/shard_map/ppermute | solution.py:36
  157.5 1.4 add_convert_fusion.13
  158.9 1.7 collective-permute-start.25
  160.6 1.4 add_convert_fusion.8
  163.4 2.0 collective-permute-start.26
  165.9 1.6 collective-permute-done.26
  167.5 1.4 add_convert_fusion.12
  168.9 1.5 collective-permute-start.27
  171.4 2.9 collective-permute-done.34
  174.3 1.4 add_convert_fusion.5
  176.0 4.7 %collective-permute-done.28 = f32[2,4,512]{2,1,0:T(4,128)S(1)} collective-permute-done((f32[2,4,512]{2,1,0:T(4,128)S(1)}, f32[2,4,512]{2,1,0:T(4,128)S(1)}, u32[]{:S(2)}, u32[]{:S(2)}) %collective-permute-start.28) | collective-permute-done | bytes 16416 | tf_op jit(solution)/shard_map/ppermute | solution.py:36
  180.7 1.4 add_convert_fusion.11
  182.7 3.2 collective-permute-done.40
  187.4 5.0 %feature_grads.1 = (f32[512,128]{1,0:T(8,128)}, bf16[16,4096]{1,0:T(8,128)(2,1)}, bf16[16,4096]{1,0:T(8,128)(2,1)}) custom-call(f32[512,512]{1,0:T(8,128)} %get-tuple-element.258.gx, f32[512,512]{1,0:T(8,128)} %get-tuple-element.228.refs_0_.source, f32[2,4,512]{2,1,0:T(4,128)} %get-tuple-element.229.refs_1_.moments, f32[2,4,512]{2,1,0:T(4,128)} %add_multiply_fusion.totals, ...), custom_call_target="tpu_custom_call" | custom-call | flops 536870912 | bytes 4194304 | tf_op jit(solution)/shard_map/feature_grads/pallas_call | solution.py:815
  192.4 1.6 add_convert_fusion.10
  194.9 5.5 %collective-permute-start.31 = (bf16[16,4096]{1,0:T(8,128)(2,1)}, bf16[16,4096]{1,0:T(8,128)(2,1)S(1)}, u32[]{:S(2)}, u32[]{:S(2)}) collective-permute-start(bf16[16,4096]{1,0:T(8,128)(2,1)} %get-tuple-element.266), channel_id=1, source_target_pairs={{0,1},{1,0},{2,3},{3,2},{4,5},{5,4},{6,7},{7,6},{8,9},{9,8},{10,11... | collective-permute-start | bytes 393224 | tf_op jit(solution)/shard_map/ppermute | solution.py:26
  200.4 1.4 add_convert_fusion.3
  204.9 1.5 add_convert_fusion.9
  208.6 1.9 collective-permute-start.37
  210.6 1.4 add_convert_fusion.2
  213.6 3.7 %collective-permute-start.44 = (f32[512,2,128]{2,1,0:T(2,128)S(1)}, f32[512,2,128]{2,1,0:T(2,128)S(1)}, u32[]{:S(2)}, u32[]{:S(2)}) collective-permute-start(f32[512,2,128]{2,1,0:T(2,128)S(1)} %bitcast.62), channel_id=1, source_target_pairs={{0,1},{1,0},{2,3},{3,2},{4,5},{5,4},{6,7},{7,6},{8,9},{9,8},{10,11... | collective-permute-start | bytes 1572872 | tf_op jit(solution)/shard_map/ppermute | solution.py:26
  217.8 1.6 add_convert_fusion.7
  220.9 5.2 %collective-permute-done.43 = bf16[64,4096]{1,0:T(8,128)(2,1)S(1)} collective-permute-done((bf16[64,4096]{1,0:T(8,128)(2,1)S(1)}, bf16[64,4096]{1,0:T(8,128)(2,1)S(1)}, u32[]{:S(2)}, u32[]{:S(2)}) %collective-permute-start.43) | collective-permute-done | bytes 524320 | tf_op jit(solution)/shard_map/ppermute | solution.py:1037
  227.6 4.1 %collective-permute-done.39 = bf16[64,4096]{1,0:T(8,128)(2,1)S(1)} collective-permute-done((bf16[64,4096]{1,0:T(8,128)(2,1)S(1)}, bf16[64,4096]{1,0:T(8,128)(2,1)S(1)}, u32[]{:S(2)}, u32[]{:S(2)}) %collective-permute-start.39) | collective-permute-done | bytes 524320 | tf_op jit(solution)/shard_map/ppermute | solution.py:1037
  231.7 5.6 %collective-permute-done.45 = bf16[64,4096]{1,0:T(8,128)(2,1)S(1)} collective-permute-done((bf16[64,4096]{1,0:T(8,128)(2,1)S(1)}, bf16[64,4096]{1,0:T(8,128)(2,1)S(1)}, u32[]{:S(2)}, u32[]{:S(2)}) %collective-permute-start.45) | collective-permute-done | bytes 524320 | tf_op jit(solution)/shard_map/ppermute | solution.py:1037
  237.3 2.1 broadcast_select_fusion.1
  239.6 1.9 collective-permute-start.46
  244.5 3.4 place_block_0.1
  247.9 1.4 collective-permute-done.48
  250.6 4.3 %collective-permute-done.47 = bf16[64,4096]{1,0:T(8,128)(2,1)S(1)} collective-permute-done((bf16[64,4096]{1,0:T(8,128)(2,1)S(1)}, bf16[64,4096]{1,0:T(8,128)(2,1)S(1)}, u32[]{:S(2)}, u32[]{:S(2)}) %collective-permute-start.47) | collective-permute-done | bytes 524320 | tf_op jit(solution)/shard_map/ppermute | solution.py:1037
  254.9 1.9 collective-permute-start.49
  259.9 3.4 place_block_1.1
  264.6 3.0 collective-permute-done.50
  267.6 1.8 collective-permute-start.52
  270.7 3.6 %place_block_2.1 = (f32[3,1024,1024]{2,1,0:T(8,128)}, f32[3,1024,512]{2,1,0:T(8,128)}, bf16[128,512]{1,0:T(8,128)(2,1)}) custom-call(bf16[80,4096]{1,0:T(8,128)(2,1)} %copy-done.2, bf16[64,4096]{1,0:T(8,128)(2,1)} %copy-done.12, bf16[128,512]{1,0:T(8,128)(2,1)} %collective-permute-done.52.refs_2_, ...), custom_call_target="tpu_custom_call", output_to_operand_aliasing={{0}: (3, {}), {1}: (4, {})} | custom-call | tf_op jit(solution)/shard_map/place_block_2/pallas_call | solution.py:951
  275.8 4.3 %collective-permute-done.53 = bf16[64,4096]{1,0:T(8,128)(2,1)S(1)} collective-permute-done((bf16[64,4096]{1,0:T(8,128)(2,1)S(1)}, bf16[64,4096]{1,0:T(8,128)(2,1)S(1)}, u32[]{:S(2)}, u32[]{:S(2)}) %collective-permute-start.53) | collective-permute-done | bytes 524320 | tf_op jit(solution)/shard_map/ppermute | solution.py:1037
  280.2 1.9 collective-permute-start.56
  284.1 5.6 %collective-permute-start.64 = (f32[1024,32]{0,1:T(8,128)}, f32[1024,32]{0,1:T(8,128)}, u32[]{:S(2)}, u32[]{:S(2)}) collective-permute-start(f32[1024,32]{0,1:T(8,128)} %get-tuple-element.372), channel_id=1, source_target_pairs={{0,2},{1,3},{4,6},{5,7},{8,10},{9,11},{12,14},{13,15},{16,18},{17,... | collective-permute-start | bytes 393224 | tf_op jit(solution)/shard_map/ppermute | solution.py:32
  289.7 3.4 place_block_3.1
  297.4 3.4 place_block_4.1
  300.8 3.3 collective-permute-done.61
  304.2 5.6 %collective-permute-done.60 = bf16[64,4096]{1,0:T(8,128)(2,1)} collective-permute-done((bf16[64,4096]{1,0:T(8,128)(2,1)S(1)}, bf16[64,4096]{1,0:T(8,128)(2,1)}, u32[]{:S(2)}, u32[]{:S(2)}) %collective-permute-start.60) | collective-permute-done | bytes 524320 | tf_op jit(solution)/shard_map/ppermute | solution.py:1037
  311.7 1.5 collective-permute-start.65
  313.2 3.4 place_block_5.1
  317.3 1.9 broadcast_select_fusion.3
  323.6 2.0 collective-permute-start.68
  327.2 3.4 place_block_6.1
  331.5 3.0 spare_totals.1
  336.9 3.4 place_block_7.1
  342.6 1.6 place_extra.1
  (276 shorter events, 83.4 us)
Async XLA Ops:
  2.8 16.3 %collective-permute-start.7 = (bf16[3,1024,1024]{2,1,0:T(8,128)(2,1)}, bf16[3,1024,1024]{2,1,0:T(8,128)(2,1)}, u32[]{:S(2)}, u32[]{:S(2)}) collective-permute-start(bf16[3,1024,1024]{2,1,0:T(8,128)(2,1)} %w0.3), channel_id=1, source_target_pairs={{0,1},{1,0},{2,3},{3,2},{4,5},{5,4},{6,7},{7,6},{8,9},{9,8},{10,11... | collective-permute-start | bytes 18874376 | tf_op jit(solution)/shard_map/ppermute | solution.py:26
  3.2 15.9 %collective-permute-start.8 = (bf16[3,1024,512]{2,1,0:T(8,128)(2,1)}, bf16[3,1024,512]{2,1,0:T(8,128)(2,1)}, u32[]{:S(2)}, u32[]{:S(2)}) collective-permute-start(bf16[3,1024,512]{2,1,0:T(8,128)(2,1)} %w2.3), channel_id=1, source_target_pairs={{0,1},{1,0},{2,3},{3,2},{4,5},{5,4},{6,7},{7,6},{8,9},{9,8},{10,11... | collective-permute-start | bytes 9437192 | tf_op jit(solution)/shard_map/ppermute | solution.py:26
  8.0 4.1 %collective-permute-start.4 = (f32[2,4,512]{2,1,0:T(4,128)}, f32[2,4,512]{2,1,0:T(4,128)S(1)}, u32[]{:S(2)}, u32[]{:S(2)}) collective-permute-start(f32[2,4,512]{2,1,0:T(4,128)} %get-tuple-element.216), channel_id=1, source_target_pairs={{0,8},{4,12},{8,0},{12,4},{16,24},{20,28},{24,16},{28,20},{1,9},{5... | collective-permute-start | bytes 49160 | tf_op jit(solution)/shard_map/ppermute | solution.py:36
  12.7 3.7 %collective-permute-start.5 = (f32[2,4,512]{2,1,0:T(4,128)S(1)}, f32[2,4,512]{2,1,0:T(4,128)S(1)}, u32[]{:S(2)}, u32[]{:S(2)}) collective-permute-start(f32[2,4,512]{2,1,0:T(4,128)S(1)} %pad_maximum_fusion.3), channel_id=1, source_target_pairs={{0,16},{4,20},{8,24},{12,28},{16,0},{20,4},{24,8},{28,12},{1,17},{... | collective-permute-start | bytes 49160 | tf_op jit(solution)/shard_map/ppermute | solution.py:36
  16.4 2.7 collective-permute-start.6
  34.4 2.9 collective-permute-start.10
  35.8 9.8 %collective-permute-start.9 = (bf16[512,512]{1,0:T(8,128)(2,1)}, bf16[512,512]{1,0:T(8,128)(2,1)S(1)}, u32[]{:S(2)}, u32[]{:S(2)}) collective-permute-start(bf16[512,512]{1,0:T(8,128)(2,1)} %get-tuple-element.223.hb), channel_id=1, source_target_pairs={{0,2},{1,3},{4,6},{5,7},{8,10},{9,11},{12,14},{13,15},{16,18},{17,... | collective-permute-start | bytes 1572872 | tf_op jit(solution)/shard_map/ppermute | solution.py:32
  38.0 3.6 %collective-permute-start.11 = (f32[2,4,512]{2,1,0:T(4,128)S(1)}, f32[2,4,512]{2,1,0:T(4,128)S(1)}, u32[]{:S(2)}, u32[]{:S(2)}) collective-permute-start(f32[2,4,512]{2,1,0:T(4,128)S(1)} %pad_maximum_fusion.5), channel_id=1, source_target_pairs={{0,16},{4,20},{8,24},{12,28},{16,0},{20,4},{24,8},{28,12},{1,17},{... | collective-permute-start | bytes 49160 | tf_op jit(solution)/shard_map/ppermute | solution.py:36
  41.5 4.0 %collective-permute-start.12 = (f32[2,4,512]{2,1,0:T(4,128)S(1)}, f32[2,4,512]{2,1,0:T(4,128)S(1)}, u32[]{:S(2)}, u32[]{:S(2)}) collective-permute-start(f32[2,4,512]{2,1,0:T(4,128)S(1)} %pad_maximum_fusion.6), channel_id=1, source_target_pairs={{0,2},{1,3},{4,6},{5,7},{8,10},{9,11},{12,14},{13,15},{16,18},{17,... | collective-permute-start | bytes 49160 | tf_op jit(solution)/shard_map/ppermute | solution.py:32
  42.8 2.7 collective-permute-start.13
  44.2 28.4 %collective-permute-start.15 = (f32[2,4,512]{2,1,0:T(4,128)S(1)}, f32[2,4,512]{2,1,0:T(4,128)S(1)}, u32[]{:S(2)}, u32[]{:S(2)}) collective-permute-start(f32[2,4,512]{2,1,0:T(4,128)S(1)} %pad_maximum_fusion.6), channel_id=1, source_target_pairs={{0,4},{4,0},{8,12},{12,8},{16,20},{20,16},{24,28},{28,24},{1,5},{5... | collective-permute-start | bytes 49160 | tf_op jit(solution)/shard_map/ppermute | solution.py:36
  49.9 20.2 %collective-permute-start.16 = (f32[2,4,512]{2,1,0:T(4,128)}, f32[2,4,512]{2,1,0:T(4,128)S(1)}, u32[]{:S(2)}, u32[]{:S(2)}) collective-permute-start(f32[2,4,512]{2,1,0:T(4,128)} %get-tuple-element.277), channel_id=1, source_target_pairs={{0,8},{4,12},{8,0},{12,4},{16,24},{20,28},{24,16},{28,20},{1,9},{5... | collective-permute-start | bytes 49160 | tf_op jit(solution)/shard_map/ppermute | solution.py:36
  51.3 38.1 %collective-permute-start.14 = (bf16[512,512]{1,0:T(8,128)(2,1)}, bf16[512,512]{1,0:T(8,128)(2,1)S(1)}, u32[]{:S(2)}, u32[]{:S(2)}) collective-permute-start(bf16[512,512]{1,0:T(8,128)(2,1)} %get-tuple-element.225), channel_id=1, source_target_pairs={{2,0},{3,1},{6,4},{7,5},{10,8},{11,9},{14,12},{15,13},{18,16},{19,... | collective-permute-start | bytes 1572872 | tf_op jit(solution)/shard_map/ppermute | solution.py:32
  70.1 3.6 %collective-permute-start.17 = (f32[2,4,512]{2,1,0:T(4,128)S(1)}, f32[2,4,512]{2,1,0:T(4,128)S(1)}, u32[]{:S(2)}, u32[]{:S(2)}) collective-permute-start(f32[2,4,512]{2,1,0:T(4,128)S(1)} %add.340), channel_id=1, source_target_pairs={{0,16},{4,20},{8,24},{12,28},{16,0},{20,4},{24,8},{28,12},{1,17},{... | collective-permute-start | bytes 49160 | tf_op jit(solution)/shard_map/ppermute | solution.py:36
  73.8 14.3 %collective-permute-start.18 = (f32[2,4,512]{2,1,0:T(4,128)S(1)}, f32[2,4,512]{2,1,0:T(4,128)S(1)}, u32[]{:S(2)}, u32[]{:S(2)}) collective-permute-start(f32[2,4,512]{2,1,0:T(4,128)S(1)} %add.341), channel_id=1, source_target_pairs={{2,0},{3,1},{6,4},{7,5},{10,8},{11,9},{14,12},{15,13},{18,16},{19,... | collective-permute-start | bytes 49160 | tf_op jit(solution)/shard_map/ppermute | solution.py:32
  75.1 14.3 %collective-permute-start.19 = (f32[2,4,512]{2,1,0:T(4,128)S(1)}, f32[2,4,512]{2,1,0:T(4,128)S(1)}, u32[]{:S(2)}, u32[]{:S(2)}) collective-permute-start(f32[2,4,512]{2,1,0:T(4,128)S(1)} %add.341), channel_id=1, source_target_pairs={{2,4},{3,5},{6,0},{7,1},{10,12},{11,13},{14,8},{15,9},{18,20},{19,... | collective-permute-start | bytes 49160 | tf_op jit(solution)/shard_map/ppermute | solution.py:69
  130.0 10.3 %collective-permute-start.21 = (bf16[64,4096]{1,0:T(8,128)(2,1)S(1)}, bf16[64,4096]{1,0:T(8,128)(2,1)S(1)}, u32[]{:S(2)}, u32[]{:S(2)}) collective-permute-start(bf16[64,4096]{1,0:T(8,128)(2,1)S(1)} %constant_dynamic-slice_fusion), channel_id=1, source_target_pairs={{0,1},{1,0},{2,3},{3,2},{4,5},{5,4},{6,7},{7,6},{8,9},{9,8},{10,11... | collective-permute-start | bytes 1572872 | tf_op jit(solution)/shard_map/ppermute | solution.py:26
  141.8 15.7 %collective-permute-start.22 = (bf16[512,4096]{1,0:T(8,128)(2,1)}, bf16[512,4096]{1,0:T(8,128)(2,1)}, u32[]{:S(2)}, u32[]{:S(2)}) collective-permute-start(bf16[512,4096]{1,0:T(8,128)(2,1)} %get-tuple-element.239), channel_id=1, source_target_pairs={{0,1},{1,0},{2,3},{3,2},{4,5},{5,4},{6,7},{7,6},{8,9},{9,8},{10,11... | collective-permute-start | bytes 12582920 | tf_op jit(solution)/shard_map/ppermute | solution.py:26
  142.0 18.6 %collective-permute-start.32 = (bf16[512,4096]{1,0:T(8,128)(2,1)}, bf16[512,4096]{1,0:T(8,128)(2,1)}, u32[]{:S(2)}, u32[]{:S(2)}) collective-permute-start(bf16[512,4096]{1,0:T(8,128)(2,1)} %get-tuple-element.270), channel_id=1, source_target_pairs={{0,1},{1,0},{2,3},{3,2},{4,5},{5,4},{6,7},{7,6},{8,9},{9,8},{10,11... | collective-permute-start | bytes 12582920 | tf_op jit(solution)/shard_map/ppermute | solution.py:26
  143.5 13.4 %collective-permute-start.23 = (bf16[64,4096]{1,0:T(8,128)(2,1)S(1)}, bf16[64,4096]{1,0:T(8,128)(2,1)S(1)}, u32[]{:S(2)}, u32[]{:S(2)}) collective-permute-start(bf16[64,4096]{1,0:T(8,128)(2,1)S(1)} %add_convert_fusion.15), channel_id=1, source_target_pairs={{0,8},{8,16},{16,24},{24,28},{28,20},{20,12},{12,4},{4,0},{5,13},{... | collective-permute-start | bytes 1572872 | tf_op jit(solution)/shard_map/ppermute | solution.py:1037
  146.0 11.5 %collective-permute-start.33 = (bf16[64,4096]{1,0:T(8,128)(2,1)S(1)}, bf16[64,4096]{1,0:T(8,128)(2,1)S(1)}, u32[]{:S(2)}, u32[]{:S(2)}) collective-permute-start(bf16[64,4096]{1,0:T(8,128)(2,1)S(1)} %add_convert_fusion.14), channel_id=1, source_target_pairs={{0,8},{8,16},{16,24},{24,28},{28,20},{20,12},{12,4},{4,0},{5,13},{... | collective-permute-start | bytes 1572872 | tf_op jit(solution)/shard_map/ppermute | solution.py:1037
  146.8 10.2 %collective-permute-start.24 = (f32[2,4,512]{2,1,0:T(4,128)S(1)}, f32[2,4,512]{2,1,0:T(4,128)S(1)}, u32[]{:S(2)}, u32[]{:S(2)}) collective-permute-start(f32[2,4,512]{2,1,0:T(4,128)S(1)} %copy-done.30), channel_id=1, source_target_pairs={{0,4},{4,0},{8,12},{12,8},{16,20},{20,16},{24,28},{28,24},{1,5},{5... | collective-permute-start | bytes 49160 | tf_op jit(solution)/shard_map/ppermute | solution.py:36
  158.9 8.6 %collective-permute-start.25 = (bf16[64,4096]{1,0:T(8,128)(2,1)S(1)}, bf16[64,4096]{1,0:T(8,128)(2,1)S(1)}, u32[]{:S(2)}, u32[]{:S(2)}) collective-permute-start(bf16[64,4096]{1,0:T(8,128)(2,1)S(1)} %add_convert_fusion.13), channel_id=1, source_target_pairs={{0,8},{8,16},{16,24},{24,28},{28,20},{20,12},{12,4},{4,0},{5,13},{... | collective-permute-start | bytes 1572872 | tf_op jit(solution)/shard_map/ppermute | solution.py:1037
  162.3 3.6 %collective-permute-start.35 = (f32[4,2048]{1,0:T(4,128)S(1)}, f32[4,2048]{1,0:T(4,128)S(1)}, u32[]{:S(2)}, u32[]{:S(2)}) collective-permute-start(f32[4,2048]{1,0:T(4,128)S(1)} %pad_maximum_fusion), channel_id=1, source_target_pairs={{0,1},{1,0},{2,3},{3,2},{4,5},{5,4},{6,7},{7,6},{8,9},{9,8},{10,11... | collective-permute-start | bytes 98312 | tf_op jit(solution)/shard_map/ppermute | solution.py:26
  163.4 4.1 %collective-permute-start.26 = (f32[2,4,512]{2,1,0:T(4,128)S(1)}, f32[2,4,512]{2,1,0:T(4,128)S(1)}, u32[]{:S(2)}, u32[]{:S(2)}) collective-permute-start(f32[2,4,512]{2,1,0:T(4,128)S(1)} %add.370), channel_id=1, source_target_pairs={{0,8},{4,12},{8,0},{12,4},{16,24},{20,28},{24,16},{28,20},{1,9},{5... | collective-permute-start | bytes 49160 | tf_op jit(solution)/shard_map/ppermute | solution.py:36
  165.4 8.9 %collective-permute-start.34 = (bf16[64,4096]{1,0:T(8,128)(2,1)S(1)}, bf16[64,4096]{1,0:T(8,128)(2,1)S(1)}, u32[]{:S(2)}, u32[]{:S(2)}) collective-permute-start(bf16[64,4096]{1,0:T(8,128)(2,1)S(1)} %add_convert_fusion.8), channel_id=1, source_target_pairs={{0,8},{8,16},{16,24},{24,28},{28,20},{20,12},{12,4},{4,0},{5,13},{... | collective-permute-start | bytes 1572872 | tf_op jit(solution)/shard_map/ppermute | solution.py:1037
  168.9 11.8 %collective-permute-start.27 = (bf16[64,4096]{1,0:T(8,128)(2,1)S(1)}, bf16[64,4096]{1,0:T(8,128)(2,1)S(1)}, u32[]{:S(2)}, u32[]{:S(2)}) collective-permute-start(bf16[64,4096]{1,0:T(8,128)(2,1)S(1)} %add_convert_fusion.12), channel_id=1, source_target_pairs={{0,8},{8,16},{16,24},{24,28},{28,20},{20,12},{12,4},{4,0},{5,13},{... | collective-permute-start | bytes 1572872 | tf_op jit(solution)/shard_map/ppermute | solution.py:1037
  170.4 10.3 %collective-permute-start.28 = (f32[2,4,512]{2,1,0:T(4,128)S(1)}, f32[2,4,512]{2,1,0:T(4,128)S(1)}, u32[]{:S(2)}, u32[]{:S(2)}) collective-permute-start(f32[2,4,512]{2,1,0:T(4,128)S(1)} %add.372), channel_id=1, source_target_pairs={{0,16},{4,20},{8,24},{12,28},{16,0},{20,4},{24,8},{28,12},{1,17},{... | collective-permute-start | bytes 49160 | tf_op jit(solution)/shard_map/ppermute | solution.py:36
  175.8 10.2 %collective-permute-start.40 = (bf16[64,4096]{1,0:T(8,128)(2,1)S(1)}, bf16[64,4096]{1,0:T(8,128)(2,1)S(1)}, u32[]{:S(2)}, u32[]{:S(2)}) collective-permute-start(bf16[64,4096]{1,0:T(8,128)(2,1)S(1)} %add_convert_fusion.5), channel_id=1, source_target_pairs={{0,8},{8,16},{16,24},{24,28},{28,20},{20,12},{12,4},{4,0},{5,13},{... | collective-permute-start | bytes 1572872 | tf_op jit(solution)/shard_map/ppermute | solution.py:1037
  182.7 9.7 %collective-permute-start.29 = (bf16[64,4096]{1,0:T(8,128)(2,1)S(1)}, bf16[64,4096]{1,0:T(8,128)(2,1)}, u32[]{:S(2)}, u32[]{:S(2)}) collective-permute-start(bf16[64,4096]{1,0:T(8,128)(2,1)S(1)} %add_convert_fusion.11), channel_id=1, source_target_pairs={{0,8},{8,16},{16,24},{24,28},{28,20},{20,12},{12,4},{4,0},{5,13},{... | collective-permute-start | bytes 1572872 | tf_op jit(solution)/shard_map/ppermute | solution.py:1037
  187.3 13.1 %collective-permute-start.41 = (bf16[64,4096]{1,0:T(8,128)(2,1)S(1)}, bf16[64,4096]{1,0:T(8,128)(2,1)S(1)}, u32[]{:S(2)}, u32[]{:S(2)}) collective-permute-start(bf16[64,4096]{1,0:T(8,128)(2,1)S(1)} %add_convert_fusion.4), channel_id=1, source_target_pairs={{0,8},{8,16},{16,24},{24,28},{28,20},{20,12},{12,4},{4,0},{5,13},{... | collective-permute-start | bytes 1572872 | tf_op jit(solution)/shard_map/ppermute | solution.py:1037
  194.0 10.3 %collective-permute-start.30 = (bf16[64,4096]{1,0:T(8,128)(2,1)S(1)}, bf16[64,4096]{1,0:T(8,128)(2,1)}, u32[]{:S(2)}, u32[]{:S(2)}) collective-permute-start(bf16[64,4096]{1,0:T(8,128)(2,1)S(1)} %add_convert_fusion.10), channel_id=1, source_target_pairs={{0,8},{8,16},{16,24},{24,28},{28,20},{20,12},{12,4},{4,0},{5,13},{... | collective-permute-start | bytes 1572872 | tf_op jit(solution)/shard_map/ppermute | solution.py:1037
  194.9 9.3 %collective-permute-start.31 = (bf16[16,4096]{1,0:T(8,128)(2,1)}, bf16[16,4096]{1,0:T(8,128)(2,1)S(1)}, u32[]{:S(2)}, u32[]{:S(2)}) collective-permute-start(bf16[16,4096]{1,0:T(8,128)(2,1)} %get-tuple-element.266), channel_id=1, source_target_pairs={{0,1},{1,0},{2,3},{3,2},{4,5},{5,4},{6,7},{7,6},{8,9},{9,8},{10,11... | collective-permute-start | bytes 393224 | tf_op jit(solution)/shard_map/ppermute | solution.py:26
  201.8 8.8 %collective-permute-start.42 = (bf16[64,4096]{1,0:T(8,128)(2,1)S(1)}, bf16[64,4096]{1,0:T(8,128)(2,1)S(1)}, u32[]{:S(2)}, u32[]{:S(2)}) collective-permute-start(bf16[64,4096]{1,0:T(8,128)(2,1)S(1)} %add_convert_fusion.3), channel_id=1, source_target_pairs={{0,8},{8,16},{16,24},{24,28},{28,20},{20,12},{12,4},{4,0},{5,13},{... | collective-permute-start | bytes 1572872 | tf_op jit(solution)/shard_map/ppermute | solution.py:1037
  203.6 37.8 %collective-permute-start.55 = (f32[512,2,32]{0,2,1:T(8,128)}, f32[512,2,32]{0,2,1:T(8,128)}, u32[]{:S(2)}, u32[]{:S(2)}) collective-permute-start(f32[512,2,32]{0,2,1:T(8,128)} %select_bitcast_fusion.1), channel_id=1, source_target_pairs={{0,1},{1,0},{2,3},{3,2},{4,5},{5,4},{6,7},{7,6},{8,9},{9,8},{10,11... | collective-permute-start | bytes 393224 | tf_op jit(solution)/shard_map/ppermute | solution.py:26
  207.5 10.3 %collective-permute-start.36 = (bf16[64,4096]{1,0:T(8,128)(2,1)S(1)}, bf16[64,4096]{1,0:T(8,128)(2,1)}, u32[]{:S(2)}, u32[]{:S(2)}) collective-permute-start(bf16[64,4096]{1,0:T(8,128)(2,1)S(1)} %add_convert_fusion.9), channel_id=1, source_target_pairs={{0,8},{8,16},{16,24},{24,28},{28,20},{20,12},{12,4},{4,0},{5,13},{... | collective-permute-start | bytes 1572872 | tf_op jit(solution)/shard_map/ppermute | solution.py:1037
  208.6 9.1 %collective-permute-start.37 = (bf16[16,4096]{1,0:T(8,128)(2,1)S(1)}, bf16[16,4096]{1,0:T(8,128)(2,1)}, u32[]{:S(2)}, u32[]{:S(2)}) collective-permute-start(bf16[16,4096]{1,0:T(8,128)(2,1)S(1)} %reduce-precision_convert_fusion), channel_id=1, source_target_pairs={{0,2},{1,3},{4,6},{5,7},{8,10},{9,11},{12,14},{13,15},{16,18},{17,... | collective-permute-start | bytes 393224 | tf_op jit(solution)/shard_map/ppermute | solution.py:32
  210.6 7.1 %collective-permute-start.38 = (f32[1,2048]{1,0:T(1,128)S(1)}, f32[1,2048]{1,0:T(1,128)S(1)}, u32[]{:S(2)}, u32[]{:S(2)}) collective-permute-start(f32[1,2048]{1,0:T(1,128)S(1)} %slice.127), channel_id=1, source_target_pairs={{0,2},{1,3},{2,0},{3,1},{4,6},{5,7},{6,4},{7,5},{8,10},{9,11},{10,... | collective-permute-start | bytes 24584 | tf_op jit(solution)/shard_map/ppermute | solution.py:1130
  213.6 5.7 %collective-permute-start.44 = (f32[512,2,128]{2,1,0:T(2,128)S(1)}, f32[512,2,128]{2,1,0:T(2,128)S(1)}, u32[]{:S(2)}, u32[]{:S(2)}) collective-permute-start(f32[512,2,128]{2,1,0:T(2,128)S(1)} %bitcast.62), channel_id=1, source_target_pairs={{0,1},{1,0},{2,3},{3,2},{4,5},{5,4},{6,7},{7,6},{8,9},{9,8},{10,11... | collective-permute-start | bytes 1572872 | tf_op jit(solution)/shard_map/ppermute | solution.py:26
  217.7 8.4 %collective-permute-start.43 = (bf16[64,4096]{1,0:T(8,128)(2,1)S(1)}, bf16[64,4096]{1,0:T(8,128)(2,1)S(1)}, u32[]{:S(2)}, u32[]{:S(2)}) collective-permute-start(bf16[64,4096]{1,0:T(8,128)(2,1)S(1)} %add_convert_fusion.2), channel_id=1, source_target_pairs={{0,8},{8,16},{16,24},{24,28},{28,20},{20,12},{12,4},{4,0},{5,13},{... | collective-permute-start | bytes 1572872 | tf_op jit(solution)/shard_map/ppermute | solution.py:1037
  219.3 12.4 %collective-permute-start.39 = (bf16[64,4096]{1,0:T(8,128)(2,1)S(1)}, bf16[64,4096]{1,0:T(8,128)(2,1)S(1)}, u32[]{:S(2)}, u32[]{:S(2)}) collective-permute-start(bf16[64,4096]{1,0:T(8,128)(2,1)S(1)} %add_convert_fusion.7), channel_id=1, source_target_pairs={{0,8},{8,16},{16,24},{24,28},{28,20},{20,12},{12,4},{4,0},{5,13},{... | collective-permute-start | bytes 1572872 | tf_op jit(solution)/shard_map/ppermute | solution.py:1037
  227.4 9.8 %collective-permute-start.45 = (bf16[64,4096]{1,0:T(8,128)(2,1)S(1)}, bf16[64,4096]{1,0:T(8,128)(2,1)S(1)}, u32[]{:S(2)}, u32[]{:S(2)}) collective-permute-start(bf16[64,4096]{1,0:T(8,128)(2,1)S(1)} %add_convert_fusion.1), channel_id=1, source_target_pairs={{0,8},{8,16},{16,24},{24,28},{28,20},{20,12},{12,4},{4,0},{5,13},{... | collective-permute-start | bytes 1572872 | tf_op jit(solution)/shard_map/ppermute | solution.py:1037
  239.5 9.9 %collective-permute-start.48 = (bf16[80,4096]{1,0:T(8,128)(2,1)S(1)}, bf16[80,4096]{1,0:T(8,128)(2,1)}, u32[]{:S(2)}, u32[]{:S(2)}) collective-permute-start(bf16[80,4096]{1,0:T(8,128)(2,1)S(1)} %maximum_maximum_fusion.refs_0_), channel_id=1, source_target_pairs={{0,8},{8,16},{16,24},{24,28},{28,20},{20,12},{12,4},{4,0},{5,13},{... | collective-permute-start | bytes 1966088 | tf_op jit(solution)/shard_map/ppermute | solution.py:1037
  239.6 4.0 %collective-permute-start.46 = (bf16[64,4096]{1,0:T(8,128)(2,1)S(1)}, bf16[64,4096]{1,0:T(8,128)(2,1)S(1)}, u32[]{:S(2)}, u32[]{:S(2)}) collective-permute-start(bf16[64,4096]{1,0:T(8,128)(2,1)S(1)} %broadcast_select_fusion.2), channel_id=1, source_target_pairs={{0,1},{1,0},{2,3},{3,2},{4,5},{5,4},{6,7},{7,6},{8,9},{9,8},{10,11... | collective-permute-start | bytes 1572872 | tf_op jit(solution)/shard_map/ppermute | solution.py:26
  243.6 11.3 %collective-permute-start.47 = (bf16[64,4096]{1,0:T(8,128)(2,1)S(1)}, bf16[64,4096]{1,0:T(8,128)(2,1)S(1)}, u32[]{:S(2)}, u32[]{:S(2)}) collective-permute-start(bf16[64,4096]{1,0:T(8,128)(2,1)S(1)} %collective-permute-done.46.refs_1_), channel_id=1, source_target_pairs={{0,8},{8,16},{16,24},{24,28},{28,20},{20,12},{12,4},{4,0},{5,13},{... | collective-permute-start | bytes 1572872 | tf_op jit(solution)/shard_map/ppermute | solution.py:1037
  250.5 12.8 %collective-permute-start.51 = (bf16[80,4096]{1,0:T(8,128)(2,1)S(1)}, bf16[80,4096]{1,0:T(8,128)(2,1)}, u32[]{:S(2)}, u32[]{:S(2)}) collective-permute-start(bf16[80,4096]{1,0:T(8,128)(2,1)S(1)} %broadcast_multiply_fusion.5.refs_0_.refs_1_), channel_id=1, source_target_pairs={{0,8},{8,16},{16,24},{24,28},{28,20},{20,12},{12,4},{4,0},{5,13},{... | collective-permute-start | bytes 1966088 | tf_op jit(solution)/shard_map/ppermute | solution.py:1037
  254.9 3.1 collective-permute-start.49
  258.6 9.0 %collective-permute-start.50 = (bf16[64,4096]{1,0:T(8,128)(2,1)S(1)}, bf16[64,4096]{1,0:T(8,128)(2,1)S(1)}, u32[]{:S(2)}, u32[]{:S(2)}) collective-permute-start(bf16[64,4096]{1,0:T(8,128)(2,1)S(1)} %broadcast_multiply_fusion.11.refs_1_), channel_id=1, source_target_pairs={{0,8},{8,16},{16,24},{24,28},{28,20},{20,12},{12,4},{4,0},{5,13},{... | collective-permute-start | bytes 1572872 | tf_op jit(solution)/shard_map/ppermute | solution.py:1037
  258.6 53.0 %collective-permute-start.63 = (f32[1024,128]{1,0:T(8,128)}, f32[1024,128]{1,0:T(8,128)}, u32[]{:S(2)}, u32[]{:S(2)}) collective-permute-start(f32[1024,128]{1,0:T(8,128)} %get-tuple-element.371), channel_id=1, source_target_pairs={{2,0},{3,1},{6,4},{7,5},{10,8},{11,9},{14,12},{15,13},{18,16},{19,... | collective-permute-start | bytes 1572872 | tf_op jit(solution)/shard_map/ppermute | solution.py:32
  264.5 10.1 %collective-permute-start.54 = (bf16[80,4096]{1,0:T(8,128)(2,1)S(1)}, bf16[80,4096]{1,0:T(8,128)(2,1)}, u32[]{:S(2)}, u32[]{:S(2)}) collective-permute-start(bf16[80,4096]{1,0:T(8,128)(2,1)S(1)} %broadcast_multiply_fusion.4.refs_0_.refs_2_), channel_id=1, source_target_pairs={{0,8},{8,16},{16,24},{24,28},{28,20},{20,12},{12,4},{4,0},{5,13},{... | collective-permute-start | bytes 1966088 | tf_op jit(solution)/shard_map/ppermute | solution.py:1037
  267.6 3.1 collective-permute-start.52
  270.7 9.4 %collective-permute-start.53 = (bf16[64,4096]{1,0:T(8,128)(2,1)S(1)}, bf16[64,4096]{1,0:T(8,128)(2,1)S(1)}, u32[]{:S(2)}, u32[]{:S(2)}) collective-permute-start(bf16[64,4096]{1,0:T(8,128)(2,1)S(1)} %broadcast_multiply_fusion.10.refs_1_), channel_id=1, source_target_pairs={{0,8},{8,16},{16,24},{24,28},{28,20},{20,12},{12,4},{4,0},{5,13},{... | collective-permute-start | bytes 1572872 | tf_op jit(solution)/shard_map/ppermute | solution.py:1037
  275.8 17.4 %collective-permute-start.58 = (bf16[80,4096]{1,0:T(8,128)(2,1)S(1)}, bf16[80,4096]{1,0:T(8,128)(2,1)}, u32[]{:S(2)}, u32[]{:S(2)}) collective-permute-start(bf16[80,4096]{1,0:T(8,128)(2,1)S(1)} %broadcast_multiply_fusion.3.refs_0_.refs_3_), channel_id=1, source_target_pairs={{0,8},{8,16},{16,24},{24,28},{28,20},{20,12},{12,4},{4,0},{5,13},{... | collective-permute-start | bytes 1966088 | tf_op jit(solution)/shard_map/ppermute | solution.py:1037
  280.2 3.1 collective-permute-start.56
  283.3 11.0 %collective-permute-start.57 = (bf16[64,4096]{1,0:T(8,128)(2,1)S(1)}, bf16[64,4096]{1,0:T(8,128)(2,1)}, u32[]{:S(2)}, u32[]{:S(2)}) collective-permute-start(bf16[64,4096]{1,0:T(8,128)(2,1)S(1)} %broadcast_multiply_fusion.9.refs_1_), channel_id=1, source_target_pairs={{0,8},{8,16},{16,24},{24,28},{28,20},{20,12},{12,4},{4,0},{5,13},{... | collective-permute-start | bytes 1572872 | tf_op jit(solution)/shard_map/ppermute | solution.py:1037
  284.1 27.6 %collective-permute-start.64 = (f32[1024,32]{0,1:T(8,128)}, f32[1024,32]{0,1:T(8,128)}, u32[]{:S(2)}, u32[]{:S(2)}) collective-permute-start(f32[1024,32]{0,1:T(8,128)} %get-tuple-element.372), channel_id=1, source_target_pairs={{0,2},{1,3},{4,6},{5,7},{8,10},{9,11},{12,14},{13,15},{16,18},{17,... | collective-permute-start | bytes 393224 | tf_op jit(solution)/shard_map/ppermute | solution.py:32
  294.3 9.8 %collective-permute-start.61 = (bf16[80,4096]{1,0:T(8,128)(2,1)S(1)}, bf16[80,4096]{1,0:T(8,128)(2,1)S(1)}, u32[]{:S(2)}, u32[]{:S(2)}) collective-permute-start(bf16[80,4096]{1,0:T(8,128)(2,1)S(1)} %broadcast_multiply_fusion.2.refs_0_.refs_4_), channel_id=1, source_target_pairs={{0,8},{8,16},{16,24},{24,28},{28,20},{20,12},{12,4},{4,0},{5,13},{... | collective-permute-start | bytes 1966088 | tf_op jit(solution)/shard_map/ppermute | solution.py:1037
  296.8 13.0 %collective-permute-start.60 = (bf16[64,4096]{1,0:T(8,128)(2,1)S(1)}, bf16[64,4096]{1,0:T(8,128)(2,1)}, u32[]{:S(2)}, u32[]{:S(2)}) collective-permute-start(bf16[64,4096]{1,0:T(8,128)(2,1)S(1)} %broadcast_multiply_fusion.8.refs_1_), channel_id=1, source_target_pairs={{0,8},{8,16},{16,24},{24,28},{28,20},{20,12},{12,4},{4,0},{5,13},{... | collective-permute-start | bytes 1572872 | tf_op jit(solution)/shard_map/ppermute | solution.py:1037
  304.1 15.1 %collective-permute-start.66 = (bf16[80,4096]{1,0:T(8,128)(2,1)S(1)}, bf16[80,4096]{1,0:T(8,128)(2,1)}, u32[]{:S(2)}, u32[]{:S(2)}) collective-permute-start(bf16[80,4096]{1,0:T(8,128)(2,1)S(1)} %broadcast_multiply_fusion.1.refs_0_.refs_5_), channel_id=1, source_target_pairs={{0,8},{8,16},{16,24},{24,28},{28,20},{20,12},{12,4},{4,0},{5,13},{... | collective-permute-start | bytes 1966088 | tf_op jit(solution)/shard_map/ppermute | solution.py:1037
  311.7 10.7 %collective-permute-start.65 = (bf16[64,4096]{1,0:T(8,128)(2,1)S(1)}, bf16[64,4096]{1,0:T(8,128)(2,1)}, u32[]{:S(2)}, u32[]{:S(2)}) collective-permute-start(bf16[64,4096]{1,0:T(8,128)(2,1)S(1)} %broadcast_multiply_fusion.7.refs_1_), channel_id=1, source_target_pairs={{0,8},{8,16},{16,24},{24,28},{28,20},{20,12},{12,4},{4,0},{5,13},{... | collective-permute-start | bytes 1572872 | tf_op jit(solution)/shard_map/ppermute | solution.py:1037
  320.3 10.3 %collective-permute-start.67 = (bf16[80,4096]{1,0:T(8,128)(2,1)S(1)}, bf16[80,4096]{1,0:T(8,128)(2,1)S(1)}, u32[]{:S(2)}, u32[]{:S(2)}) collective-permute-start(bf16[80,4096]{1,0:T(8,128)(2,1)S(1)} %broadcast_multiply_fusion.refs_0_.refs_6_), channel_id=1, source_target_pairs={{0,8},{8,16},{16,24},{24,28},{28,20},{20,12},{12,4},{4,0},{5,13},{... | collective-permute-start | bytes 1966088 | tf_op jit(solution)/shard_map/ppermute | solution.py:1037
  323.5 12.3 %collective-permute-start.70 = (bf16[64,4096]{1,0:T(8,128)(2,1)S(1)}, bf16[64,4096]{1,0:T(8,128)(2,1)}, u32[]{:S(2)}, u32[]{:S(2)}) collective-permute-start(bf16[64,4096]{1,0:T(8,128)(2,1)S(1)} %broadcast_multiply_fusion.6.refs_1_), channel_id=1, source_target_pairs={{0,8},{8,16},{16,24},{24,28},{28,20},{20,12},{12,4},{4,0},{5,13},{... | collective-permute-start | bytes 1572872 | tf_op jit(solution)/shard_map/ppermute | solution.py:1037
  323.6 3.0 collective-permute-start.68
  334.5 6.4 %collective-permute-start.69 = (f32[12,4096]{1,0:T(8,128)}, f32[12,4096]{1,0:T(8,128)S(1)}, u32[]{:S(2)}, u32[]{:S(2)}) collective-permute-start(f32[12,4096]{1,0:T(8,128)} %get-tuple-element.399), channel_id=1, source_target_pairs={{0,1},{1,0},{2,3},{3,2},{4,5},{5,4},{6,7},{7,6},{8,9},{9,8},{10,11... | collective-permute-start | bytes 589832 | tf_op jit(solution)/shard_map/ppermute | solution.py:26
  (56 other events, 313.2 us)
where the time goes:
time: 351 us; the launch traced here: 344 us
  Pallas kernels  115 us (33%)
  waiting for transfers between devices  86.7 us (25%)
  starting transfers between devices  84.2 us (24%)
  other arithmetic  42.4 us (12%)
  local copies, waits for them, and re-layouts  13.8 us (4%)
    ppermute x28, waiting for transfers between devices, step(): got = lax.ppermute(held, ('dp', 'pipe'), self.pairs)  45.8 us
    pallas_call x1, Pallas kernels, layer1_backward(): pl.pallas_call(kernel, out_shape=(jax.ShapeDtypeStruct((rows, width), F32...  38.6 us
    ppermute x24, starting transfers between devices, core_swap(): lax.ppermute(value, 'pipe', [(i, i ^ 1) for i in range(lax.axis_size('pip...  33.5 us
    pallas_call x2, Pallas kernels, layer1_forward(): pl.pallas_call(kernel, out_shape=out_shape, in_specs=[VM] * len(args) + [...  32.2 us
    pallas_call x8, Pallas kernels, place_block(): pl.pallas_call(kernel, out_shape=(jax.ShapeDtypeStruct(gate.shape, F32),...  27.4 us
    ppermute x11, waiting for transfers between devices, dp_swap(): lax.ppermute(value, 'dp', [(i, i ^ step) for i in range(lax.axis_size('dp...  20.6 us
    ppermute x11, starting transfers between devices, dp_swap(): lax.ppermute(value, 'dp', [(i, i ^ step) for i in range(lax.axis_size('dp...  20.6 us
    convert_element_type x12, other arithmetic, step(): got = (self.block(self.spot - self.done) + got.astype(F32)).astype(BF)  17.2 us
  transfers between devices with their start and end apart: 73, of which 39 were waited for; matrix products, arithmetic and copies ran while one was open for 14% of the time, Pallas kernels for 18%

commit v1 on v0

--- a/solution.py
+++ b/solution.py
@@ -328,11 +328,11 @@
 
 
 class Terms:
-    def __init__(self, count, a, b, grads, made, sems, arrays, after=None):
-        self.first_core = lax.axis_index("pipe") % 2 == 0
-        self.count, self.a, self.b, self.grads, self.made, self.sems = count, a, b, grads, made, sems
+    def __init__(self, count, operands, grads, made, sems, arrays, after=None):
+        self.hidden = 1 - lax.axis_index("pipe") % 2
+        self.count, self.operands, self.grads, self.made, self.sems = count, operands, grads, made, sems
         self.arrays, self.after = arrays, after
-        self.width = a.shape[-1]
+        self.width = operands.shape[-1] // 3
 
     def slot(self, k):
         return (self.count - 1 - k) % 2
@@ -365,70 +365,62 @@
 
     def stage(self, k, at, operands):
         m, *others = operands()
-        if not others:
-            self.a[0, at, :] = m
-            return
-        for i, upper in enumerate((~self.first_core, self.first_core)):
-            self.a[i, at, :] = jnp.where(upper, others[0], m)
-            self.b[i, at, :] = jnp.where(upper, others[1], m)
-
-    def __call__(self, k, source=0, a=None, b=None, grads=None):
         w = self.width
-        a, b = (self.a, self.b) if a is None else (a, b)
+        self.operands[0, at, w : 2 * w] = m
+        if others:
+            self.operands[0, at, :w] = others[0]
+            self.operands[0, at, 2 * w :] = others[1]
+
+    def __call__(self, k, operands=None, grads=None):
+        w = self.width
+        operands = self.operands.at[0] if operands is None else operands
         grads = self.grads.at[k % 2] if grads is None else grads
         self.each(k, lambda k: self.wait(k + 2))
-        for i in range(2):
-            self.made[self.slot(k), i, :, : 2 * w] = tn(a[i], grads[:, : 2 * w]).astype(BF)
-            self.made[self.slot(k), i, :, 2 * w :] = tn(b[i], grads[:, 2 * w :]).astype(BF)
+        made = self.made.at[self.slot(k)]
+        made[self.hidden, :, : 2 * w] = tn(operands[:, :w], grads[:, : 2 * w]).astype(BF)
+        made[self.hidden, :, 2 * w :] = tn(operands[:, 2 * w :], grads[:, 2 * w :]).astype(BF)
+        made[1 - self.hidden] = tn(operands[:, w : 2 * w], grads[...]).astype(BF)
         self.each(k, self.start)
         if self.after:
             self.after(k)
 
-    def first(self, a=None, grads=None):
+    def first(self, operands=None, grads=None):
         w = self.width
-        a = self.a if a is None else a
+        operands = self.operands.at[0] if operands is None else operands
         grads = self.grads.at[0] if grads is None else grads
         self.wait(2)
-        for i, upper in enumerate((~self.first_core, self.first_core)):
-            at = pl.multiple_of(jnp.where(upper, 0, w), w)
-            self.made[self.slot(0), i, :, :w] = tn(a[0], grads[:, pl.ds(at, w)]).astype(BF)
+        made = self.made.at[self.slot(0)]
+        made[self.hidden, :, :w] = tn(operands[:, w : 2 * w], grads[:, :w]).astype(BF)
+        made[1 - self.hidden, :, :w] = tn(operands[:, w : 2 * w], grads[:, w : 2 * w]).astype(BF)
         self.start(0)
         self.wait(1)
         self.wait(0)
 
 
-def terms_from_hbm(terms, operands, grads, buffers, sems):
-    a, b, g = buffers
+def terms_from_hbm(terms, operands_in, grads_in, sems):
     count = terms.count
-    width = terms.width
 
     def copies(k):
         slot = k % 2
-        pieces = []
-        if k == 0:
-            pieces = [(operands.at[0, :, pl.ds(width, width)], a.at[2 * slot])]
-        else:
-            for j, upper in enumerate((~terms.first_core, terms.first_core)):
-                at_a = pl.multiple_of(jnp.where(upper, 0, width), width)
-                at_b = pl.multiple_of(jnp.where(upper, 2 * width, width), width)
-                pieces += [(operands.at[k, :, pl.ds(at_a, width)], a.at[2 * slot + j]),
-                           (operands.at[k, :, pl.ds(at_b, width)], b.at[2 * slot + j])]
-        pieces.append((grads.at[k], g.at[slot]))
-        return [pltpu.make_async_copy(x, y, sems.at[slot, j]) for j, (x, y) in enumerate(pieces)]
+        return [pltpu.make_async_copy(x.at[k], y.at[slot], sems.at[slot, j])
+                for j, (x, y) in enumerate(((operands_in, terms.operands), (grads_in, terms.grads)))]
 
     for copy in copies(count - 1):
         copy.start()
-    for k in range(count - 1, -1, -1):
-        slot = k % 2
-        if k:
-            for copy in copies(k - 1):
-                copy.start()
+
+    def segment(i, _):
+        k = count - 1 - i
+        for copy in copies(k - 1):
+            copy.start()
         for copy in copies(k):
             copy.wait()
-        if k:
-            terms(k, a=a.at[pl.ds(2 * slot, 2)], b=b.at[pl.ds(2 * slot, 2)], grads=g.at[slot])
-        else:
-            terms.first(a=a.at[pl.ds(2 * slot, 2)], grads=g.at[slot])
+        terms(k, terms.operands.at[k % 2], terms.grads.at[k % 2])
+        return 0
+
+    lax.fori_loop(0, count - 1, segment, 0)
+    for copy in copies(0):
+        copy.wait()
+    terms.first()
 
 
 def norm_sums(gx, xhat_of, sums):
@@ -623,7 +615,7 @@
     def kernel(gxr, hb, moments2, total_a, total_b, source, moments, affine, scales, w0, w1, w2, w3,
                kept_h, kept_z, kept_r, kept_c, operands_in, grads_in,
                gx, nsums, sums, sent_a, sent_b, mine_a, mine_b,
-               x, gate, cand, wsems, h, z, r, c, ksems, g, loaded, a, b, lsems, made, msems):
+               x, gate, cand, wsems, h, z, r, c, ksems, g, loaded, staged, lsems, made, msems):
         held = Weights((w0, w1, w2, w3), (gate, cand, wsems))
         states = ((kept_h, h), (kept_z, z), (kept_r, r), (kept_c, c))
 
@@ -646,12 +638,12 @@
             def _():
                 load(k - slots)
 
-        terms = Terms(count, a, b, loaded, made, msems, ((sent_a, sent_b), (mine_a, mine_b)), after)
+        terms = Terms(count, staged, loaded, made, msems, ((sent_a, sent_b), (mine_a, mine_b)), after)
 
         @pl.when(when_active(1))
         def _():
             terms.after = None
-            terms_from_hbm(terms, operands_in, grads_in, (a, b, loaded), lsems)
+            terms_from_hbm(terms, operands_in, grads_in, lsems)
 
         @pl.when(when_active(0))
         def _():
@@ -691,8 +683,8 @@
                         pltpu.SemaphoreType.DMA((4, slots)),
                         pltpu.VMEM((rows, width), F32),
                         pltpu.VMEM((2, rows, 3 * width), BF),
-                        pltpu.VMEM((4, rows, width), BF), pltpu.VMEM((4, rows, width), BF),
-                        pltpu.SemaphoreType.DMA((2, 5)),
+                        pltpu.VMEM((2, rows, 3 * width), BF),
+                        pltpu.SemaphoreType.DMA((2, 2)),
                         pltpu.VMEM((2, 2, width, 3 * width), BF),
                         pltpu.SemaphoreType.DMA((2, 2, 2))],
         compiler_params=pltpu.CompilerParams(vmem_limit_bytes=LIMIT),
@@ -1142,12 +1134,11 @@
 
     totals1 = nsums1
     used = columns // 2
-    chain = [("sum", level) for level in levels_of_dp] + [("features",), ("cores",), ("layers",)]
+    chain = [("",)] + [("sum", level) for level in levels_of_dp] + [("features",), ("cores",), ("layers",)]
     while lower.done < places - 1:
         act = chain.pop(0) if chain else ("",)
         if act[0] == "sum":
-            got, *_ = upper.step(((functools.partial(dp_swap, step=act[1]), totals1),),
-                                 ends=None if lower.done else (lambda held: held, (lower.held,)))
+            got, = upper.step(((functools.partial(dp_swap, step=act[1]), totals1),))
             totals1 = totals1 + got
         elif act[0] == "features":
             numeric_back, table_sent, table = upper.step(work=(features, (gx1, totals1 / counted)))
@@ -1160,7 +1151,7 @@
             low_part = jnp.concatenate([small[:half], small[half:] + got_sums]) - high
             table = jnp.concatenate([pick(got, table)[:used], jnp.concatenate([high, low_part], 1).astype(BF)])
         else:
-            upper.step()
+            upper.step(ends=None if lower.done else (lambda held: held, (lower.held,)))
         if lower.done == 1:
             small, = lower.step(work=(small_sums, (sums1, sums2, nsums1, nsums2)))
         elif lower.done == 5:

time: 351 us -> 342 us (0.974)
  waiting for transfers between devices: 86.7 us -> 75.9 us
  starting transfers between devices: 84.2 us -> 94.6 us
  Pallas kernels: 115 us -> 106 us
    ppermute x28, starting transfers between devices: 13.4 us -> 30.5 us  [step(): got = lax.ppermute(held, ('dp', 'pipe'), self.pairs)]
    pallas_call x1, Pallas kernels: 38.6 us -> 29.6 us  [layer1_backward(): pl.pallas_call(kernel, out_shape=(jax.ShapeDtypeStruct((rows, width), F32...]
    ppermute x11, waiting for transfers between devices: 20.6 us -> 14.5 us  [dp_swap(): lax.ppermute(value, 'dp', [(i, i ^ step) for i in range(lax.axis_size('dp...]
    ppermute x28, waiting for transfers between devices: 45.8 us -> 40.5 us  [step(): got = lax.ppermute(held, ('dp', 'pipe'), self.pairs)]
    unnamed x96 -> x94, local copies, waits for them, and re-layouts: 7.35 us -> 7.41 us
  transfers between devices with their start and end apart: 73 -> 73, of which waited for: 39 -> 42; matrix products, arithmetic and copies ran while one was open for 14% -> 14% of each run, Pallas kernels for 18% -> 18%
where the time goes in v1:
time: 342 us; the launch traced here: 335 us
  Pallas kernels  106 us (31%)
  starting transfers between devices  94.6 us (28%)
  waiting for transfers between devices  75.9 us (22%)
  other arithmetic  43.6 us (13%)
  local copies, waits for them, and re-layouts  12.9 us (4%)
    ppermute x28, waiting for transfers between devices, step(): got = lax.ppermute(held, ('dp', 'pipe'), self.pairs)  40.5 us
    pallas_call x2, Pallas kernels, layer1_forward(): pl.pallas_call(kernel, out_shape=out_shape, in_specs=[VM] * len(args) + [...  32.2 us
    ppermute x24, starting transfers between devices, core_swap(): lax.ppermute(value, 'pipe', [(i, i ^ 1) for i in range(lax.axis_size('pip...  30.8 us
    ppermute x28, starting transfers between devices, step(): got = lax.ppermute(held, ('dp', 'pipe'), self.pairs)  30.5 us
    pallas_call x1, Pallas kernels, layer1_backward(): pl.pallas_call(kernel, out_shape=(jax.ShapeDtypeStruct((rows, width), F32...  29.6 us
    pallas_call x8, Pallas kernels, place_block(): pl.pallas_call(kernel, out_shape=(jax.ShapeDtypeStruct(gate.shape, F32),...  27.5 us
    convert_element_type x12, other arithmetic, step(): got = (self.block(self.spot - self.done) + got.astype(F32)).astype(BF)  18.8 us
    ppermute x11, starting transfers between devices, dp_swap(): lax.ppermute(value, 'dp', [(i, i ^ step) for i in range(lax.axis_size('dp...  17.6 us
  transfers between devices with their start and end apart: 73, of which 42 were waited for; matrix products, arithmetic and copies ran while one was open for 14% of the time, Pallas kernels for 18%

profile of v1, /device:TPU:1, one launch (start us, length us, event | category | flops | bytes accessed | tf_op | source)
XLA Modules:
  0.0 335.2 jit_solution(1951853949008619775)
XLA Ops:
  3.4 4.6 %embed.1 = (f32[512,512]{1,0:T(8,128)}, f32[2,4,512]{2,1,0:T(4,128)}, f32[6,512]{1,0:T(8,128)}, f32[6,1024]{1,0:T(8,128)}, f32[6,512]{1,0:T(8,128)}, /*index=5*/f32[2,2,512]{2,1,0:T(2,128)}) custom-call(f32[1024,128]{1,0:T(8,128)} %numeric.1, s32[24,1024]{1,0:T(8,128)} %bitcast.65, bf16[384,256]{1,0:T(8,128)(2,1)} %bitcast.67, f32[3,512]{1,0:T(4,128)} %logits.1, ...), custom_call_target="tpu_custom_call" | custom-call | flops 536870912 | bytes 2097152 | tf_op jit(solution)/shard_map/embed/pallas_call | solution.py:752
  8.0 2.7 collective-permute-start.4
  12.7 2.5 collective-permute-start.5
  19.7 14.6 %layer1_forward.1 = (bf16[512,512]{1,0:T(8,128)(2,1)}, f32[2,4,512]{2,1,0:T(4,128)}, f32[2,4,512]{2,1,0:T(4,128)}) custom-call(f32[512,512]{1,0:T(8,128)} %get-tuple-element.229.refs_0_.source, f32[2,4,512]{2,1,0:T(4,128)} %copy-done.30, f32[2,4,512]{2,1,0:T(4,128)} %copy-done.41, f32[2,2,512]{2,1,0:T(2,128)} %get-tuple-element.218.refs_3_.affine.refs_2_, ...), custom_call_target="tpu_custom_call" | custom-call | flops 9663676416 | bytes 44040192 | tf_op jit(solution)/shard_map/layer1_forward/pallas_call | solution.py:508
  34.4 1.4 collective-permute-start.10
  38.0 2.4 collective-permute-start.11
  46.9 2.6 layer2_both.1
  52.3 17.5 %layer1_states.1 = (f32[6,512,512]{2,1,0:T(8,128)}, f32[6,512,512]{2,1,0:T(8,128)}, f32[6,512,512]{2,1,0:T(8,128)}, f32[6,512,512]{2,1,0:T(8,128)}) custom-call(f32[512,512]{1,0:T(8,128)} %get-tuple-element.229.refs_0_.source, f32[2,4,512]{2,1,0:T(4,128)} %get-tuple-element.230.refs_1_.moments, f32[2,2,512]{2,1,0:T(2,128)} %get-tuple-element.218.refs_3_.affine.refs_2_, ...), custom_call_target="tpu_custom_call" | custom-call | flops 9663676416 | bytes 44040192 | tf_op jit(solution)/shard_map/layer1_states/pallas_call | solution.py:508
  69.8 2.4 collective-permute-start.17
  76.7 11.1 %collective-permute-done.18.total_a = f32[2,4,512]{2,1,0:T(4,128)S(1)} collective-permute-done((f32[2,4,512]{2,1,0:T(4,128)S(1)}, f32[2,4,512]{2,1,0:T(4,128)S(1)}, u32[]{:S(2)}, u32[]{:S(2)}) %collective-permute-start.18) | collective-permute-done | bytes 16416 | tf_op jit(solution)/shard_map/ppermute | solution.py:32
  89.9 29.6 %layer1_backward.1 = (f32[512,512]{1,0:T(8,128)}, f32[2,4,512]{2,1,0:T(4,128)}, f32[6,2048]{1,0:T(8,128)}, bf16[512,4096]{1,0:T(8,128)(2,1)}, bf16[512,4096]{1,0...) custom-call(bf16[512,512]{1,0:T(8,128)(2,1)} %copy-done.33, ...), custom_call_target="tpu_custom_call" | custom-call | flops 19327352832 | bytes 44040192 | tf_op jit(solution)/shard_map/layer1_backward/pallas_call | solution.py:671
  120.6 8.8 %collective-permute-start.21 = (bf16[64,4096]{1,0:T(8,128)(2,1)S(1)}, bf16[64,4096]{1,0:T(8,128)(2,1)S(1)}, u32[]{:S(2)}, u32[]{:S(2)}) collective-permute-start(bf16[64,4096]{1,0:T(8,128)(2,1)S(1)} %constant_dynamic-slice_fusion), channel_id=1, source_target_pairs={{0,1},{1,0},{2,3},{3,2},{4,5},{5,4},{6,7},{7,6},{8,9},{9,8},{10,11... | collective-permute-start | bytes 1572872 | tf_op jit(solution)/shard_map/ppermute | solution.py:26
  130.9 1.6 collective-permute-done.20
  134.2 1.5 collective-permute-start.23
  137.6 5.1 %collective-permute-done.23 = bf16[64,4096]{1,0:T(8,128)(2,1)S(1)} collective-permute-done((bf16[64,4096]{1,0:T(8,128)(2,1)S(1)}, bf16[64,4096]{1,0:T(8,128)(2,1)S(1)}, u32[]{:S(2)}, u32[]{:S(2)}) %collective-permute-start.23) | collective-permute-done | bytes 524320 | tf_op jit(solution)/shard_map/ppermute | solution.py:1029
  142.7 5.6 %collective-permute-done.34 = bf16[64,4096]{1,0:T(8,128)(2,1)S(1)} collective-permute-done((bf16[64,4096]{1,0:T(8,128)(2,1)S(1)}, bf16[64,4096]{1,0:T(8,128)(2,1)S(1)}, u32[]{:S(2)}, u32[]{:S(2)}) %collective-permute-start.34) | collective-permute-done | bytes 524320 | tf_op jit(solution)/shard_map/ppermute | solution.py:1029
  148.3 1.4 add_convert_fusion.13
  151.0 1.4 add_convert_fusion.7
  155.7 1.6 collective-permute-done.25
  159.5 1.5 collective-permute-start.26
  161.0 2.7 collective-permute-done.35
  165.1 1.7 collective-permute-start.40
  166.8 2.9 collective-permute-done.27
  169.7 1.4 add_convert_fusion.11
  173.6 1.7 collective-permute-done.40
  178.0 3.8 %collective-permute-done.29 = f32[2,4,512]{2,1,0:T(4,128)S(1)} collective-permute-done((f32[2,4,512]{2,1,0:T(4,128)S(1)}, f32[2,4,512]{2,1,0:T(4,128)S(1)}, u32[]{:S(2)}, u32[]{:S(2)}) %collective-permute-start.29) | collective-permute-done | bytes 16416 | tf_op jit(solution)/shard_map/ppermute | solution.py:36
  181.8 2.2 add_convert_fusion.10
  185.0 1.9 collective-permute-done.41
  189.2 5.0 %feature_grads.1 = (f32[512,128]{1,0:T(8,128)}, bf16[16,4096]{1,0:T(8,128)(2,1)}, bf16[16,4096]{1,0:T(8,128)(2,1)}) custom-call(f32[512,512]{1,0:T(8,128)} %get-tuple-element.260.gx, f32[512,512]{1,0:T(8,128)} %get-tuple-element.229.refs_0_.source, f32[2,4,512]{2,1,0:T(4,128)} %get-tuple-element.230.refs_1_.moments, f32[2,4,512]{2,1,0:T(4,128)} %add_multiply_fusion.totals, ...), custom_call_target="tpu_custom_call" | custom-call | flops 536870912 | bytes 4194304 | tf_op jit(solution)/shard_map/feature_grads/pallas_call | solution.py:807
  194.3 2.4 add_convert_fusion.9
  198.0 3.6 %collective-permute-start.32 = (bf16[16,4096]{1,0:T(8,128)(2,1)}, bf16[16,4096]{1,0:T(8,128)(2,1)}, u32[]{:S(2)}, u32[]{:S(2)}) collective-permute-start(bf16[16,4096]{1,0:T(8,128)(2,1)} %get-tuple-element.268), channel_id=1, source_target_pairs={{0,1},{1,0},{2,3},{3,2},{4,5},{5,4},{6,7},{7,6},{8,9},{9,8},{10,11... | collective-permute-start | bytes 393224 | tf_op jit(solution)/shard_map/ppermute | solution.py:26
  201.6 1.5 add_convert_fusion.2
  203.9 1.8 fusion.13
  206.7 1.7 collective-permute-start.43
  209.0 1.6 add_convert_fusion.8
  213.8 1.9 maximum_select_fusion
  215.8 1.4 add_convert_fusion.1
  218.2 2.4 collective-permute-done.37
  220.7 5.5 %collective-permute-done.45 = bf16[64,4096]{1,0:T(8,128)(2,1)S(1)} collective-permute-done((bf16[64,4096]{1,0:T(8,128)(2,1)S(1)}, bf16[64,4096]{1,0:T(8,128)(2,1)S(1)}, u32[]{:S(2)}, u32[]{:S(2)}) %collective-permute-start.45) | collective-permute-done | bytes 524320 | tf_op jit(solution)/shard_map/ppermute | solution.py:1029
  226.3 2.0 broadcast_select_fusion.1
  228.4 1.8 collective-permute-start.48
  230.2 1.6 collective-permute-start.46
  234.2 3.6 %place_block_0.1 = (f32[3,1024,1024]{2,1,0:T(8,128)}, f32[3,1024,512]{2,1,0:T(8,128)}, bf16[128,512]{1,0:T(8,128)(2,1)}) custom-call(bf16[80,4096]{1,0:T(8,128)(2,1)} %copy-done, bf16[64,4096]{1,0:T(8,128)(2,1)} %copy-done.16, f32[3,1024,1024]{2,1,0:T(8,128)} %get-tuple-element.301.refs_2_, ...), custom_call_target="tpu_custom_call", output_to_operand_aliasing={{0}: (2, {}), {1}: (3, {})} | custom-call | tf_op jit(solution)/shard_map/place_block_0/pallas_call | solution.py:943
  239.4 1.8 collective-permute-start.51
  241.2 2.6 collective-permute-done.47
  243.8 2.3 collective-permute-start.49
  250.4 3.4 %place_block_1.1 = (f32[3,1024,1024]{2,1,0:T(8,128)}, f32[3,1024,512]{2,1,0:T(8,128)}, bf16[128,512]{1,0:T(8,128)(2,1)}) custom-call(bf16[80,4096]{1,0:T(8,128)(2,1)} %copy-done.1, bf16[64,4096]{1,0:T(8,128)(2,1)} %copy-done.11, bf16[128,512]{1,0:T(8,128)(2,1)} %copy-done.22, ...), custom_call_target="tpu_custom_call", output_to_operand_aliasing={{0}: (3, {}), {1}: (4, {})} | custom-call | tf_op jit(solution)/shard_map/place_block_1/pallas_call | solution.py:943
  256.5 2.2 collective-permute-start.52
  261.2 3.4 %place_block_2.1 = (f32[3,1024,1024]{2,1,0:T(8,128)}, f32[3,1024,512]{2,1,0:T(8,128)}, bf16[128,512]{1,0:T(8,128)(2,1)}) custom-call(bf16[80,4096]{1,0:T(8,128)(2,1)} %copy-done.2, bf16[64,4096]{1,0:T(8,128)(2,1)} %copy-done.12, bf16[128,512]{1,0:T(8,128)(2,1)} %collective-permute-done.52.refs_2_, ...), custom_call_target="tpu_custom_call", output_to_operand_aliasing={{0}: (3, {}), {1}: (4, {})} | custom-call | tf_op jit(solution)/shard_map/place_block_2/pallas_call | solution.py:943
  267.0 3.4 %collective-permute-done.53 = bf16[64,4096]{1,0:T(8,128)(2,1)S(1)} collective-permute-done((bf16[64,4096]{1,0:T(8,128)(2,1)S(1)}, bf16[64,4096]{1,0:T(8,128)(2,1)S(1)}, u32[]{:S(2)}, u32[]{:S(2)}) %collective-permute-start.53) | collective-permute-done | bytes 524320 | tf_op jit(solution)/shard_map/ppermute | solution.py:1029
  270.4 1.8 collective-permute-start.56
  273.8 5.3 %collective-permute-start.64 = (f32[1024,32]{0,1:T(8,128)}, f32[1024,32]{0,1:T(8,128)}, u32[]{:S(2)}, u32[]{:S(2)}) collective-permute-start(f32[1024,32]{0,1:T(8,128)} %get-tuple-element.374), channel_id=1, source_target_pairs={{0,2},{1,3},{4,6},{5,7},{8,10},{9,11},{12,14},{13,15},{16,18},{17,... | collective-permute-start | bytes 393224 | tf_op jit(solution)/shard_map/ppermute | solution.py:32
  279.1 3.4 %place_block_3.1 = (f32[3,1024,1024]{2,1,0:T(8,128)}, f32[3,1024,512]{2,1,0:T(8,128)}, bf16[128,512]{1,0:T(8,128)(2,1)}) custom-call(bf16[80,4096]{1,0:T(8,128)(2,1)} %copy-done.3, bf16[64,4096]{1,0:T(8,128)(2,1)} %copy-done.10, bf16[128,512]{1,0:T(8,128)(2,1)} %copy-done.20, ...), custom_call_target="tpu_custom_call", output_to_operand_aliasing={{0}: (3, {}), {1}: (4, {})} | custom-call | tf_op jit(solution)/shard_map/place_block_3/pallas_call | solution.py:943
  288.2 3.4 %place_block_4.1 = (f32[3,1024,1024]{2,1,0:T(8,128)}, f32[3,1024,512]{2,1,0:T(8,128)}, bf16[128,512]{1,0:T(8,128)(2,1)}) custom-call(bf16[80,4096]{1,0:T(8,128)(2,1)} %copy-done.4, bf16[64,4096]{1,0:T(8,128)(2,1)} %copy-done.13, bf16[128,512]{1,0:T(8,128)(2,1)} %collective-permute-done.59.refs_2_, ...), custom_call_target="tpu_custom_call", output_to_operand_aliasing={{0}: (3, {}), {1}: (4, {})} | custom-call | tf_op jit(solution)/shard_map/place_block_4/pallas_call | solution.py:943
  291.6 1.9 collective-permute-done.61
  294.7 4.5 %collective-permute-done.60 = bf16[64,4096]{1,0:T(8,128)(2,1)} collective-permute-done((bf16[64,4096]{1,0:T(8,128)(2,1)S(1)}, bf16[64,4096]{1,0:T(8,128)(2,1)}, u32[]{:S(2)}, u32[]{:S(2)}) %collective-permute-start.60) | collective-permute-done | bytes 524320 | tf_op jit(solution)/shard_map/ppermute | solution.py:1029
  299.2 2.2 collective-permute-start.62
  303.6 3.4 %place_block_5.1 = (f32[3,1024,1024]{2,1,0:T(8,128)}, f32[3,1024,512]{2,1,0:T(8,128)}, bf16[128,512]{1,0:T(8,128)(2,1)}) custom-call(bf16[80,4096]{1,0:T(8,128)(2,1)} %copy-done.5, bf16[64,4096]{1,0:T(8,128)(2,1)} %copy-done.9, bf16[128,512]{1,0:T(8,128)(2,1)} %copy-done.19, ...), custom_call_target="tpu_custom_call", output_to_operand_aliasing={{0}: (3, {}), {1}: (4, {})} | custom-call | tf_op jit(solution)/shard_map/place_block_5/pallas_call | solution.py:943
  307.7 1.9 broadcast_select_fusion.3
  314.1 2.1 collective-permute-start.68
  317.9 3.4 %place_block_6.1 = (f32[3,1024,1024]{2,1,0:T(8,128)}, f32[3,1024,512]{2,1,0:T(8,128)}, bf16[128,512]{1,0:T(8,128)(2,1)}) custom-call(bf16[80,4096]{1,0:T(8,128)(2,1)} %copy-done.6, bf16[64,4096]{1,0:T(8,128)(2,1)} %copy-done.8, bf16[128,512]{1,0:T(8,128)(2,1)} %copy-done.24, ...), custom_call_target="tpu_custom_call", output_to_operand_aliasing={{0}: (3, {}), {1}: (4, {})} | custom-call | tf_op jit(solution)/shard_map/place_block_6/pallas_call | solution.py:943
  322.1 3.0 spare_totals.1
  327.6 3.4 %place_block_7.1 = (f32[3,1024,1024]{2,1,0:T(8,128)}, f32[3,1024,512]{2,1,0:T(8,128)}, bf16[128,512]{1,0:T(8,128)(2,1)}) custom-call(bf16[80,4096]{1,0:T(8,128)(2,1)} %copy-done.7, bf16[64,4096]{1,0:T(8,128)(2,1)} %collective-permute-done.70.refs_1_, bf16[128,512]{1,0:T(8,128)(2,1)} %copy-done.23, ...), custom_call_target="tpu_custom_call", output_to_operand_aliasing={{0}: (3, {}), {1}: (4, {})} | custom-call | tf_op jit(solution)/shard_map/place_block_7/pallas_call | solution.py:943
  333.3 1.6 place_extra.1
  (274 shorter events, 96.6 us)
Async XLA Ops:
  2.8 16.3 %collective-permute-start.7 = (bf16[3,1024,1024]{2,1,0:T(8,128)(2,1)}, bf16[3,1024,1024]{2,1,0:T(8,128)(2,1)}, u32[]{:S(2)}, u32[]{:S(2)}) collective-permute-start(bf16[3,1024,1024]{2,1,0:T(8,128)(2,1)} %w0.3), channel_id=1, source_target_pairs={{0,1},{1,0},{2,3},{3,2},{4,5},{5,4},{6,7},{7,6},{8,9},{9,8},{10,11... | collective-permute-start | bytes 18874376 | tf_op jit(solution)/shard_map/ppermute | solution.py:26
  3.2 15.9 %collective-permute-start.8 = (bf16[3,1024,512]{2,1,0:T(8,128)(2,1)}, bf16[3,1024,512]{2,1,0:T(8,128)(2,1)}, u32[]{:S(2)}, u32[]{:S(2)}) collective-permute-start(bf16[3,1024,512]{2,1,0:T(8,128)(2,1)} %w2.3), channel_id=1, source_target_pairs={{0,1},{1,0},{2,3},{3,2},{4,5},{5,4},{6,7},{7,6},{8,9},{9,8},{10,11... | collective-permute-start | bytes 9437192 | tf_op jit(solution)/shard_map/ppermute | solution.py:26
  8.0 4.0 %collective-permute-start.4 = (f32[2,4,512]{2,1,0:T(4,128)}, f32[2,4,512]{2,1,0:T(4,128)S(1)}, u32[]{:S(2)}, u32[]{:S(2)}) collective-permute-start(f32[2,4,512]{2,1,0:T(4,128)} %get-tuple-element.217), channel_id=1, source_target_pairs={{0,8},{4,12},{8,0},{12,4},{16,24},{20,28},{24,16},{28,20},{1,9},{5... | collective-permute-start | bytes 49160 | tf_op jit(solution)/shard_map/ppermute | solution.py:36
  12.7 3.7 %collective-permute-start.5 = (f32[2,4,512]{2,1,0:T(4,128)S(1)}, f32[2,4,512]{2,1,0:T(4,128)S(1)}, u32[]{:S(2)}, u32[]{:S(2)}) collective-permute-start(f32[2,4,512]{2,1,0:T(4,128)S(1)} %pad_maximum_fusion.3), channel_id=1, source_target_pairs={{0,16},{4,20},{8,24},{12,28},{16,0},{20,4},{24,8},{28,12},{1,17},{... | collective-permute-start | bytes 49160 | tf_op jit(solution)/shard_map/ppermute | solution.py:36
  34.4 2.9 collective-permute-start.10
  35.8 9.8 %collective-permute-start.9 = (bf16[512,512]{1,0:T(8,128)(2,1)}, bf16[512,512]{1,0:T(8,128)(2,1)S(1)}, u32[]{:S(2)}, u32[]{:S(2)}) collective-permute-start(bf16[512,512]{1,0:T(8,128)(2,1)} %get-tuple-element.224.hb), channel_id=1, source_target_pairs={{0,2},{1,3},{4,6},{5,7},{8,10},{9,11},{12,14},{13,15},{16,18},{17,... | collective-permute-start | bytes 1572872 | tf_op jit(solution)/shard_map/ppermute | solution.py:32
  38.0 3.6 %collective-permute-start.11 = (f32[2,4,512]{2,1,0:T(4,128)S(1)}, f32[2,4,512]{2,1,0:T(4,128)S(1)}, u32[]{:S(2)}, u32[]{:S(2)}) collective-permute-start(f32[2,4,512]{2,1,0:T(4,128)S(1)} %pad_maximum_fusion.5), channel_id=1, source_target_pairs={{0,16},{4,20},{8,24},{12,28},{16,0},{20,4},{24,8},{28,12},{1,17},{... | collective-permute-start | bytes 49160 | tf_op jit(solution)/shard_map/ppermute | solution.py:36
  41.5 4.0 %collective-permute-start.12 = (f32[2,4,512]{2,1,0:T(4,128)S(1)}, f32[2,4,512]{2,1,0:T(4,128)S(1)}, u32[]{:S(2)}, u32[]{:S(2)}) collective-permute-start(f32[2,4,512]{2,1,0:T(4,128)S(1)} %pad_maximum_fusion.6), channel_id=1, source_target_pairs={{0,2},{1,3},{4,6},{5,7},{8,10},{9,11},{12,14},{13,15},{16,18},{17,... | collective-permute-start | bytes 49160 | tf_op jit(solution)/shard_map/ppermute | solution.py:32
  42.8 2.7 collective-permute-start.13
  44.2 28.1 %collective-permute-start.15 = (f32[2,4,512]{2,1,0:T(4,128)S(1)}, f32[2,4,512]{2,1,0:T(4,128)S(1)}, u32[]{:S(2)}, u32[]{:S(2)}) collective-permute-start(f32[2,4,512]{2,1,0:T(4,128)S(1)} %pad_maximum_fusion.6), channel_id=1, source_target_pairs={{0,4},{4,0},{8,12},{12,8},{16,20},{20,16},{24,28},{28,24},{1,5},{5... | collective-permute-start | bytes 49160 | tf_op jit(solution)/shard_map/ppermute | solution.py:36
  49.6 20.2 %collective-permute-start.16 = (f32[2,4,512]{2,1,0:T(4,128)}, f32[2,4,512]{2,1,0:T(4,128)S(1)}, u32[]{:S(2)}, u32[]{:S(2)}) collective-permute-start(f32[2,4,512]{2,1,0:T(4,128)} %get-tuple-element.279), channel_id=1, source_target_pairs={{0,8},{4,12},{8,0},{12,4},{16,24},{20,28},{24,16},{28,20},{1,9},{5... | collective-permute-start | bytes 49160 | tf_op jit(solution)/shard_map/ppermute | solution.py:36
  51.0 38.1 %collective-permute-start.14 = (bf16[512,512]{1,0:T(8,128)(2,1)}, bf16[512,512]{1,0:T(8,128)(2,1)S(1)}, u32[]{:S(2)}, u32[]{:S(2)}) collective-permute-start(bf16[512,512]{1,0:T(8,128)(2,1)} %get-tuple-element.226), channel_id=1, source_target_pairs={{2,0},{3,1},{6,4},{7,5},{10,8},{11,9},{14,12},{15,13},{18,16},{19,... | collective-permute-start | bytes 1572872 | tf_op jit(solution)/shard_map/ppermute | solution.py:32
  69.8 3.6 %collective-permute-start.17 = (f32[2,4,512]{2,1,0:T(4,128)S(1)}, f32[2,4,512]{2,1,0:T(4,128)S(1)}, u32[]{:S(2)}, u32[]{:S(2)}) collective-permute-start(f32[2,4,512]{2,1,0:T(4,128)S(1)} %add.340), channel_id=1, source_target_pairs={{0,16},{4,20},{8,24},{12,28},{16,0},{20,4},{24,8},{28,12},{1,17},{... | collective-permute-start | bytes 49160 | tf_op jit(solution)/shard_map/ppermute | solution.py:36
  73.5 14.3 %collective-permute-start.18 = (f32[2,4,512]{2,1,0:T(4,128)S(1)}, f32[2,4,512]{2,1,0:T(4,128)S(1)}, u32[]{:S(2)}, u32[]{:S(2)}) collective-permute-start(f32[2,4,512]{2,1,0:T(4,128)S(1)} %add.341), channel_id=1, source_target_pairs={{2,0},{3,1},{6,4},{7,5},{10,8},{11,9},{14,12},{15,13},{18,16},{19,... | collective-permute-start | bytes 49160 | tf_op jit(solution)/shard_map/ppermute | solution.py:32
  74.7 14.3 %collective-permute-start.19 = (f32[2,4,512]{2,1,0:T(4,128)S(1)}, f32[2,4,512]{2,1,0:T(4,128)S(1)}, u32[]{:S(2)}, u32[]{:S(2)}) collective-permute-start(f32[2,4,512]{2,1,0:T(4,128)S(1)} %add.341), channel_id=1, source_target_pairs={{2,4},{3,5},{6,0},{7,1},{10,12},{11,13},{14,8},{15,9},{18,20},{19,... | collective-permute-start | bytes 49160 | tf_op jit(solution)/shard_map/ppermute | solution.py:69
  120.6 10.3 %collective-permute-start.21 = (bf16[64,4096]{1,0:T(8,128)(2,1)S(1)}, bf16[64,4096]{1,0:T(8,128)(2,1)S(1)}, u32[]{:S(2)}, u32[]{:S(2)}) collective-permute-start(bf16[64,4096]{1,0:T(8,128)(2,1)S(1)} %constant_dynamic-slice_fusion), channel_id=1, source_target_pairs={{0,1},{1,0},{2,3},{3,2},{4,5},{5,4},{6,7},{7,6},{8,9},{9,8},{10,11... | collective-permute-start | bytes 1572872 | tf_op jit(solution)/shard_map/ppermute | solution.py:26
  132.5 15.8 %collective-permute-start.22 = (bf16[512,4096]{1,0:T(8,128)(2,1)}, bf16[512,4096]{1,0:T(8,128)(2,1)}, u32[]{:S(2)}, u32[]{:S(2)}) collective-permute-start(bf16[512,4096]{1,0:T(8,128)(2,1)} %get-tuple-element.240), channel_id=1, source_target_pairs={{0,1},{1,0},{2,3},{3,2},{4,5},{5,4},{6,7},{7,6},{8,9},{9,8},{10,11... | collective-permute-start | bytes 12582920 | tf_op jit(solution)/shard_map/ppermute | solution.py:26
  132.6 18.4 %collective-permute-start.33 = (bf16[512,4096]{1,0:T(8,128)(2,1)}, bf16[512,4096]{1,0:T(8,128)(2,1)}, u32[]{:S(2)}, u32[]{:S(2)}) collective-permute-start(bf16[512,4096]{1,0:T(8,128)(2,1)} %get-tuple-element.272), channel_id=1, source_target_pairs={{0,1},{1,0},{2,3},{3,2},{4,5},{5,4},{6,7},{7,6},{8,9},{9,8},{10,11... | collective-permute-start | bytes 12582920 | tf_op jit(solution)/shard_map/ppermute | solution.py:26
  134.2 8.6 %collective-permute-start.23 = (bf16[64,4096]{1,0:T(8,128)(2,1)S(1)}, bf16[64,4096]{1,0:T(8,128)(2,1)S(1)}, u32[]{:S(2)}, u32[]{:S(2)}) collective-permute-start(bf16[64,4096]{1,0:T(8,128)(2,1)S(1)} %add_convert_fusion.15), channel_id=1, source_target_pairs={{0,8},{8,16},{16,24},{24,28},{28,20},{20,12},{12,4},{4,0},{5,13},{... | collective-permute-start | bytes 1572872 | tf_op jit(solution)/shard_map/ppermute | solution.py:1029
  136.8 11.5 %collective-permute-start.34 = (bf16[64,4096]{1,0:T(8,128)(2,1)S(1)}, bf16[64,4096]{1,0:T(8,128)(2,1)S(1)}, u32[]{:S(2)}, u32[]{:S(2)}) collective-permute-start(bf16[64,4096]{1,0:T(8,128)(2,1)S(1)} %add_convert_fusion.14), channel_id=1, source_target_pairs={{0,8},{8,16},{16,24},{24,28},{28,20},{20,12},{12,4},{4,0},{5,13},{... | collective-permute-start | bytes 1572872 | tf_op jit(solution)/shard_map/ppermute | solution.py:1029
  149.7 8.4 %collective-permute-start.24 = (bf16[64,4096]{1,0:T(8,128)(2,1)S(1)}, bf16[64,4096]{1,0:T(8,128)(2,1)S(1)}, u32[]{:S(2)}, u32[]{:S(2)}) collective-permute-start(bf16[64,4096]{1,0:T(8,128)(2,1)S(1)} %add_convert_fusion.13), channel_id=1, source_target_pairs={{0,8},{8,16},{16,24},{24,28},{28,20},{20,12},{12,4},{4,0},{5,13},{... | collective-permute-start | bytes 1572872 | tf_op jit(solution)/shard_map/ppermute | solution.py:1029
  152.7 3.0 collective-permute-start.36
  154.2 3.2 collective-permute-start.25
  155.0 8.7 %collective-permute-start.35 = (bf16[64,4096]{1,0:T(8,128)(2,1)S(1)}, bf16[64,4096]{1,0:T(8,128)(2,1)S(1)}, u32[]{:S(2)}, u32[]{:S(2)}) collective-permute-start(bf16[64,4096]{1,0:T(8,128)(2,1)S(1)} %add_convert_fusion.7), channel_id=1, source_target_pairs={{0,8},{8,16},{16,24},{24,28},{28,20},{20,12},{12,4},{4,0},{5,13},{... | collective-permute-start | bytes 1572872 | tf_op jit(solution)/shard_map/ppermute | solution.py:1029
  159.5 10.2 %collective-permute-start.26 = (bf16[64,4096]{1,0:T(8,128)(2,1)S(1)}, bf16[64,4096]{1,0:T(8,128)(2,1)S(1)}, u32[]{:S(2)}, u32[]{:S(2)}) collective-permute-start(bf16[64,4096]{1,0:T(8,128)(2,1)S(1)} %add_convert_fusion.12), channel_id=1, source_target_pairs={{0,8},{8,16},{16,24},{24,28},{28,20},{20,12},{12,4},{4,0},{5,13},{... | collective-permute-start | bytes 1572872 | tf_op jit(solution)/shard_map/ppermute | solution.py:1029
  161.0 8.7 %collective-permute-start.27 = (f32[2,4,512]{2,1,0:T(4,128)S(1)}, f32[2,4,512]{2,1,0:T(4,128)S(1)}, u32[]{:S(2)}, u32[]{:S(2)}) collective-permute-start(f32[2,4,512]{2,1,0:T(4,128)S(1)} %add.371), channel_id=1, source_target_pairs={{0,8},{4,12},{8,0},{12,4},{16,24},{20,28},{24,16},{28,20},{1,9},{5... | collective-permute-start | bytes 49160 | tf_op jit(solution)/shard_map/ppermute | solution.py:36
  165.1 10.2 %collective-permute-start.40 = (bf16[64,4096]{1,0:T(8,128)(2,1)S(1)}, bf16[64,4096]{1,0:T(8,128)(2,1)S(1)}, u32[]{:S(2)}, u32[]{:S(2)}) collective-permute-start(bf16[64,4096]{1,0:T(8,128)(2,1)S(1)} %add_convert_fusion.5), channel_id=1, source_target_pairs={{0,8},{8,16},{16,24},{24,28},{28,20},{20,12},{12,4},{4,0},{5,13},{... | collective-permute-start | bytes 1572872 | tf_op jit(solution)/shard_map/ppermute | solution.py:1029
  171.1 10.7 %collective-permute-start.28 = (bf16[64,4096]{1,0:T(8,128)(2,1)S(1)}, bf16[64,4096]{1,0:T(8,128)(2,1)S(1)}, u32[]{:S(2)}, u32[]{:S(2)}) collective-permute-start(bf16[64,4096]{1,0:T(8,128)(2,1)S(1)} %add_convert_fusion.11), channel_id=1, source_target_pairs={{0,8},{8,16},{16,24},{24,28},{28,20},{20,12},{12,4},{4,0},{5,13},{... | collective-permute-start | bytes 1572872 | tf_op jit(solution)/shard_map/ppermute | solution.py:1029
  172.4 9.4 %collective-permute-start.29 = (f32[2,4,512]{2,1,0:T(4,128)S(1)}, f32[2,4,512]{2,1,0:T(4,128)S(1)}, u32[]{:S(2)}, u32[]{:S(2)}) collective-permute-start(f32[2,4,512]{2,1,0:T(4,128)S(1)} %add.373), channel_id=1, source_target_pairs={{0,16},{4,20},{8,24},{12,28},{16,0},{20,4},{24,8},{28,12},{1,17},{... | collective-permute-start | bytes 49160 | tf_op jit(solution)/shard_map/ppermute | solution.py:36
  176.7 10.2 %collective-permute-start.41 = (bf16[64,4096]{1,0:T(8,128)(2,1)S(1)}, bf16[64,4096]{1,0:T(8,128)(2,1)S(1)}, u32[]{:S(2)}, u32[]{:S(2)}) collective-permute-start(bf16[64,4096]{1,0:T(8,128)(2,1)S(1)} %add_convert_fusion.4), channel_id=1, source_target_pairs={{0,8},{8,16},{16,24},{24,28},{28,20},{20,12},{12,4},{4,0},{5,13},{... | collective-permute-start | bytes 1572872 | tf_op jit(solution)/shard_map/ppermute | solution.py:1029
  184.6 9.7 %collective-permute-start.30 = (bf16[64,4096]{1,0:T(8,128)(2,1)}, bf16[64,4096]{1,0:T(8,128)(2,1)}, u32[]{:S(2)}, u32[]{:S(2)}) collective-permute-start(bf16[64,4096]{1,0:T(8,128)(2,1)} %add_convert_fusion.10), channel_id=1, source_target_pairs={{0,8},{8,16},{16,24},{24,28},{28,20},{20,12},{12,4},{4,0},{5,13},{... | collective-permute-start | bytes 1572872 | tf_op jit(solution)/shard_map/ppermute | solution.py:1029
  188.3 13.3 %collective-permute-start.42 = (bf16[64,4096]{1,0:T(8,128)(2,1)S(1)}, bf16[64,4096]{1,0:T(8,128)(2,1)}, u32[]{:S(2)}, u32[]{:S(2)}) collective-permute-start(bf16[64,4096]{1,0:T(8,128)(2,1)S(1)} %add_convert_fusion.3), channel_id=1, source_target_pairs={{0,8},{8,16},{16,24},{24,28},{28,20},{20,12},{12,4},{4,0},{5,13},{... | collective-permute-start | bytes 1572872 | tf_op jit(solution)/shard_map/ppermute | solution.py:1029
  196.7 12.3 %collective-permute-start.31 = (bf16[64,4096]{1,0:T(8,128)(2,1)}, bf16[64,4096]{1,0:T(8,128)(2,1)}, u32[]{:S(2)}, u32[]{:S(2)}) collective-permute-start(bf16[64,4096]{1,0:T(8,128)(2,1)} %add_convert_fusion.9), channel_id=1, source_target_pairs={{0,8},{8,16},{16,24},{24,28},{28,20},{20,12},{12,4},{4,0},{5,13},{... | collective-permute-start | bytes 1572872 | tf_op jit(solution)/shard_map/ppermute | solution.py:1029
  198.0 10.9 %collective-permute-start.32 = (bf16[16,4096]{1,0:T(8,128)(2,1)}, bf16[16,4096]{1,0:T(8,128)(2,1)}, u32[]{:S(2)}, u32[]{:S(2)}) collective-permute-start(bf16[16,4096]{1,0:T(8,128)(2,1)} %get-tuple-element.268), channel_id=1, source_target_pairs={{0,1},{1,0},{2,3},{3,2},{4,5},{5,4},{6,7},{7,6},{8,9},{9,8},{10,11... | collective-permute-start | bytes 393224 | tf_op jit(solution)/shard_map/ppermute | solution.py:26
  205.6 8.1 %collective-permute-start.44 = (f32[512,2,128]{2,1,0:T(2,128)}, f32[512,2,128]{2,1,0:T(2,128)}, u32[]{:S(2)}, u32[]{:S(2)}) collective-permute-start(f32[512,2,128]{2,1,0:T(2,128)} %bitcast.7), channel_id=1, source_target_pairs={{0,1},{1,0},{2,3},{3,2},{4,5},{5,4},{6,7},{7,6},{8,9},{9,8},{10,11... | collective-permute-start | bytes 1572872 | tf_op jit(solution)/shard_map/ppermute | solution.py:26
  206.7 9.1 %collective-permute-start.43 = (bf16[64,4096]{1,0:T(8,128)(2,1)S(1)}, bf16[64,4096]{1,0:T(8,128)(2,1)S(1)}, u32[]{:S(2)}, u32[]{:S(2)}) collective-permute-start(bf16[64,4096]{1,0:T(8,128)(2,1)S(1)} %add_convert_fusion.2), channel_id=1, source_target_pairs={{0,8},{8,16},{16,24},{24,28},{28,20},{20,12},{12,4},{4,0},{5,13},{... | collective-permute-start | bytes 1572872 | tf_op jit(solution)/shard_map/ppermute | solution.py:1029
  208.6 23.2 %collective-permute-start.55 = (f32[512,2,32]{0,2,1:T(8,128)S(1)}, f32[512,2,32]{0,2,1:T(8,128)S(1)}, u32[]{:S(2)}, u32[]{:S(2)}) collective-permute-start(f32[512,2,32]{0,2,1:T(8,128)S(1)} %select_bitcast_fusion.1), channel_id=1, source_target_pairs={{0,1},{1,0},{2,3},{3,2},{4,5},{5,4},{6,7},{7,6},{8,9},{9,8},{10,11... | collective-permute-start | bytes 393224 | tf_op jit(solution)/shard_map/ppermute | solution.py:26
  211.5 9.1 %collective-permute-start.37 = (bf16[64,4096]{1,0:T(8,128)(2,1)S(1)}, bf16[64,4096]{1,0:T(8,128)(2,1)S(1)}, u32[]{:S(2)}, u32[]{:S(2)}) collective-permute-start(bf16[64,4096]{1,0:T(8,128)(2,1)S(1)} %add_convert_fusion.8), channel_id=1, source_target_pairs={{0,8},{8,16},{16,24},{24,28},{28,20},{20,12},{12,4},{4,0},{5,13},{... | collective-permute-start | bytes 1572872 | tf_op jit(solution)/shard_map/ppermute | solution.py:1029
  212.4 5.8 %collective-permute-start.38 = (bf16[16,4096]{1,0:T(8,128)(2,1)S(1)}, bf16[16,4096]{1,0:T(8,128)(2,1)S(1)}, u32[]{:S(2)}, u32[]{:S(2)}) collective-permute-start(bf16[16,4096]{1,0:T(8,128)(2,1)S(1)} %reduce-precision_convert_fusion), channel_id=1, source_target_pairs={{0,2},{1,3},{4,6},{5,7},{8,10},{9,11},{12,14},{13,15},{16,18},{17,... | collective-permute-start | bytes 393224 | tf_op jit(solution)/shard_map/ppermute | solution.py:32
  213.7 4.5 %collective-permute-start.39 = (f32[1,2048]{1,0:T(1,128)S(1)}, f32[1,2048]{1,0:T(1,128)S(1)}, u32[]{:S(2)}, u32[]{:S(2)}) collective-permute-start(f32[1,2048]{1,0:T(1,128)S(1)} %slice.127), channel_id=1, source_target_pairs={{0,2},{1,3},{2,0},{3,1},{4,6},{5,7},{6,4},{7,5},{8,10},{9,11},{10,... | collective-permute-start | bytes 24584 | tf_op jit(solution)/shard_map/ppermute | solution.py:1122
  217.2 9.1 %collective-permute-start.45 = (bf16[64,4096]{1,0:T(8,128)(2,1)S(1)}, bf16[64,4096]{1,0:T(8,128)(2,1)S(1)}, u32[]{:S(2)}, u32[]{:S(2)}) collective-permute-start(bf16[64,4096]{1,0:T(8,128)(2,1)S(1)} %add_convert_fusion.1), channel_id=1, source_target_pairs={{0,8},{8,16},{16,24},{24,28},{28,20},{20,12},{12,4},{4,0},{5,13},{... | collective-permute-start | bytes 1572872 | tf_op jit(solution)/shard_map/ppermute | solution.py:1029
  228.4 9.9 %collective-permute-start.48 = (bf16[80,4096]{1,0:T(8,128)(2,1)S(1)}, bf16[80,4096]{1,0:T(8,128)(2,1)}, u32[]{:S(2)}, u32[]{:S(2)}) collective-permute-start(bf16[80,4096]{1,0:T(8,128)(2,1)S(1)} %maximum_maximum_fusion.refs_0_), channel_id=1, source_target_pairs={{0,8},{8,16},{16,24},{24,28},{28,20},{20,12},{12,4},{4,0},{5,13},{... | collective-permute-start | bytes 1966088 | tf_op jit(solution)/shard_map/ppermute | solution.py:1029
  230.2 3.1 collective-permute-start.46
  233.4 10.4 %collective-permute-start.47 = (bf16[64,4096]{1,0:T(8,128)(2,1)S(1)}, bf16[64,4096]{1,0:T(8,128)(2,1)S(1)}, u32[]{:S(2)}, u32[]{:S(2)}) collective-permute-start(bf16[64,4096]{1,0:T(8,128)(2,1)S(1)} %collective-permute-done.46.refs_1_), channel_id=1, source_target_pairs={{0,8},{8,16},{16,24},{24,28},{28,20},{20,12},{12,4},{4,0},{5,13},{... | collective-permute-start | bytes 1572872 | tf_op jit(solution)/shard_map/ppermute | solution.py:1029
  239.4 14.4 %collective-permute-start.51 = (bf16[80,4096]{1,0:T(8,128)(2,1)S(1)}, bf16[80,4096]{1,0:T(8,128)(2,1)}, u32[]{:S(2)}, u32[]{:S(2)}) collective-permute-start(bf16[80,4096]{1,0:T(8,128)(2,1)S(1)} %broadcast_multiply_fusion.5.refs_0_.refs_1_), channel_id=1, source_target_pairs={{0,8},{8,16},{16,24},{24,28},{28,20},{20,12},{12,4},{4,0},{5,13},{... | collective-permute-start | bytes 1966088 | tf_op jit(solution)/shard_map/ppermute | solution.py:1029
  243.8 3.5 %collective-permute-start.49 = (bf16[128,512]{1,0:T(8,128)(2,1)}, bf16[128,512]{1,0:T(8,128)(2,1)S(1)}, u32[]{:S(2)}, u32[]{:S(2)}) collective-permute-start(bf16[128,512]{1,0:T(8,128)(2,1)} %get-tuple-element.308), channel_id=1, source_target_pairs={{0,1},{1,0},{2,3},{3,2},{4,5},{5,4},{6,7},{7,6},{8,9},{9,8},{10,11... | collective-permute-start | bytes 393224 | tf_op jit(solution)/shard_map/ppermute | solution.py:26
  247.9 8.6 %collective-permute-start.50 = (bf16[64,4096]{1,0:T(8,128)(2,1)S(1)}, bf16[64,4096]{1,0:T(8,128)(2,1)S(1)}, u32[]{:S(2)}, u32[]{:S(2)}) collective-permute-start(bf16[64,4096]{1,0:T(8,128)(2,1)S(1)} %broadcast_multiply_fusion.11.refs_1_), channel_id=1, source_target_pairs={{0,8},{8,16},{16,24},{24,28},{28,20},{20,12},{12,4},{4,0},{5,13},{... | collective-permute-start | bytes 1572872 | tf_op jit(solution)/shard_map/ppermute | solution.py:1029
  249.1 53.4 %collective-permute-start.63 = (f32[1024,128]{1,0:T(8,128)}, f32[1024,128]{1,0:T(8,128)}, u32[]{:S(2)}, u32[]{:S(2)}) collective-permute-start(f32[1024,128]{1,0:T(8,128)} %get-tuple-element.373), channel_id=1, source_target_pairs={{2,0},{3,1},{6,4},{7,5},{10,8},{11,9},{14,12},{15,13},{18,16},{19,... | collective-permute-start | bytes 1572872 | tf_op jit(solution)/shard_map/ppermute | solution.py:32
  255.0 9.9 %collective-permute-start.54 = (bf16[80,4096]{1,0:T(8,128)(2,1)S(1)}, bf16[80,4096]{1,0:T(8,128)(2,1)}, u32[]{:S(2)}, u32[]{:S(2)}) collective-permute-start(bf16[80,4096]{1,0:T(8,128)(2,1)S(1)} %broadcast_multiply_fusion.4.refs_0_.refs_2_), channel_id=1, source_target_pairs={{0,8},{8,16},{16,24},{24,28},{28,20},{20,12},{12,4},{4,0},{5,13},{... | collective-permute-start | bytes 1966088 | tf_op jit(solution)/shard_map/ppermute | solution.py:1029
  256.5 3.5 %collective-permute-start.52 = (bf16[128,512]{1,0:T(8,128)(2,1)}, bf16[128,512]{1,0:T(8,128)(2,1)}, u32[]{:S(2)}, u32[]{:S(2)}) collective-permute-start(bf16[128,512]{1,0:T(8,128)(2,1)} %get-tuple-element.323), channel_id=1, source_target_pairs={{0,1},{1,0},{2,3},{3,2},{4,5},{5,4},{6,7},{7,6},{8,9},{9,8},{10,11... | collective-permute-start | bytes 393224 | tf_op jit(solution)/shard_map/ppermute | solution.py:26
  260.0 10.4 %collective-permute-start.53 = (bf16[64,4096]{1,0:T(8,128)(2,1)S(1)}, bf16[64,4096]{1,0:T(8,128)(2,1)S(1)}, u32[]{:S(2)}, u32[]{:S(2)}) collective-permute-start(bf16[64,4096]{1,0:T(8,128)(2,1)S(1)} %broadcast_multiply_fusion.10.refs_1_), channel_id=1, source_target_pairs={{0,8},{8,16},{16,24},{24,28},{28,20},{20,12},{12,4},{4,0},{5,13},{... | collective-permute-start | bytes 1572872 | tf_op jit(solution)/shard_map/ppermute | solution.py:1029
  266.0 16.5 %collective-permute-start.58 = (bf16[80,4096]{1,0:T(8,128)(2,1)S(1)}, bf16[80,4096]{1,0:T(8,128)(2,1)}, u32[]{:S(2)}, u32[]{:S(2)}) collective-permute-start(bf16[80,4096]{1,0:T(8,128)(2,1)S(1)} %broadcast_multiply_fusion.3.refs_0_.refs_3_), channel_id=1, source_target_pairs={{0,8},{8,16},{16,24},{24,28},{28,20},{20,12},{12,4},{4,0},{5,13},{... | collective-permute-start | bytes 1966088 | tf_op jit(solution)/shard_map/ppermute | solution.py:1029
  270.4 3.0 collective-permute-start.56
  273.5 11.4 %collective-permute-start.57 = (bf16[64,4096]{1,0:T(8,128)(2,1)S(1)}, bf16[64,4096]{1,0:T(8,128)(2,1)}, u32[]{:S(2)}, u32[]{:S(2)}) collective-permute-start(bf16[64,4096]{1,0:T(8,128)(2,1)S(1)} %broadcast_multiply_fusion.9.refs_1_), channel_id=1, source_target_pairs={{0,8},{8,16},{16,24},{24,28},{28,20},{20,12},{12,4},{4,0},{5,13},{... | collective-permute-start | bytes 1572872 | tf_op jit(solution)/shard_map/ppermute | solution.py:1029
  273.8 28.7 %collective-permute-start.64 = (f32[1024,32]{0,1:T(8,128)}, f32[1024,32]{0,1:T(8,128)}, u32[]{:S(2)}, u32[]{:S(2)}) collective-permute-start(f32[1024,32]{0,1:T(8,128)} %get-tuple-element.374), channel_id=1, source_target_pairs={{0,2},{1,3},{4,6},{5,7},{8,10},{9,11},{12,14},{13,15},{16,18},{17,... | collective-permute-start | bytes 393224 | tf_op jit(solution)/shard_map/ppermute | solution.py:32
  283.7 9.8 %collective-permute-start.61 = (bf16[80,4096]{1,0:T(8,128)(2,1)S(1)}, bf16[80,4096]{1,0:T(8,128)(2,1)S(1)}, u32[]{:S(2)}, u32[]{:S(2)}) collective-permute-start(bf16[80,4096]{1,0:T(8,128)(2,1)S(1)} %broadcast_multiply_fusion.2.refs_0_.refs_4_), channel_id=1, source_target_pairs={{0,8},{8,16},{16,24},{24,28},{28,20},{20,12},{12,4},{4,0},{5,13},{... | collective-permute-start | bytes 1966088 | tf_op jit(solution)/shard_map/ppermute | solution.py:1029
  287.4 11.8 %collective-permute-start.60 = (bf16[64,4096]{1,0:T(8,128)(2,1)S(1)}, bf16[64,4096]{1,0:T(8,128)(2,1)}, u32[]{:S(2)}, u32[]{:S(2)}) collective-permute-start(bf16[64,4096]{1,0:T(8,128)(2,1)S(1)} %broadcast_multiply_fusion.8.refs_1_), channel_id=1, source_target_pairs={{0,8},{8,16},{16,24},{24,28},{28,20},{20,12},{12,4},{4,0},{5,13},{... | collective-permute-start | bytes 1572872 | tf_op jit(solution)/shard_map/ppermute | solution.py:1029
  293.6 16.0 %collective-permute-start.66 = (bf16[80,4096]{1,0:T(8,128)(2,1)S(1)}, bf16[80,4096]{1,0:T(8,128)(2,1)}, u32[]{:S(2)}, u32[]{:S(2)}) collective-permute-start(bf16[80,4096]{1,0:T(8,128)(2,1)S(1)} %broadcast_multiply_fusion.1.refs_0_.refs_5_), channel_id=1, source_target_pairs={{0,8},{8,16},{16,24},{24,28},{28,20},{20,12},{12,4},{4,0},{5,13},{... | collective-permute-start | bytes 1966088 | tf_op jit(solution)/shard_map/ppermute | solution.py:1029
  299.2 3.4 %collective-permute-start.62 = (bf16[128,512]{1,0:T(8,128)(2,1)}, bf16[128,512]{1,0:T(8,128)(2,1)S(1)}, u32[]{:S(2)}, u32[]{:S(2)}) collective-permute-start(bf16[128,512]{1,0:T(8,128)(2,1)} %get-tuple-element.370), channel_id=1, source_target_pairs={{0,1},{1,0},{2,3},{3,2},{4,5},{5,4},{6,7},{7,6},{8,9},{9,8},{10,11... | collective-permute-start | bytes 393224 | tf_op jit(solution)/shard_map/ppermute | solution.py:26
  302.6 9.2 %collective-permute-start.65 = (bf16[64,4096]{1,0:T(8,128)(2,1)S(1)}, bf16[64,4096]{1,0:T(8,128)(2,1)}, u32[]{:S(2)}, u32[]{:S(2)}) collective-permute-start(bf16[64,4096]{1,0:T(8,128)(2,1)S(1)} %broadcast_multiply_fusion.7.refs_1_), channel_id=1, source_target_pairs={{0,8},{8,16},{16,24},{24,28},{28,20},{20,12},{12,4},{4,0},{5,13},{... | collective-permute-start | bytes 1572872 | tf_op jit(solution)/shard_map/ppermute | solution.py:1029
  310.7 10.6 %collective-permute-start.67 = (bf16[80,4096]{1,0:T(8,128)(2,1)S(1)}, bf16[80,4096]{1,0:T(8,128)(2,1)S(1)}, u32[]{:S(2)}, u32[]{:S(2)}) collective-permute-start(bf16[80,4096]{1,0:T(8,128)(2,1)S(1)} %broadcast_multiply_fusion.refs_0_.refs_6_), channel_id=1, source_target_pairs={{0,8},{8,16},{16,24},{24,28},{28,20},{20,12},{12,4},{4,0},{5,13},{... | collective-permute-start | bytes 1966088 | tf_op jit(solution)/shard_map/ppermute | solution.py:1029
  313.0 13.3 %collective-permute-start.70 = (bf16[64,4096]{1,0:T(8,128)(2,1)S(1)}, bf16[64,4096]{1,0:T(8,128)(2,1)}, u32[]{:S(2)}, u32[]{:S(2)}) collective-permute-start(bf16[64,4096]{1,0:T(8,128)(2,1)S(1)} %broadcast_multiply_fusion.6.refs_1_), channel_id=1, source_target_pairs={{0,8},{8,16},{16,24},{24,28},{28,20},{20,12},{12,4},{4,0},{5,13},{... | collective-permute-start | bytes 1572872 | tf_op jit(solution)/shard_map/ppermute | solution.py:1029
  314.1 3.1 collective-permute-start.68
  325.1 6.4 %collective-permute-start.69 = (f32[12,4096]{1,0:T(8,128)}, f32[12,4096]{1,0:T(8,128)S(1)}, u32[]{:S(2)}, u32[]{:S(2)}) collective-permute-start(f32[12,4096]{1,0:T(8,128)} %get-tuple-element.401), channel_id=1, source_target_pairs={{0,1},{1,0},{2,3},{3,2},{4,5},{5,4},{6,7},{7,6},{8,9},{9,8},{10,11... | collective-permute-start | bytes 589832 | tf_op jit(solution)/shard_map/ppermute | solution.py:26
  (55 other events, 313.2 us)

commit v2 on v1

--- a/solution.py
+++ b/solution.py
@@ -1156,6 +1156,8 @@
             small, = lower.step(work=(small_sums, (sums1, sums2, nsums1, nsums2)))
         elif lower.done == 5:
             block, = lower.step(work=(layer_columns, (h2,)))
+        elif lower.done == 6:
+            numeric_part, = lower.step(work=(layer_columns, (numeric_back,)))
         elif lower.done == 2:
             gate_w, cand_w = lower.step(work=(lambda: blank_outputs(half, width), ()))
         else:
@@ -1184,24 +1186,17 @@
         own.step()
         sends, ends, works = (), None, [(place, values)]
         if s == 1:
-            sends = ((functools.partial(to_layer, up=False), block[:, 0]),)
-        elif s == 2:
-            ends = (layer_columns, (numeric_back,))
-        elif s == 3:
-            sends = ((functools.partial(to_layer, up=True), numeric_part[:, 1]),)
+            sends = ((functools.partial(to_layer, up=False), block[:, 0]),
+                     (functools.partial(to_layer, up=True), numeric_part[:, 1]))
         elif s == 5:
             works.append((lambda a, b, c, d: (pick(a, b), pick(c, d)),
                           (block[:, 1], got_block, got_numeric, numeric_part[:, 0])))
         outs = other.step(sends, works, ends, wait=False)
         if s == 1:
-            got_block = outs.pop(0)
-        elif s == 3:
-            got_numeric = outs.pop(0)
+            got_block, got_numeric, *outs = outs
         gate_w, cand_w, extra, *outs = outs
         extra = core_swap(extra)
-        if s == 2:
-            numeric_part, = outs
-        elif s == 5:
+        if s == 5:
             block_out, numeric_grad = outs
     cand_w = place_extra(places - 1, places, core_swap(extra), cand_w)
     table, gate_b, cand_b, logit, gain, bias = spare_totals(mine, block_rows, used, mask_logits, feature_allow)

time: 342 us -> 342 us (level)
  waiting for transfers between devices: 75.9 us -> 80.5 us
    ppermute x28, waiting for transfers between devices: 40.5 us -> 46 us  [step(): got = lax.ppermute(held, ('dp', 'pipe'), self.pairs)]
    unnamed x94 -> x90, local copies, waits for them, and re-layouts: 7.41 us -> 7.4 us
  transfers between devices with their start and end apart: 73 -> 73, of which waited for: 42 -> 42; matrix products, arithmetic and copies ran while one was open for 14% -> 13% of each run, Pallas kernels for 18% -> 18%
where the time goes in v2:
time: 342 us; the launch traced here: 335 us
  Pallas kernels  106 us (31%)
  starting transfers between devices  93.9 us (27%)
  waiting for transfers between devices  80.5 us (24%)
  other arithmetic  40.2 us (12%)
  local copies, waits for them, and re-layouts  12.9 us (4%)
    ppermute x28, waiting for transfers between devices, step(): got = lax.ppermute(held, ('dp', 'pipe'), self.pairs)  46 us
    pallas_call x2, Pallas kernels, layer1_forward(): pl.pallas_call(kernel, out_shape=out_shape, in_specs=[VM] * len(args) + [...  32.2 us
    ppermute x28, starting transfers between devices, step(): got = lax.ppermute(held, ('dp', 'pipe'), self.pairs)  30.3 us
    pallas_call x1, Pallas kernels, layer1_backward(): pl.pallas_call(kernel, out_shape=(jax.ShapeDtypeStruct((rows, width), F32...  29.7 us
    ppermute x24, starting transfers between devices, core_swap(): lax.ppermute(value, 'pipe', [(i, i ^ 1) for i in range(lax.axis_size('pip...  29.5 us
    pallas_call x8, Pallas kernels, place_block(): pl.pallas_call(kernel, out_shape=(jax.ShapeDtypeStruct(gate.shape, F32),...  27.4 us
    convert_element_type x12, other arithmetic, step(): got = (self.block(self.spot - self.done) + got.astype(F32)).astype(BF)  18.8 us
    ppermute x11, starting transfers between devices, dp_swap(): lax.ppermute(value, 'dp', [(i, i ^ step) for i in range(lax.axis_size('dp...  17.6 us
  transfers between devices with their start and end apart: 73, of which 42 were waited for; matrix products, arithmetic and copies ran while one was open for 13% of the time, Pallas kernels for 18%

profile of v2, /device:TPU:1, one launch (start us, length us, event | category | flops | bytes accessed | tf_op | source)
XLA Modules:
  0.0 335.5 jit_solution(16687735840077301875)
XLA Ops:
  3.4 4.6 %embed.1 = (f32[512,512]{1,0:T(8,128)}, f32[2,4,512]{2,1,0:T(4,128)}, f32[6,512]{1,0:T(8,128)}, f32[6,1024]{1,0:T(8,128)}, f32[6,512]{1,0:T(8,128)}, /*index=5*/f32[2,2,512]{2,1,0:T(2,128)}) custom-call(f32[1024,128]{1,0:T(8,128)} %numeric.1, s32[24,1024]{1,0:T(8,128)} %bitcast.67, bf16[384,256]{1,0:T(8,128)(2,1)} %bitcast.69, f32[3,512]{1,0:T(4,128)} %logits.1, ...), custom_call_target="tpu_custom_call" | custom-call | flops 536870912 | bytes 2097152 | tf_op jit(solution)/shard_map/embed/pallas_call | solution.py:752
  7.9 2.7 collective-permute-start.4
  12.7 2.5 collective-permute-start.5
  19.7 14.6 %layer1_forward.1 = (bf16[512,512]{1,0:T(8,128)(2,1)}, f32[2,4,512]{2,1,0:T(4,128)}, f32[2,4,512]{2,1,0:T(4,128)}) custom-call(f32[512,512]{1,0:T(8,128)} %get-tuple-element.232.refs_0_.source, f32[2,4,512]{2,1,0:T(4,128)} %copy-done.28, f32[2,4,512]{2,1,0:T(4,128)} %copy-done.39, f32[2,2,512]{2,1,0:T(2,128)} %get-tuple-element.221.refs_3_.affine.refs_2_, ...), custom_call_target="tpu_custom_call" | custom-call | flops 9663676416 | bytes 44040192 | tf_op jit(solution)/shard_map/layer1_forward/pallas_call | solution.py:508
  34.3 1.4 collective-permute-start.10
  37.9 2.4 collective-permute-start.11
  46.9 2.6 layer2_both.1
  52.2 17.5 %layer1_states.1 = (f32[6,512,512]{2,1,0:T(8,128)}, f32[6,512,512]{2,1,0:T(8,128)}, f32[6,512,512]{2,1,0:T(8,128)}, f32[6,512,512]{2,1,0:T(8,128)}) custom-call(f32[512,512]{1,0:T(8,128)} %get-tuple-element.232.refs_0_.source, f32[2,4,512]{2,1,0:T(4,128)} %get-tuple-element.233.refs_1_.moments, f32[2,2,512]{2,1,0:T(2,128)} %get-tuple-element.221.refs_3_.affine.refs_2_, ...), custom_call_target="tpu_custom_call" | custom-call | flops 9663676416 | bytes 44040192 | tf_op jit(solution)/shard_map/layer1_states/pallas_call | solution.py:508
  69.8 2.4 collective-permute-start.17
  76.6 11.1 %collective-permute-done.18.total_a = f32[2,4,512]{2,1,0:T(4,128)S(1)} collective-permute-done((f32[2,4,512]{2,1,0:T(4,128)S(1)}, f32[2,4,512]{2,1,0:T(4,128)S(1)}, u32[]{:S(2)}, u32[]{:S(2)}) %collective-permute-start.18) | collective-permute-done | bytes 16416 | tf_op jit(solution)/shard_map/ppermute | solution.py:32
  89.9 29.7 %layer1_backward.1 = (f32[512,512]{1,0:T(8,128)}, f32[2,4,512]{2,1,0:T(4,128)}, f32[6,2048]{1,0:T(8,128)}, bf16[512,4096]{1,0:T(8,128)(2,1)}, bf16[512,4096]{1,0...) custom-call(bf16[512,512]{1,0:T(8,128)(2,1)} %copy-done.31, ...), custom_call_target="tpu_custom_call" | custom-call | flops 19327352832 | bytes 44040192 | tf_op jit(solution)/shard_map/layer1_backward/pallas_call | solution.py:671
  120.6 8.7 %collective-permute-start.21 = (bf16[64,4096]{1,0:T(8,128)(2,1)S(1)}, bf16[64,4096]{1,0:T(8,128)(2,1)S(1)}, u32[]{:S(2)}, u32[]{:S(2)}) collective-permute-start(bf16[64,4096]{1,0:T(8,128)(2,1)S(1)} %constant_dynamic-slice_fusion), channel_id=1, source_target_pairs={{0,1},{1,0},{2,3},{3,2},{4,5},{5,4},{6,7},{7,6},{8,9},{9,8},{10,11... | collective-permute-start | bytes 1572872 | tf_op jit(solution)/shard_map/ppermute | solution.py:26
  130.9 1.6 collective-permute-done.20
  134.2 1.5 collective-permute-start.23
  137.6 5.1 %collective-permute-done.23 = bf16[64,4096]{1,0:T(8,128)(2,1)S(1)} collective-permute-done((bf16[64,4096]{1,0:T(8,128)(2,1)S(1)}, bf16[64,4096]{1,0:T(8,128)(2,1)S(1)}, u32[]{:S(2)}, u32[]{:S(2)}) %collective-permute-start.23) | collective-permute-done | bytes 524320 | tf_op jit(solution)/shard_map/ppermute | solution.py:1029
  142.7 5.6 %collective-permute-done.34 = bf16[64,4096]{1,0:T(8,128)(2,1)S(1)} collective-permute-done((bf16[64,4096]{1,0:T(8,128)(2,1)S(1)}, bf16[64,4096]{1,0:T(8,128)(2,1)S(1)}, u32[]{:S(2)}, u32[]{:S(2)}) %collective-permute-start.34) | collective-permute-done | bytes 524320 | tf_op jit(solution)/shard_map/ppermute | solution.py:1029
  148.3 1.4 add_convert_fusion.13
  151.0 1.4 add_convert_fusion.7
  155.7 1.6 collective-permute-done.25
  159.5 1.5 collective-permute-start.26
  161.0 2.7 collective-permute-done.35
  165.1 1.7 collective-permute-start.40
  166.8 2.9 collective-permute-done.27
  169.7 1.4 add_convert_fusion.11
  173.6 1.7 collective-permute-done.40
  178.0 3.8 %collective-permute-done.29 = f32[2,4,512]{2,1,0:T(4,128)S(1)} collective-permute-done((f32[2,4,512]{2,1,0:T(4,128)S(1)}, f32[2,4,512]{2,1,0:T(4,128)S(1)}, u32[]{:S(2)}, u32[]{:S(2)}) %collective-permute-start.29) | collective-permute-done | bytes 16416 | tf_op jit(solution)/shard_map/ppermute | solution.py:36
  181.8 2.2 add_convert_fusion.10
  185.0 1.9 collective-permute-done.41
  189.3 5.0 %feature_grads.1 = (f32[512,128]{1,0:T(8,128)}, bf16[16,4096]{1,0:T(8,128)(2,1)}, bf16[16,4096]{1,0:T(8,128)(2,1)}) custom-call(f32[512,512]{1,0:T(8,128)} %get-tuple-element.263.gx, f32[512,512]{1,0:T(8,128)} %get-tuple-element.232.refs_0_.source, f32[2,4,512]{2,1,0:T(4,128)} %get-tuple-element.233.refs_1_.moments, f32[2,4,512]{2,1,0:T(4,128)} %add_multiply_fusion.totals, ...), custom_call_target="tpu_custom_call" | custom-call | flops 536870912 | bytes 4194304 | tf_op jit(solution)/shard_map/feature_grads/pallas_call | solution.py:807
  194.3 2.3 add_convert_fusion.9
  197.9 3.6 %collective-permute-start.32 = (bf16[16,4096]{1,0:T(8,128)(2,1)}, bf16[16,4096]{1,0:T(8,128)(2,1)S(1)}, u32[]{:S(2)}, u32[]{:S(2)}) collective-permute-start(bf16[16,4096]{1,0:T(8,128)(2,1)} %get-tuple-element.271), channel_id=1, source_target_pairs={{0,1},{1,0},{2,3},{3,2},{4,5},{5,4},{6,7},{7,6},{8,9},{9,8},{10,11... | collective-permute-start | bytes 393224 | tf_op jit(solution)/shard_map/ppermute | solution.py:26
  201.5 1.5 add_convert_fusion.2
  205.9 1.7 collective-permute-start.43
  208.0 1.6 add_convert_fusion.8
  210.6 2.0 collective-permute-start.38
  217.3 1.5 collective-permute-start.45
  221.0 4.6 %collective-permute-done.45 = bf16[64,4096]{1,0:T(8,128)(2,1)S(1)} collective-permute-done((bf16[64,4096]{1,0:T(8,128)(2,1)S(1)}, bf16[64,4096]{1,0:T(8,128)(2,1)S(1)}, u32[]{:S(2)}, u32[]{:S(2)}) %collective-permute-start.45) | collective-permute-done | bytes 524320 | tf_op jit(solution)/shard_map/ppermute | solution.py:1029
  225.7 2.1 broadcast_select_fusion.1
  227.8 1.7 collective-permute-start.49
  232.7 3.6 %place_block_0.1 = (f32[3,1024,1024]{2,1,0:T(8,128)}, f32[3,1024,512]{2,1,0:T(8,128)}, bf16[128,512]{1,0:T(8,128)(2,1)}) custom-call(bf16[80,4096]{1,0:T(8,128)(2,1)} %copy-done, bf16[64,4096]{1,0:T(8,128)(2,1)} %collective-permute-done.47.refs_1_, f32[3,1024,1024]{2,1,0:T(8,128)} %get-tuple-element.308.refs_2_, ...), custom_call_target="tpu_custom_call", output_to_operand_aliasing={{0}: (2, {}), {1}: (3, {})} | custom-call | tf_op jit(solution)/shard_map/place_block_0/pallas_call | solution.py:943
  236.2 1.4 collective-permute-done.49
  237.7 1.7 collective-permute-start.52
  239.3 4.0 %collective-permute-done.48 = bf16[64,4096]{1,0:T(8,128)(2,1)} collective-permute-done((bf16[64,4096]{1,0:T(8,128)(2,1)}, bf16[64,4096]{1,0:T(8,128)(2,1)}, u32[]{:S(2)}, u32[]{:S(2)}) %collective-permute-start.48) | collective-permute-done | bytes 524320 | tf_op jit(solution)/shard_map/ppermute | solution.py:1029
  243.3 2.0 collective-permute-start.50
  247.2 1.4 collective-permute-start.51
  249.9 5.4 %collective-permute-start.64 = (f32[1024,32]{0,1:T(8,128)}, f32[1024,32]{0,1:T(8,128)}, u32[]{:S(2)}, u32[]{:S(2)}) collective-permute-start(f32[1024,32]{0,1:T(8,128)} %get-tuple-element.380), channel_id=1, source_target_pairs={{0,2},{1,3},{4,6},{5,7},{8,10},{9,11},{12,14},{13,15},{16,18},{17,... | collective-permute-start | bytes 393224 | tf_op jit(solution)/shard_map/ppermute | solution.py:32
  255.4 3.4 %place_block_1.1 = (f32[3,1024,1024]{2,1,0:T(8,128)}, f32[3,1024,512]{2,1,0:T(8,128)}, bf16[128,512]{1,0:T(8,128)(2,1)}) custom-call(bf16[80,4096]{1,0:T(8,128)(2,1)} %copy-done.1, bf16[64,4096]{1,0:T(8,128)(2,1)} %copy-done.10, bf16[128,512]{1,0:T(8,128)(2,1)} %copy-done.19, ...), custom_call_target="tpu_custom_call", output_to_operand_aliasing={{0}: (3, {}), {1}: (4, {})} | custom-call | tf_op jit(solution)/shard_map/place_block_1/pallas_call | solution.py:943
  263.0 3.4 %place_block_2.1 = (f32[3,1024,1024]{2,1,0:T(8,128)}, f32[3,1024,512]{2,1,0:T(8,128)}, bf16[128,512]{1,0:T(8,128)(2,1)}) custom-call(bf16[80,4096]{1,0:T(8,128)(2,1)} %copy-done.2, bf16[64,4096]{1,0:T(8,128)(2,1)} %copy-done.11, bf16[128,512]{1,0:T(8,128)(2,1)} %collective-permute-done.53.refs_2_, ...), custom_call_target="tpu_custom_call", output_to_operand_aliasing={{0}: (3, {}), {1}: (4, {})} | custom-call | tf_op jit(solution)/shard_map/place_block_2/pallas_call | solution.py:943
  266.4 2.2 collective-permute-done.55
  269.7 4.7 %collective-permute-done.54 = bf16[64,4096]{1,0:T(8,128)(2,1)} collective-permute-done((bf16[64,4096]{1,0:T(8,128)(2,1)S(1)}, bf16[64,4096]{1,0:T(8,128)(2,1)}, u32[]{:S(2)}, u32[]{:S(2)}) %collective-permute-start.54) | collective-permute-done | bytes 524320 | tf_op jit(solution)/shard_map/ppermute | solution.py:1029
  274.4 1.5 collective-permute-start.56
  277.7 3.4 %place_block_3.1 = (f32[3,1024,1024]{2,1,0:T(8,128)}, f32[3,1024,512]{2,1,0:T(8,128)}, bf16[128,512]{1,0:T(8,128)(2,1)}) custom-call(bf16[80,4096]{1,0:T(8,128)(2,1)} %copy-done.3, bf16[64,4096]{1,0:T(8,128)(2,1)} %copy-done.12, bf16[128,512]{1,0:T(8,128)(2,1)} %collective-permute-done.56.refs_2_, ...), custom_call_target="tpu_custom_call", output_to_operand_aliasing={{0}: (3, {}), {1}: (4, {})} | custom-call | tf_op jit(solution)/shard_map/place_block_3/pallas_call | solution.py:943
  282.6 4.4 %collective-permute-done.57 = bf16[64,4096]{1,0:T(8,128)(2,1)} collective-permute-done((bf16[64,4096]{1,0:T(8,128)(2,1)S(1)}, bf16[64,4096]{1,0:T(8,128)(2,1)}, u32[]{:S(2)}, u32[]{:S(2)}) %collective-permute-start.57) | collective-permute-done | bytes 524320 | tf_op jit(solution)/shard_map/ppermute | solution.py:1029
  287.0 1.5 collective-permute-start.59
  290.4 3.4 %place_block_4.1 = (f32[3,1024,1024]{2,1,0:T(8,128)}, f32[3,1024,512]{2,1,0:T(8,128)}, bf16[128,512]{1,0:T(8,128)(2,1)}) custom-call(bf16[80,4096]{1,0:T(8,128)(2,1)} %copy-done.4, bf16[64,4096]{1,0:T(8,128)(2,1)} %copy-done.13, bf16[128,512]{1,0:T(8,128)(2,1)} %collective-permute-done.59.refs_2_, ...), custom_call_target="tpu_custom_call", output_to_operand_aliasing={{0}: (3, {}), {1}: (4, {})} | custom-call | tf_op jit(solution)/shard_map/place_block_4/pallas_call | solution.py:943
  295.3 4.4 %collective-permute-done.60 = bf16[64,4096]{1,0:T(8,128)(2,1)} collective-permute-done((bf16[64,4096]{1,0:T(8,128)(2,1)S(1)}, bf16[64,4096]{1,0:T(8,128)(2,1)}, u32[]{:S(2)}, u32[]{:S(2)}) %collective-permute-start.60) | collective-permute-done | bytes 524320 | tf_op jit(solution)/shard_map/ppermute | solution.py:1029
  299.7 1.5 collective-permute-start.62
  303.0 3.4 %place_block_5.1 = (f32[3,1024,1024]{2,1,0:T(8,128)}, f32[3,1024,512]{2,1,0:T(8,128)}, bf16[128,512]{1,0:T(8,128)(2,1)}) custom-call(bf16[80,4096]{1,0:T(8,128)(2,1)} %copy-done.5, bf16[64,4096]{1,0:T(8,128)(2,1)} %copy-done.9, bf16[128,512]{1,0:T(8,128)(2,1)} %copy-done.18, ...), custom_call_target="tpu_custom_call", output_to_operand_aliasing={{0}: (3, {}), {1}: (4, {})} | custom-call | tf_op jit(solution)/shard_map/place_block_5/pallas_call | solution.py:943
  307.2 1.9 broadcast_select_fusion.3
  314.3 2.2 collective-permute-start.68
  318.1 3.4 %place_block_6.1 = (f32[3,1024,1024]{2,1,0:T(8,128)}, f32[3,1024,512]{2,1,0:T(8,128)}, bf16[128,512]{1,0:T(8,128)(2,1)}) custom-call(bf16[80,4096]{1,0:T(8,128)(2,1)} %copy-done.6, bf16[64,4096]{1,0:T(8,128)(2,1)} %copy-done.8, bf16[128,512]{1,0:T(8,128)(2,1)} %copy-done.22, ...), custom_call_target="tpu_custom_call", output_to_operand_aliasing={{0}: (3, {}), {1}: (4, {})} | custom-call | tf_op jit(solution)/shard_map/place_block_6/pallas_call | solution.py:943
  322.4 3.0 spare_totals.1
  327.9 3.4 %place_block_7.1 = (f32[3,1024,1024]{2,1,0:T(8,128)}, f32[3,1024,512]{2,1,0:T(8,128)}, bf16[128,512]{1,0:T(8,128)(2,1)}) custom-call(bf16[80,4096]{1,0:T(8,128)(2,1)} %copy-done.7, bf16[64,4096]{1,0:T(8,128)(2,1)} %collective-permute-done.70.refs_1_, bf16[128,512]{1,0:T(8,128)(2,1)} %copy-done.21, ...), custom_call_target="tpu_custom_call", output_to_operand_aliasing={{0}: (3, {}), {1}: (4, {})} | custom-call | tf_op jit(solution)/shard_map/place_block_7/pallas_call | solution.py:943
  333.6 1.6 place_extra.1
  (270 shorter events, 95.4 us)
Async XLA Ops:
  2.8 16.3 %collective-permute-start.7 = (bf16[3,1024,1024]{2,1,0:T(8,128)(2,1)}, bf16[3,1024,1024]{2,1,0:T(8,128)(2,1)}, u32[]{:S(2)}, u32[]{:S(2)}) collective-permute-start(bf16[3,1024,1024]{2,1,0:T(8,128)(2,1)} %w0.3), channel_id=1, source_target_pairs={{0,1},{1,0},{2,3},{3,2},{4,5},{5,4},{6,7},{7,6},{8,9},{9,8},{10,11... | collective-permute-start | bytes 18874376 | tf_op jit(solution)/shard_map/ppermute | solution.py:26
  3.2 15.9 %collective-permute-start.8 = (bf16[3,1024,512]{2,1,0:T(8,128)(2,1)}, bf16[3,1024,512]{2,1,0:T(8,128)(2,1)}, u32[]{:S(2)}, u32[]{:S(2)}) collective-permute-start(bf16[3,1024,512]{2,1,0:T(8,128)(2,1)} %w2.3), channel_id=1, source_target_pairs={{0,1},{1,0},{2,3},{3,2},{4,5},{5,4},{6,7},{7,6},{8,9},{9,8},{10,11... | collective-permute-start | bytes 9437192 | tf_op jit(solution)/shard_map/ppermute | solution.py:26
  7.9 4.0 %collective-permute-start.4 = (f32[2,4,512]{2,1,0:T(4,128)}, f32[2,4,512]{2,1,0:T(4,128)S(1)}, u32[]{:S(2)}, u32[]{:S(2)}) collective-permute-start(f32[2,4,512]{2,1,0:T(4,128)} %get-tuple-element.220), channel_id=1, source_target_pairs={{0,8},{4,12},{8,0},{12,4},{16,24},{20,28},{24,16},{28,20},{1,9},{5... | collective-permute-start | bytes 49160 | tf_op jit(solution)/shard_map/ppermute | solution.py:36
  12.7 3.7 %collective-permute-start.5 = (f32[2,4,512]{2,1,0:T(4,128)S(1)}, f32[2,4,512]{2,1,0:T(4,128)S(1)}, u32[]{:S(2)}, u32[]{:S(2)}) collective-permute-start(f32[2,4,512]{2,1,0:T(4,128)S(1)} %pad_maximum_fusion.3), channel_id=1, source_target_pairs={{0,16},{4,20},{8,24},{12,28},{16,0},{20,4},{24,8},{28,12},{1,17},{... | collective-permute-start | bytes 49160 | tf_op jit(solution)/shard_map/ppermute | solution.py:36
  16.4 2.7 collective-permute-start.6
  34.3 2.9 collective-permute-start.10
  35.8 9.8 %collective-permute-start.9 = (bf16[512,512]{1,0:T(8,128)(2,1)}, bf16[512,512]{1,0:T(8,128)(2,1)S(1)}, u32[]{:S(2)}, u32[]{:S(2)}) collective-permute-start(bf16[512,512]{1,0:T(8,128)(2,1)} %get-tuple-element.227.hb), channel_id=1, source_target_pairs={{0,2},{1,3},{4,6},{5,7},{8,10},{9,11},{12,14},{13,15},{16,18},{17,... | collective-permute-start | bytes 1572872 | tf_op jit(solution)/shard_map/ppermute | solution.py:32
  37.9 3.6 %collective-permute-start.11 = (f32[2,4,512]{2,1,0:T(4,128)S(1)}, f32[2,4,512]{2,1,0:T(4,128)S(1)}, u32[]{:S(2)}, u32[]{:S(2)}) collective-permute-start(f32[2,4,512]{2,1,0:T(4,128)S(1)} %pad_maximum_fusion.5), channel_id=1, source_target_pairs={{0,16},{4,20},{8,24},{12,28},{16,0},{20,4},{24,8},{28,12},{1,17},{... | collective-permute-start | bytes 49160 | tf_op jit(solution)/shard_map/ppermute | solution.py:36
  41.5 4.0 %collective-permute-start.12 = (f32[2,4,512]{2,1,0:T(4,128)S(1)}, f32[2,4,512]{2,1,0:T(4,128)S(1)}, u32[]{:S(2)}, u32[]{:S(2)}) collective-permute-start(f32[2,4,512]{2,1,0:T(4,128)S(1)} %pad_maximum_fusion.6), channel_id=1, source_target_pairs={{0,2},{1,3},{4,6},{5,7},{8,10},{9,11},{12,14},{13,15},{16,18},{17,... | collective-permute-start | bytes 49160 | tf_op jit(solution)/shard_map/ppermute | solution.py:32
  42.8 2.7 collective-permute-start.13
  44.2 28.1 %collective-permute-start.15 = (f32[2,4,512]{2,1,0:T(4,128)S(1)}, f32[2,4,512]{2,1,0:T(4,128)S(1)}, u32[]{:S(2)}, u32[]{:S(2)}) collective-permute-start(f32[2,4,512]{2,1,0:T(4,128)S(1)} %pad_maximum_fusion.6), channel_id=1, source_target_pairs={{0,4},{4,0},{8,12},{12,8},{16,20},{20,16},{24,28},{28,24},{1,5},{5... | collective-permute-start | bytes 49160 | tf_op jit(solution)/shard_map/ppermute | solution.py:36
  49.6 20.2 %collective-permute-start.16 = (f32[2,4,512]{2,1,0:T(4,128)}, f32[2,4,512]{2,1,0:T(4,128)S(1)}, u32[]{:S(2)}, u32[]{:S(2)}) collective-permute-start(f32[2,4,512]{2,1,0:T(4,128)} %get-tuple-element.282), channel_id=1, source_target_pairs={{0,8},{4,12},{8,0},{12,4},{16,24},{20,28},{24,16},{28,20},{1,9},{5... | collective-permute-start | bytes 49160 | tf_op jit(solution)/shard_map/ppermute | solution.py:36
  50.9 38.1 %collective-permute-start.14 = (bf16[512,512]{1,0:T(8,128)(2,1)}, bf16[512,512]{1,0:T(8,128)(2,1)S(1)}, u32[]{:S(2)}, u32[]{:S(2)}) collective-permute-start(bf16[512,512]{1,0:T(8,128)(2,1)} %get-tuple-element.229), channel_id=1, source_target_pairs={{2,0},{3,1},{6,4},{7,5},{10,8},{11,9},{14,12},{15,13},{18,16},{19,... | collective-permute-start | bytes 1572872 | tf_op jit(solution)/shard_map/ppermute | solution.py:32
  69.8 3.6 %collective-permute-start.17 = (f32[2,4,512]{2,1,0:T(4,128)S(1)}, f32[2,4,512]{2,1,0:T(4,128)S(1)}, u32[]{:S(2)}, u32[]{:S(2)}) collective-permute-start(f32[2,4,512]{2,1,0:T(4,128)S(1)} %add.340), channel_id=1, source_target_pairs={{0,16},{4,20},{8,24},{12,28},{16,0},{20,4},{24,8},{28,12},{1,17},{... | collective-permute-start | bytes 49160 | tf_op jit(solution)/shard_map/ppermute | solution.py:36
  73.4 14.3 %collective-permute-start.18 = (f32[2,4,512]{2,1,0:T(4,128)S(1)}, f32[2,4,512]{2,1,0:T(4,128)S(1)}, u32[]{:S(2)}, u32[]{:S(2)}) collective-permute-start(f32[2,4,512]{2,1,0:T(4,128)S(1)} %add.341), channel_id=1, source_target_pairs={{2,0},{3,1},{6,4},{7,5},{10,8},{11,9},{14,12},{15,13},{18,16},{19,... | collective-permute-start | bytes 49160 | tf_op jit(solution)/shard_map/ppermute | solution.py:32
  74.7 14.4 %collective-permute-start.19 = (f32[2,4,512]{2,1,0:T(4,128)S(1)}, f32[2,4,512]{2,1,0:T(4,128)S(1)}, u32[]{:S(2)}, u32[]{:S(2)}) collective-permute-start(f32[2,4,512]{2,1,0:T(4,128)S(1)} %add.341), channel_id=1, source_target_pairs={{2,4},{3,5},{6,0},{7,1},{10,12},{11,13},{14,8},{15,9},{18,20},{19,... | collective-permute-start | bytes 49160 | tf_op jit(solution)/shard_map/ppermute | solution.py:69
  120.6 10.3 %collective-permute-start.21 = (bf16[64,4096]{1,0:T(8,128)(2,1)S(1)}, bf16[64,4096]{1,0:T(8,128)(2,1)S(1)}, u32[]{:S(2)}, u32[]{:S(2)}) collective-permute-start(bf16[64,4096]{1,0:T(8,128)(2,1)S(1)} %constant_dynamic-slice_fusion), channel_id=1, source_target_pairs={{0,1},{1,0},{2,3},{3,2},{4,5},{5,4},{6,7},{7,6},{8,9},{9,8},{10,11... | collective-permute-start | bytes 1572872 | tf_op jit(solution)/shard_map/ppermute | solution.py:26
  132.5 15.8 %collective-permute-start.22 = (bf16[512,4096]{1,0:T(8,128)(2,1)}, bf16[512,4096]{1,0:T(8,128)(2,1)}, u32[]{:S(2)}, u32[]{:S(2)}) collective-permute-start(bf16[512,4096]{1,0:T(8,128)(2,1)} %get-tuple-element.243), channel_id=1, source_target_pairs={{0,1},{1,0},{2,3},{3,2},{4,5},{5,4},{6,7},{7,6},{8,9},{9,8},{10,11... | collective-permute-start | bytes 12582920 | tf_op jit(solution)/shard_map/ppermute | solution.py:26
  132.6 18.4 %collective-permute-start.33 = (bf16[512,4096]{1,0:T(8,128)(2,1)}, bf16[512,4096]{1,0:T(8,128)(2,1)}, u32[]{:S(2)}, u32[]{:S(2)}) collective-permute-start(bf16[512,4096]{1,0:T(8,128)(2,1)} %get-tuple-element.275), channel_id=1, source_target_pairs={{0,1},{1,0},{2,3},{3,2},{4,5},{5,4},{6,7},{7,6},{8,9},{9,8},{10,11... | collective-permute-start | bytes 12582920 | tf_op jit(solution)/shard_map/ppermute | solution.py:26
  134.2 8.6 %collective-permute-start.23 = (bf16[64,4096]{1,0:T(8,128)(2,1)S(1)}, bf16[64,4096]{1,0:T(8,128)(2,1)S(1)}, u32[]{:S(2)}, u32[]{:S(2)}) collective-permute-start(bf16[64,4096]{1,0:T(8,128)(2,1)S(1)} %add_convert_fusion.15), channel_id=1, source_target_pairs={{0,8},{8,16},{16,24},{24,28},{28,20},{20,12},{12,4},{4,0},{5,13},{... | collective-permute-start | bytes 1572872 | tf_op jit(solution)/shard_map/ppermute | solution.py:1029
  136.8 11.5 %collective-permute-start.34 = (bf16[64,4096]{1,0:T(8,128)(2,1)S(1)}, bf16[64,4096]{1,0:T(8,128)(2,1)S(1)}, u32[]{:S(2)}, u32[]{:S(2)}) collective-permute-start(bf16[64,4096]{1,0:T(8,128)(2,1)S(1)} %add_convert_fusion.14), channel_id=1, source_target_pairs={{0,8},{8,16},{16,24},{24,28},{28,20},{20,12},{12,4},{4,0},{5,13},{... | collective-permute-start | bytes 1572872 | tf_op jit(solution)/shard_map/ppermute | solution.py:1029
  149.7 8.4 %collective-permute-start.24 = (bf16[64,4096]{1,0:T(8,128)(2,1)S(1)}, bf16[64,4096]{1,0:T(8,128)(2,1)S(1)}, u32[]{:S(2)}, u32[]{:S(2)}) collective-permute-start(bf16[64,4096]{1,0:T(8,128)(2,1)S(1)} %add_convert_fusion.13), channel_id=1, source_target_pairs={{0,8},{8,16},{16,24},{24,28},{28,20},{20,12},{12,4},{4,0},{5,13},{... | collective-permute-start | bytes 1572872 | tf_op jit(solution)/shard_map/ppermute | solution.py:1029
  152.7 3.0 collective-permute-start.36
  154.1 3.2 collective-permute-start.25
  155.0 8.8 %collective-permute-start.35 = (bf16[64,4096]{1,0:T(8,128)(2,1)S(1)}, bf16[64,4096]{1,0:T(8,128)(2,1)S(1)}, u32[]{:S(2)}, u32[]{:S(2)}) collective-permute-start(bf16[64,4096]{1,0:T(8,128)(2,1)S(1)} %add_convert_fusion.7), channel_id=1, source_target_pairs={{0,8},{8,16},{16,24},{24,28},{28,20},{20,12},{12,4},{4,0},{5,13},{... | collective-permute-start | bytes 1572872 | tf_op jit(solution)/shard_map/ppermute | solution.py:1029
  159.5 10.2 %collective-permute-start.26 = (bf16[64,4096]{1,0:T(8,128)(2,1)S(1)}, bf16[64,4096]{1,0:T(8,128)(2,1)S(1)}, u32[]{:S(2)}, u32[]{:S(2)}) collective-permute-start(bf16[64,4096]{1,0:T(8,128)(2,1)S(1)} %add_convert_fusion.12), channel_id=1, source_target_pairs={{0,8},{8,16},{16,24},{24,28},{28,20},{20,12},{12,4},{4,0},{5,13},{... | collective-permute-start | bytes 1572872 | tf_op jit(solution)/shard_map/ppermute | solution.py:1029
  161.0 8.7 %collective-permute-start.27 = (f32[2,4,512]{2,1,0:T(4,128)S(1)}, f32[2,4,512]{2,1,0:T(4,128)S(1)}, u32[]{:S(2)}, u32[]{:S(2)}) collective-permute-start(f32[2,4,512]{2,1,0:T(4,128)S(1)} %add.371), channel_id=1, source_target_pairs={{0,8},{4,12},{8,0},{12,4},{16,24},{20,28},{24,16},{28,20},{1,9},{5... | collective-permute-start | bytes 49160 | tf_op jit(solution)/shard_map/ppermute | solution.py:36
  165.1 10.2 %collective-permute-start.40 = (bf16[64,4096]{1,0:T(8,128)(2,1)S(1)}, bf16[64,4096]{1,0:T(8,128)(2,1)S(1)}, u32[]{:S(2)}, u32[]{:S(2)}) collective-permute-start(bf16[64,4096]{1,0:T(8,128)(2,1)S(1)} %add_convert_fusion.5), channel_id=1, source_target_pairs={{0,8},{8,16},{16,24},{24,28},{28,20},{20,12},{12,4},{4,0},{5,13},{... | collective-permute-start | bytes 1572872 | tf_op jit(solution)/shard_map/ppermute | solution.py:1029
  171.1 10.7 %collective-permute-start.28 = (bf16[64,4096]{1,0:T(8,128)(2,1)S(1)}, bf16[64,4096]{1,0:T(8,128)(2,1)S(1)}, u32[]{:S(2)}, u32[]{:S(2)}) collective-permute-start(bf16[64,4096]{1,0:T(8,128)(2,1)S(1)} %add_convert_fusion.11), channel_id=1, source_target_pairs={{0,8},{8,16},{16,24},{24,28},{28,20},{20,12},{12,4},{4,0},{5,13},{... | collective-permute-start | bytes 1572872 | tf_op jit(solution)/shard_map/ppermute | solution.py:1029
  172.4 9.4 %collective-permute-start.29 = (f32[2,4,512]{2,1,0:T(4,128)S(1)}, f32[2,4,512]{2,1,0:T(4,128)S(1)}, u32[]{:S(2)}, u32[]{:S(2)}) collective-permute-start(f32[2,4,512]{2,1,0:T(4,128)S(1)} %add.373), channel_id=1, source_target_pairs={{0,16},{4,20},{8,24},{12,28},{16,0},{20,4},{24,8},{28,12},{1,17},{... | collective-permute-start | bytes 49160 | tf_op jit(solution)/shard_map/ppermute | solution.py:36
  176.7 10.2 %collective-permute-start.41 = (bf16[64,4096]{1,0:T(8,128)(2,1)S(1)}, bf16[64,4096]{1,0:T(8,128)(2,1)S(1)}, u32[]{:S(2)}, u32[]{:S(2)}) collective-permute-start(bf16[64,4096]{1,0:T(8,128)(2,1)S(1)} %add_convert_fusion.4), channel_id=1, source_target_pairs={{0,8},{8,16},{16,24},{24,28},{28,20},{20,12},{12,4},{4,0},{5,13},{... | collective-permute-start | bytes 1572872 | tf_op jit(solution)/shard_map/ppermute | solution.py:1029
  184.6 9.6 %collective-permute-start.30 = (bf16[64,4096]{1,0:T(8,128)(2,1)}, bf16[64,4096]{1,0:T(8,128)(2,1)}, u32[]{:S(2)}, u32[]{:S(2)}) collective-permute-start(bf16[64,4096]{1,0:T(8,128)(2,1)} %add_convert_fusion.10), channel_id=1, source_target_pairs={{0,8},{8,16},{16,24},{24,28},{28,20},{20,12},{12,4},{4,0},{5,13},{... | collective-permute-start | bytes 1572872 | tf_op jit(solution)/shard_map/ppermute | solution.py:1029
  188.3 13.2 %collective-permute-start.42 = (bf16[64,4096]{1,0:T(8,128)(2,1)S(1)}, bf16[64,4096]{1,0:T(8,128)(2,1)}, u32[]{:S(2)}, u32[]{:S(2)}) collective-permute-start(bf16[64,4096]{1,0:T(8,128)(2,1)S(1)} %add_convert_fusion.3), channel_id=1, source_target_pairs={{0,8},{8,16},{16,24},{24,28},{28,20},{20,12},{12,4},{4,0},{5,13},{... | collective-permute-start | bytes 1572872 | tf_op jit(solution)/shard_map/ppermute | solution.py:1029
  196.6 11.4 %collective-permute-start.31 = (bf16[64,4096]{1,0:T(8,128)(2,1)}, bf16[64,4096]{1,0:T(8,128)(2,1)}, u32[]{:S(2)}, u32[]{:S(2)}) collective-permute-start(bf16[64,4096]{1,0:T(8,128)(2,1)} %add_convert_fusion.9), channel_id=1, source_target_pairs={{0,8},{8,16},{16,24},{24,28},{28,20},{20,12},{12,4},{4,0},{5,13},{... | collective-permute-start | bytes 1572872 | tf_op jit(solution)/shard_map/ppermute | solution.py:1029
  197.9 10.0 %collective-permute-start.32 = (bf16[16,4096]{1,0:T(8,128)(2,1)}, bf16[16,4096]{1,0:T(8,128)(2,1)S(1)}, u32[]{:S(2)}, u32[]{:S(2)}) collective-permute-start(bf16[16,4096]{1,0:T(8,128)(2,1)} %get-tuple-element.271), channel_id=1, source_target_pairs={{0,1},{1,0},{2,3},{3,2},{4,5},{5,4},{6,7},{7,6},{8,9},{9,8},{10,11... | collective-permute-start | bytes 393224 | tf_op jit(solution)/shard_map/ppermute | solution.py:26
  204.7 7.8 %collective-permute-start.44 = (f32[512,2,128]{2,1,0:T(2,128)S(1)}, f32[512,2,128]{2,1,0:T(2,128)S(1)}, u32[]{:S(2)}, u32[]{:S(2)}) collective-permute-start(f32[512,2,128]{2,1,0:T(2,128)S(1)} %bitcast.62), channel_id=1, source_target_pairs={{0,1},{1,0},{2,3},{3,2},{4,5},{5,4},{6,7},{7,6},{8,9},{9,8},{10,11... | collective-permute-start | bytes 1572872 | tf_op jit(solution)/shard_map/ppermute | solution.py:26
  205.9 8.3 %collective-permute-start.43 = (bf16[64,4096]{1,0:T(8,128)(2,1)S(1)}, bf16[64,4096]{1,0:T(8,128)(2,1)S(1)}, u32[]{:S(2)}, u32[]{:S(2)}) collective-permute-start(bf16[64,4096]{1,0:T(8,128)(2,1)S(1)} %add_convert_fusion.2), channel_id=1, source_target_pairs={{0,8},{8,16},{16,24},{24,28},{28,20},{20,12},{12,4},{4,0},{5,13},{... | collective-permute-start | bytes 1572872 | tf_op jit(solution)/shard_map/ppermute | solution.py:1029
  209.6 10.4 %collective-permute-start.37 = (bf16[64,4096]{1,0:T(8,128)(2,1)S(1)}, bf16[64,4096]{1,0:T(8,128)(2,1)S(1)}, u32[]{:S(2)}, u32[]{:S(2)}) collective-permute-start(bf16[64,4096]{1,0:T(8,128)(2,1)S(1)} %add_convert_fusion.8), channel_id=1, source_target_pairs={{0,8},{8,16},{16,24},{24,28},{28,20},{20,12},{12,4},{4,0},{5,13},{... | collective-permute-start | bytes 1572872 | tf_op jit(solution)/shard_map/ppermute | solution.py:1029
  210.6 9.5 %collective-permute-start.38 = (bf16[16,4096]{1,0:T(8,128)(2,1)S(1)}, bf16[16,4096]{1,0:T(8,128)(2,1)}, u32[]{:S(2)}, u32[]{:S(2)}) collective-permute-start(bf16[16,4096]{1,0:T(8,128)(2,1)S(1)} %reduce-precision_convert_fusion), channel_id=1, source_target_pairs={{0,2},{1,3},{4,6},{5,7},{8,10},{9,11},{12,14},{13,15},{16,18},{17,... | collective-permute-start | bytes 393224 | tf_op jit(solution)/shard_map/ppermute | solution.py:32
  215.8 2.9 collective-permute-start.46
  217.2 2.9 collective-permute-start.39
  217.3 8.4 %collective-permute-start.45 = (bf16[64,4096]{1,0:T(8,128)(2,1)S(1)}, bf16[64,4096]{1,0:T(8,128)(2,1)S(1)}, u32[]{:S(2)}, u32[]{:S(2)}) collective-permute-start(bf16[64,4096]{1,0:T(8,128)(2,1)S(1)} %add_convert_fusion.1), channel_id=1, source_target_pairs={{0,8},{8,16},{16,24},{24,28},{28,20},{20,12},{12,4},{4,0},{5,13},{... | collective-permute-start | bytes 1572872 | tf_op jit(solution)/shard_map/ppermute | solution.py:1029
  227.8 9.8 %collective-permute-start.49 = (bf16[80,4096]{1,0:T(8,128)(2,1)S(1)}, bf16[80,4096]{1,0:T(8,128)(2,1)S(1)}, u32[]{:S(2)}, u32[]{:S(2)}) collective-permute-start(bf16[80,4096]{1,0:T(8,128)(2,1)S(1)} %maximum_maximum_fusion.refs_0_), channel_id=1, source_target_pairs={{0,8},{8,16},{16,24},{24,28},{28,20},{20,12},{12,4},{4,0},{5,13},{... | collective-permute-start | bytes 1966088 | tf_op jit(solution)/shard_map/ppermute | solution.py:1029
  232.2 11.2 %collective-permute-start.48 = (bf16[64,4096]{1,0:T(8,128)(2,1)}, bf16[64,4096]{1,0:T(8,128)(2,1)}, u32[]{:S(2)}, u32[]{:S(2)}) collective-permute-start(bf16[64,4096]{1,0:T(8,128)(2,1)} %collective-permute-done.47.refs_1_), channel_id=1, source_target_pairs={{0,8},{8,16},{16,24},{24,28},{28,20},{20,12},{12,4},{4,0},{5,13},{... | collective-permute-start | bytes 1572872 | tf_op jit(solution)/shard_map/ppermute | solution.py:1029
  237.7 21.1 %collective-permute-start.52 = (bf16[80,4096]{1,0:T(8,128)(2,1)S(1)}, bf16[80,4096]{1,0:T(8,128)(2,1)S(1)}, u32[]{:S(2)}, u32[]{:S(2)}) collective-permute-start(bf16[80,4096]{1,0:T(8,128)(2,1)S(1)} %broadcast_multiply_fusion.5.refs_0_.refs_1_), channel_id=1, source_target_pairs={{0,8},{8,16},{16,24},{24,28},{28,20},{20,12},{12,4},{4,0},{5,13},{... | collective-permute-start | bytes 1966088 | tf_op jit(solution)/shard_map/ppermute | solution.py:1029
  243.3 3.2 collective-permute-start.50
  247.2 12.6 %collective-permute-start.51 = (bf16[64,4096]{1,0:T(8,128)(2,1)S(1)}, bf16[64,4096]{1,0:T(8,128)(2,1)}, u32[]{:S(2)}, u32[]{:S(2)}) collective-permute-start(bf16[64,4096]{1,0:T(8,128)(2,1)S(1)} %broadcast_multiply_fusion.11.refs_1_), channel_id=1, source_target_pairs={{0,8},{8,16},{16,24},{24,28},{28,20},{20,12},{12,4},{4,0},{5,13},{... | collective-permute-start | bytes 1572872 | tf_op jit(solution)/shard_map/ppermute | solution.py:1029
  248.6 53.6 %collective-permute-start.63 = (f32[1024,128]{1,0:T(8,128)}, f32[1024,128]{1,0:T(8,128)}, u32[]{:S(2)}, u32[]{:S(2)}) collective-permute-start(f32[1024,128]{1,0:T(8,128)} %get-tuple-element.379), channel_id=1, source_target_pairs={{2,0},{3,1},{6,4},{7,5},{10,8},{11,9},{14,12},{15,13},{18,16},{19,... | collective-permute-start | bytes 1572872 | tf_op jit(solution)/shard_map/ppermute | solution.py:32
  249.9 52.3 %collective-permute-start.64 = (f32[1024,32]{0,1:T(8,128)}, f32[1024,32]{0,1:T(8,128)}, u32[]{:S(2)}, u32[]{:S(2)}) collective-permute-start(f32[1024,32]{0,1:T(8,128)} %get-tuple-element.380), channel_id=1, source_target_pairs={{0,2},{1,3},{4,6},{5,7},{8,10},{9,11},{12,14},{13,15},{16,18},{17,... | collective-permute-start | bytes 393224 | tf_op jit(solution)/shard_map/ppermute | solution.py:32
  258.9 9.8 %collective-permute-start.55 = (bf16[80,4096]{1,0:T(8,128)(2,1)S(1)}, bf16[80,4096]{1,0:T(8,128)(2,1)S(1)}, u32[]{:S(2)}, u32[]{:S(2)}) collective-permute-start(bf16[80,4096]{1,0:T(8,128)(2,1)S(1)} %broadcast_multiply_fusion.4.refs_0_.refs_2_), channel_id=1, source_target_pairs={{0,8},{8,16},{16,24},{24,28},{28,20},{20,12},{12,4},{4,0},{5,13},{... | collective-permute-start | bytes 1966088 | tf_op jit(solution)/shard_map/ppermute | solution.py:1029
  262.5 11.9 %collective-permute-start.54 = (bf16[64,4096]{1,0:T(8,128)(2,1)S(1)}, bf16[64,4096]{1,0:T(8,128)(2,1)}, u32[]{:S(2)}, u32[]{:S(2)}) collective-permute-start(bf16[64,4096]{1,0:T(8,128)(2,1)S(1)} %broadcast_multiply_fusion.10.refs_1_), channel_id=1, source_target_pairs={{0,8},{8,16},{16,24},{24,28},{28,20},{20,12},{12,4},{4,0},{5,13},{... | collective-permute-start | bytes 1572872 | tf_op jit(solution)/shard_map/ppermute | solution.py:1029
  268.7 12.6 %collective-permute-start.58 = (bf16[80,4096]{1,0:T(8,128)(2,1)S(1)}, bf16[80,4096]{1,0:T(8,128)(2,1)S(1)}, u32[]{:S(2)}, u32[]{:S(2)}) collective-permute-start(bf16[80,4096]{1,0:T(8,128)(2,1)S(1)} %broadcast_multiply_fusion.3.refs_0_.refs_3_), channel_id=1, source_target_pairs={{0,8},{8,16},{16,24},{24,28},{28,20},{20,12},{12,4},{4,0},{5,13},{... | collective-permute-start | bytes 1966088 | tf_op jit(solution)/shard_map/ppermute | solution.py:1029
  274.4 2.8 collective-permute-start.56
  277.2 9.9 %collective-permute-start.57 = (bf16[64,4096]{1,0:T(8,128)(2,1)S(1)}, bf16[64,4096]{1,0:T(8,128)(2,1)}, u32[]{:S(2)}, u32[]{:S(2)}) collective-permute-start(bf16[64,4096]{1,0:T(8,128)(2,1)S(1)} %broadcast_multiply_fusion.9.refs_1_), channel_id=1, source_target_pairs={{0,8},{8,16},{16,24},{24,28},{28,20},{20,12},{12,4},{4,0},{5,13},{... | collective-permute-start | bytes 1572872 | tf_op jit(solution)/shard_map/ppermute | solution.py:1029
  281.4 12.6 %collective-permute-start.61 = (bf16[80,4096]{1,0:T(8,128)(2,1)S(1)}, bf16[80,4096]{1,0:T(8,128)(2,1)S(1)}, u32[]{:S(2)}, u32[]{:S(2)}) collective-permute-start(bf16[80,4096]{1,0:T(8,128)(2,1)S(1)} %broadcast_multiply_fusion.2.refs_0_.refs_4_), channel_id=1, source_target_pairs={{0,8},{8,16},{16,24},{24,28},{28,20},{20,12},{12,4},{4,0},{5,13},{... | collective-permute-start | bytes 1966088 | tf_op jit(solution)/shard_map/ppermute | solution.py:1029
  287.0 2.8 collective-permute-start.59
  289.8 9.9 %collective-permute-start.60 = (bf16[64,4096]{1,0:T(8,128)(2,1)S(1)}, bf16[64,4096]{1,0:T(8,128)(2,1)}, u32[]{:S(2)}, u32[]{:S(2)}) collective-permute-start(bf16[64,4096]{1,0:T(8,128)(2,1)S(1)} %broadcast_multiply_fusion.8.refs_1_), channel_id=1, source_target_pairs={{0,8},{8,16},{16,24},{24,28},{28,20},{20,12},{12,4},{4,0},{5,13},{... | collective-permute-start | bytes 1572872 | tf_op jit(solution)/shard_map/ppermute | solution.py:1029
  294.0 15.1 %collective-permute-start.66 = (bf16[80,4096]{1,0:T(8,128)(2,1)S(1)}, bf16[80,4096]{1,0:T(8,128)(2,1)}, u32[]{:S(2)}, u32[]{:S(2)}) collective-permute-start(bf16[80,4096]{1,0:T(8,128)(2,1)S(1)} %broadcast_multiply_fusion.1.refs_0_.refs_5_), channel_id=1, source_target_pairs={{0,8},{8,16},{16,24},{24,28},{28,20},{20,12},{12,4},{4,0},{5,13},{... | collective-permute-start | bytes 1966088 | tf_op jit(solution)/shard_map/ppermute | solution.py:1029
  299.7 2.7 collective-permute-start.62
  302.3 10.0 %collective-permute-start.65 = (bf16[64,4096]{1,0:T(8,128)(2,1)S(1)}, bf16[64,4096]{1,0:T(8,128)(2,1)}, u32[]{:S(2)}, u32[]{:S(2)}) collective-permute-start(bf16[64,4096]{1,0:T(8,128)(2,1)S(1)} %broadcast_multiply_fusion.7.refs_1_), channel_id=1, source_target_pairs={{0,8},{8,16},{16,24},{24,28},{28,20},{20,12},{12,4},{4,0},{5,13},{... | collective-permute-start | bytes 1572872 | tf_op jit(solution)/shard_map/ppermute | solution.py:1029
  310.2 11.4 %collective-permute-start.67 = (bf16[80,4096]{1,0:T(8,128)(2,1)S(1)}, bf16[80,4096]{1,0:T(8,128)(2,1)S(1)}, u32[]{:S(2)}, u32[]{:S(2)}) collective-permute-start(bf16[80,4096]{1,0:T(8,128)(2,1)S(1)} %broadcast_multiply_fusion.refs_0_.refs_6_), channel_id=1, source_target_pairs={{0,8},{8,16},{16,24},{24,28},{28,20},{20,12},{12,4},{4,0},{5,13},{... | collective-permute-start | bytes 1966088 | tf_op jit(solution)/shard_map/ppermute | solution.py:1029
  313.4 12.6 %collective-permute-start.70 = (bf16[64,4096]{1,0:T(8,128)(2,1)S(1)}, bf16[64,4096]{1,0:T(8,128)(2,1)}, u32[]{:S(2)}, u32[]{:S(2)}) collective-permute-start(bf16[64,4096]{1,0:T(8,128)(2,1)S(1)} %broadcast_multiply_fusion.6.refs_1_), channel_id=1, source_target_pairs={{0,8},{8,16},{16,24},{24,28},{28,20},{20,12},{12,4},{4,0},{5,13},{... | collective-permute-start | bytes 1572872 | tf_op jit(solution)/shard_map/ppermute | solution.py:1029
  314.3 3.2 collective-permute-start.68
  325.4 6.4 %collective-permute-start.69 = (f32[12,4096]{1,0:T(8,128)}, f32[12,4096]{1,0:T(8,128)S(1)}, u32[]{:S(2)}, u32[]{:S(2)}) collective-permute-start(f32[12,4096]{1,0:T(8,128)} %get-tuple-element.407), channel_id=1, source_target_pairs={{0,1},{1,0},{2,3},{3,2},{4,5},{5,4},{6,7},{7,6},{8,9},{9,8},{10,11... | collective-permute-start | bytes 589832 | tf_op jit(solution)/shard_map/ppermute | solution.py:26
  (53 other events, 286.2 us)
